TPU v7x, 32 devices: a whole 2x2x4 slice. The times are simulated.
32 devices in a mesh: seq: 16 (over z, y, x), head: 2 (over core).
Axes of the slice: x: 2, y: 2, z: 4, core: 2. Of those that a mesh axis runs over, the one named last changes fastest.
Arguments:
- queries: bfloat16 [2048, 512], P('seq', 'head')
- keys_values: bfloat16 [2048, 256], P(('seq', 'head'))
- selected: int32 [16, 3], replicated, may hold values from -1 to 3, as said below
Outputs:
- attended: bfloat16 [2048, 512], P('seq', 'head')
Inputs may be any that keep to these rules, and one draw needn't show every extreme that they name: selected[c, 0] = c // 4, the span's own block; selected[c, 1] and selected[c, 2] are two different blocks before it, chosen at random; where fewer than two earlier blocks exist, the missing entries are -1 (column 1 first filled).
All inputs are finite; a program needn't handle non-finite values.
Results may differ from a plain program's by a relative error of at most 0.0052.
Values may be sent and summed in bfloat16 or wider, within the bound.
No kernel may reach another device: no remote copies, remote signals or barrier semaphores. Data moves between devices by JAX's collectives and lax.ppermute only.
A program may use at most 64 MiB of HBM per device.

v0:
```python
import jax
import jax.numpy as jnp
from jax import lax
from jax.sharding import PartitionSpec as P

DH = 128
GROUP = 4
TOPK = 3


def swapped(block, axis, stride):
    count = lax.axis_size(axis)
    route = []
    for low in range(count):
        high = low | 1 << stride
        if high != low and high < count:
            route += [(low, high), (high, low)]
    return lax.ppermute(block, axis, route)


def attend_rows(query_rows, block_kv, query_pos, key_pos):
    count = query_rows.shape[0]
    heads = query_rows.shape[1] // DH
    shaped = query_rows.reshape(count, heads, DH)
    keys = block_kv[:, :DH]
    values = block_kv[:, DH:]
    scores = jnp.einsum("nhd,kd->hnk", shaped, keys, preferred_element_type=jnp.float32) * DH ** (
        -0.5
    )
    if query_pos is not None:
        allowed = key_pos[None, :] <= query_pos[:, None]
        scores = jnp.where(allowed[None], scores, -1e30)
    top = jnp.max(scores, axis=-1)
    expo = jnp.exp(scores - top[..., None])
    total = jnp.sum(expo, axis=-1)
    weights = expo.astype(jnp.bfloat16)
    outputs = jnp.einsum("hnk,kd->nhd", weights, values, preferred_element_type=jnp.float32)
    outputs = outputs / jnp.transpose(total)[..., None]
    lse = jnp.transpose(top + jnp.log(total))
    return (outputs, lse)


def blocked_attend(query_rows, block_kv, query_pos, key_pos):
    count = query_rows.shape[0]
    step_rows = 512 if count % 512 == 0 else count
    steps = count // step_rows
    grouped = query_rows.reshape(steps, step_rows, query_rows.shape[1])
    if query_pos is None:
        outputs, lse = lax.map(lambda rows: attend_rows(rows, block_kv, None, None), grouped)
    else:
        grouped_pos = query_pos.reshape(steps, step_rows)
        outputs, lse = lax.map(
            lambda pair: attend_rows(pair[0], block_kv, pair[1], key_pos), (grouped, grouped_pos)
        )
    return (outputs.reshape(count, outputs.shape[2], DH), lse.reshape(count, lse.shape[2]))


def shards(queries, keys_values, selected):
    kv_rows = lax.all_gather(keys_values, "head", axis=0, tiled=True)
    tok_rows = kv_rows.shape[0]
    seq_count = lax.axis_size("seq")
    seq_index = lax.axis_index("seq")
    piece_rows = tok_rows // GROUP
    block_count = seq_count // GROUP
    width = queries.shape[1]
    heads = width // DH
    block_kv = kv_rows
    for bit_number in range(GROUP.bit_length() - 1):
        partner = swapped(block_kv, "seq", bit_number)
        upper = seq_index >> bit_number & 1 == 1
        block_kv = jnp.where(
            upper, jnp.concatenate([partner, block_kv], 0), jnp.concatenate([block_kv, partner], 0)
        )
    row_sel = lax.dynamic_slice_in_dim(selected, seq_index, 1, 0)[0]
    my_block = seq_index // GROUP
    block_start = my_block * GROUP * tok_rows
    query_pos = seq_index * tok_rows + jnp.arange(tok_rows, dtype=jnp.int32)
    key_pos = block_start + jnp.arange(GROUP * tok_rows, dtype=jnp.int32)
    pieces = queries.reshape(GROUP, piece_rows, width)
    tiled = jnp.tile(pieces, (block_count, 1, 1))
    target = jnp.arange(seq_count, dtype=jnp.int32) // GROUP
    wanted = (target == row_sel[1]) | (target == row_sel[2])
    outgoing = jnp.where(wanted[:, None, None], tiled, jnp.zeros_like(tiled))
    arrived = lax.all_to_all(outgoing, "seq", split_axis=0, concat_axis=0, tiled=True)
    senders = arrived.shape[0]
    items = arrived.shape[1]
    flat = arrived.reshape(senders * items, width)
    outputs, lse = blocked_attend(flat, block_kv, None, None)
    outputs = outputs.astype(jnp.bfloat16).reshape(senders, items, width)
    lse = lse.reshape(senders, items, heads)
    back_out = lax.all_to_all(outputs, "seq", split_axis=0, concat_axis=0, tiled=True)
    back_lse = lax.all_to_all(lse, "seq", split_axis=0, concat_axis=0, tiled=True)
    own_out, own_lse = blocked_attend(queries, block_kv, query_pos, key_pos)
    outs_list = [own_out]
    lse_list = [own_lse]
    for column in range(1, TOPK):
        block_id = row_sel[column]
        safe = jnp.maximum(block_id, 0) * GROUP
        part_out = (
            lax.dynamic_slice_in_dim(back_out, safe, GROUP, 0)
            .reshape(tok_rows, heads, DH)
            .astype(jnp.float32)
        )
        part_lse = lax.dynamic_slice_in_dim(back_lse, safe, GROUP, 0).reshape(tok_rows, heads)
        part_lse = jnp.where(block_id >= 0, part_lse, -1e30)
        outs_list.append(part_out)
        lse_list.append(part_lse)
    lse_all = jnp.stack(lse_list)
    outs_all = jnp.stack(outs_list)
    largest = jnp.max(lse_all, axis=0)
    factor = jnp.exp(lse_all - largest[None])
    merged = jnp.sum(factor[..., None] * outs_all, axis=0) / jnp.sum(factor, axis=0)[..., None]
    return merged.reshape(tok_rows, width).astype(jnp.bfloat16)


def solution(mesh):
    in_specs = (P("seq", "head"), P(("seq", "head"), None), P())
    out_specs = P("seq", "head")
    return jax.shard_map(shards, mesh=mesh, in_specs=in_specs, out_specs=out_specs, check_vma=False)
```

profile of v0, /device:TPU:0, one launch (start us, length us, event | category | flops | bytes accessed | tf_op | source)
XLA Modules:
  0.0 55.4 jit_solution(6713606426760109902)
XLA Ops:
  0.0 0.7 %copy-done = s32[16,3]{0,1:T(4,128)S(1)} copy-done((s32[16,3]{0,1:T(4,128)S(1)}, s32[16,3]{0,1:T(4,128)}, u32[]{:S(2)}) %copy-start) | copy-done | bytes 216
  0.8 0.6 %fusion.26 = (s32[1,1]{0,1:T(1,128)}, s32[1,1]{0,1:T(1,128)}) fusion(s32[1,3]{0,1:T(4,128)S(1)} %constant_dynamic-slice_fusion), kind=kLoop, calls=%fused_computation.53 | loop fusion | bytes 16 | tf_op jit(solution)/shard_map/slice | solution.py:97
  1.3 1.3 %compare_or_fusion = pred[16]{0:T(512)(128)(4,1)S(1)} fusion(s32[]{:T(128)} %bitcast.6, s32[]{:T(128)} %bitcast.5), kind=kLoop, calls=%fused_computation.41 | loop fusion | flops 176 | bytes 24 | tf_op jit(solution)/shard_map/or | solution.py:82
  2.6 1.6 %bitcast_select_fusion = bf16[16,32,256]{2,1,0:T(8,128)(2,1)} fusion(pred[16]{0:T(512)(128)(4,1)S(1)} %compare_or_fusion, bf16[4,32,256]{2,1,0:T(8,128)(2,1)} %bitcast.82), kind=kLoop, calls=%fused_computation.22 | loop fusion | flops 131072 | bytes 327696 | tf_op jit(solution)/shard_map/jit(_where)/select_n | solution.py:83
  4.2 8.3 %all-to-all-start = ((bf16[16,32,256]{2,1,0:T(8,128)(2,1)}), bf16[16,32,256]{2,1,0:T(8,128)(2,1)S(1)}, u32[]{:S(2)}, u32[]{:S(2)}) async-start(bf16[16,32,256]{2,1,0:T(8,128)(2,1)} %bitcast_select_fusion), calls=%async_computation | async-start | bytes 524288 | tf_op jit(solution)/shard_map/all_to_all | solution.py:84
  12.6 2.1 %all_gather.3 = bf16[128,256]{1,0:T(8,128)(2,1)S(1)} all-gather(bf16[64,256]{1,0:T(8,128)(2,1)} %param.4), channel_id=1, replica_groups=mesh['seq'=16,'head'=2] {'head'}, dimensions={0}, use_global_device_ids=true | all-gather | bytes 98304 | tf_op jit(solution)/shard_map/all_gather | solution.py:59
  14.6 1.9 %collective-permute-start = (bf16[128,256]{1,0:T(8,128)(2,1)S(1)}, bf16[128,256]{1,0:T(8,128)(2,1)S(1)}, u32[]{:S(2)}, u32[]{:S(2)}) collective-permute-start(bf16[128,256]{1,0:T(8,128)(2,1)S(1)} %all_gather.3), channel_id=1, source_target_pairs={{0,2},{2,0},{4,6},{6,4},{8,10},{10,8},{12,14},{14,12},{16,18},{18,... | collective-permute-start | bytes 196616 | tf_op jit(solution)/shard_map/ppermute | solution.py:18
  19.2 0.7 %collective-permute-done = bf16[128,256]{1,0:T(8,128)(2,1)S(1)} collective-permute-done((bf16[128,256]{1,0:T(8,128)(2,1)S(1)}, bf16[128,256]{1,0:T(8,128)(2,1)S(1)}, u32[]{:S(2)}, u32[]{:S(2)}) %collective-permute-start) | collective-permute-done | bytes 65568 | tf_op jit(solution)/shard_map/ppermute | solution.py:18
  19.9 1.6 %collective-permute-start.1 = (bf16[256,256]{1,0:T(8,128)(2,1)S(1)}, bf16[256,256]{1,0:T(8,128)(2,1)S(1)}, u32[]{:S(2)}, u32[]{:S(2)}) collective-permute-start(bf16[256,256]{1,0:T(8,128)(2,1)S(1)} %maximum_select_fusion.1), channel_id=1, source_target_pairs={{0,4},{4,0},{2,6},{6,2},{8,12},{12,8},{10,14},{14,10},{16,20},{20,... | collective-permute-start | bytes 393224 | tf_op jit(solution)/shard_map/ppermute | solution.py:18
  21.5 0.1 broadcast_compare_fusion
  21.7 3.5 %collective-permute-done.1 = bf16[256,256]{1,0:T(8,128)(2,1)S(1)} collective-permute-done((bf16[256,256]{1,0:T(8,128)(2,1)S(1)}, bf16[256,256]{1,0:T(8,128)(2,1)S(1)}, u32[]{:S(2)}, u32[]{:S(2)}) %collective-permute-start.1) | collective-permute-done | bytes 131104 | tf_op jit(solution)/shard_map/ppermute | solution.py:18
  25.3 1.1 %fusion.27 = (f32[2,128]{1,0:T(2,128)S(1)}, f32[2,128,512]{1,2,0:T(8,128)S(1)}) fusion(bf16[512,256]{1,0:T(8,128)(2,1)S(1)} %maximum_select_fusion, pred[128,512]{0,1:T(8,128)(4,1)S(1)} %broadcast_compare_fusion, bf16[128,256]{1,0:T(8,128)(2,1)} %param.3), kind=kOutput, calls=%fused_computation.54 | convolution fusion | flops 33947392 | bytes 787456 | tf_op jit(solution)/shard_map/while/body/eval_jaxpr/nhd,kd->hnk/dot_general | solution.py:27
  26.5 0.2 fusion.8
  26.9 0.4 bitcast_reduce_fusion
  27.3 0.4 fusion.2
  27.8 0.6 %copy.30 = f32[16,32,2]{1,2,0:T(2,128)} copy(f32[16,32,2]{1,0,2:T(8,128)S(1)} %reshape_reshape.4) | data formatting | bytes 8192 | tf_op jit(solution)/shard_map/reshape;reshape | solution.py:90
  28.4 6.5 %all-to-all-start.1 = ((f32[16,32,2]{1,2,0:T(2,128)}), f32[16,32,2]{1,2,0:T(2,128)S(1)}, u32[]{:S(2)}, u32[]{:S(2)}) async-start(f32[16,32,2]{1,2,0:T(2,128)} %copy.30), calls=%async_computation.1 | async-start | bytes 32768 | tf_op jit(solution)/shard_map/all_to_all | solution.py:92
  34.9 0.5 fusion.6
  35.4 0.2 copy.39
  35.6 0.9 %convert_element_type.50 = bf16[16,32,256]{2,1,0:T(8,128)(2,1)} reshape(bf16[512,2,128]{2,1,0:T(2,128)(2,1)S(1)} %copy.39) | data formatting | bytes 524288 | tf_op jit(solution)/shard_map/convert_element_type | solution.py:89
  36.4 5.8 %all-to-all-done.1 = f32[16,32,2]{1,2,0:T(2,128)S(1)} async-done(((f32[16,32,2]{1,2,0:T(2,128)}), f32[16,32,2]{1,2,0:T(2,128)S(1)}, u32[]{:S(2)}, u32[]{:S(2)}) %all-to-all-start.1) | async-done | bytes 4128 | tf_op jit(solution)/shard_map/all_to_all | solution.py:92
  42.2 3.5 %all-to-all-start.2 = ((bf16[16,32,256]{2,1,0:T(8,128)(2,1)}), bf16[16,32,256]{2,1,0:T(8,128)(2,1)S(1)}, u32[]{:S(2)}, u32[]{:S(2)}) async-start(bf16[16,32,256]{2,1,0:T(8,128)(2,1)} %convert_element_type.50), calls=%async_computation.2 | async-start | bytes 524288 | tf_op jit(solution)/shard_map/all_to_all | solution.py:91
  46.1 8.1 %all-to-all-done.2 = bf16[16,32,256]{2,1,0:T(8,128)(2,1)S(1)} async-done(((bf16[16,32,256]{2,1,0:T(8,128)(2,1)}), bf16[16,32,256]{2,1,0:T(8,128)(2,1)S(1)}, u32[]{:S(2)}, u32[]{:S(2)}) %all-to-all-start.2) | async-done | bytes 262176 | tf_op jit(solution)/shard_map/all_to_all | solution.py:91
  54.7 0.7 %copy.42 = bf16[128,256]{1,0:T(8,128)(2,1)} copy(bf16[128,256]{0,1:T(8,128)(2,1)S(1)} %bitcast.81) | data formatting | bytes 131072 | tf_op jit(solution)/shard_map/convert_element_type | solution.py:113
  (27 shorter events, 1.2 us)
Async XLA Ops:
  0.0 0.7 %copy-start = (s32[16,3]{0,1:T(4,128)S(1)}, s32[16,3]{0,1:T(4,128)}, u32[]{:S(2)}) copy-start(s32[16,3]{0,1:T(4,128)} %param.5) | copy-start | bytes 580
  4.2 22.5 %all-to-all-start = ((bf16[16,32,256]{2,1,0:T(8,128)(2,1)}), bf16[16,32,256]{2,1,0:T(8,128)(2,1)S(1)}, u32[]{:S(2)}, u32[]{:S(2)}) async-start(bf16[16,32,256]{2,1,0:T(8,128)(2,1)} %bitcast_select_fusion), calls=%async_computation | async-start | bytes 524288 | tf_op jit(solution)/shard_map/all_to_all | solution.py:84
  14.6 5.3 %collective-permute-start = (bf16[128,256]{1,0:T(8,128)(2,1)S(1)}, bf16[128,256]{1,0:T(8,128)(2,1)S(1)}, u32[]{:S(2)}, u32[]{:S(2)}) collective-permute-start(bf16[128,256]{1,0:T(8,128)(2,1)S(1)} %all_gather.3), channel_id=1, source_target_pairs={{0,2},{2,0},{4,6},{6,4},{8,10},{10,8},{12,14},{14,12},{16,18},{18,... | collective-permute-start | bytes 196616 | tf_op jit(solution)/shard_map/ppermute | solution.py:18
  19.9 5.3 %collective-permute-start.1 = (bf16[256,256]{1,0:T(8,128)(2,1)S(1)}, bf16[256,256]{1,0:T(8,128)(2,1)S(1)}, u32[]{:S(2)}, u32[]{:S(2)}) collective-permute-start(bf16[256,256]{1,0:T(8,128)(2,1)S(1)} %maximum_select_fusion.1), channel_id=1, source_target_pairs={{0,4},{4,0},{2,6},{6,2},{8,12},{12,8},{10,14},{14,10},{16,20},{20,... | collective-permute-start | bytes 393224 | tf_op jit(solution)/shard_map/ppermute | solution.py:18
  28.4 13.8 %all-to-all-start.1 = ((f32[16,32,2]{1,2,0:T(2,128)}), f32[16,32,2]{1,2,0:T(2,128)S(1)}, u32[]{:S(2)}, u32[]{:S(2)}) async-start(f32[16,32,2]{1,2,0:T(2,128)} %copy.30), calls=%async_computation.1 | async-start | bytes 32768 | tf_op jit(solution)/shard_map/all_to_all | solution.py:92
  42.2 12.0 %all-to-all-start.2 = ((bf16[16,32,256]{2,1,0:T(8,128)(2,1)}), bf16[16,32,256]{2,1,0:T(8,128)(2,1)S(1)}, u32[]{:S(2)}, u32[]{:S(2)}) async-start(bf16[16,32,256]{2,1,0:T(8,128)(2,1)} %convert_element_type.50), calls=%async_computation.2 | async-start | bytes 524288 | tf_op jit(solution)/shard_map/all_to_all | solution.py:91
where the time goes:
time: 55.9 us; the launch traced here: 55.4 us
  starting transfers between devices  21.9 us (39%)
  waiting for transfers between devices  18.1 us (32%)
  local copies, waits for them, and re-layouts  4.54 us (8%)
  other arithmetic  3.75 us (7%)
  between operations  2.77 us (5%)
  matrix products  2.31 us (4%)
  blocking collectives  2.06 us (4%)
    all_to_all x1, starting transfers between devices, shards(): lax.all_to_all(outgoing, 'seq', split_axis=0, concat_axis=0, tiled=True)  8.31 us
    all_to_all x1, waiting for transfers between devices, shards(): lax.all_to_all(outputs, 'seq', split_axis=0, concat_axis=0, tiled=True)  8.07 us
    all_to_all x1, starting transfers between devices, shards(): lax.all_to_all(lse, 'seq', split_axis=0, concat_axis=0, tiled=True)  6.47 us
    all_to_all x1, waiting for transfers between devices, shards(): lax.all_to_all(lse, 'seq', split_axis=0, concat_axis=0, tiled=True)  5.76 us
    ppermute x2, waiting for transfers between devices, swapped(): return lax.ppermute(block, axis, route)  4.25 us
    ppermute x2, starting transfers between devices, swapped(): return lax.ppermute(block, axis, route)  3.59 us
    all_to_all x1, starting transfers between devices, shards(): lax.all_to_all(outputs, 'seq', split_axis=0, concat_axis=0, tiled=True)  3.53 us
    all_gather x1, blocking collectives, shards(): kv_rows = lax.all_gather(keys_values, 'head', axis=0, tiled=True)  2.06 us
  transfers between devices with their start and end apart: 5, of which 4 were waited for; matrix products, arithmetic and copies ran while one was open for 7% of the time, Pallas kernels for 0%

commit v1 on v0

v1 whole, which is shorter than its diff:
```python
import functools

import jax
import jax.numpy as jnp
from jax import lax
from jax.experimental import pallas as pl
from jax.experimental.pallas import tpu as pltpu
from jax.sharding import PartitionSpec as P

DH = 128
GROUP = 4
TOPK = 3
LOG2E = 1.4426950408889634
LOW = -3e38


def swapped(rows, axis, step):
    count = lax.axis_size(axis)
    return lax.ppermute(rows, axis, [(i, i ^ step) for i in range(count)])


def pick_kernel(blocks, me_ref, selected_ref, *refs):
    held, messages = refs[:blocks], refs[blocks:]
    rows = held[0].shape[0]
    me = me_ref[0]
    mine = me // GROUP
    for step in range(GROUP):
        messages[step][0:rows, :] = held[0][...]
        for column in range(1, TOPK):
            wanted = jnp.maximum(selected_ref[me ^ step, column], 0) ^ mine
            for index in range(blocks):

                @pl.when(wanted == index)
                def _():
                    messages[step][column * rows : (column + 1) * rows, :] = held[index][...]


def pick(me, selected, held):
    rows, width = held[0].shape
    message = jax.ShapeDtypeStruct((TOPK * rows, width), held[0].dtype)
    smem = pl.BlockSpec(memory_space=pltpu.SMEM)
    vmem = pl.BlockSpec(memory_space=pltpu.VMEM)
    return pl.pallas_call(
        functools.partial(pick_kernel, len(held)),
        out_shape=[message] * GROUP,
        in_specs=[smem, smem] + [vmem] * len(held),
        out_specs=[vmem] * GROUP,
        name="pick",
    )(me, selected, *held)


def attend_kernel(where_ref, selected_ref, queries_ref, *refs):
    pieces, out_ref = refs[:-1], refs[-1]
    tokens, width = queries_ref.shape
    heads = width // DH
    length = pieces[0].shape[0]
    rows = length // TOPK
    me, head = where_ref[0], where_ref[1]
    part = me % GROUP
    queries = queries_ref[...]
    stacked = jnp.concatenate([queries[:, h * DH : (h + 1) * DH] for h in range(heads)], axis=0)
    kv = jnp.concatenate([piece[...] for piece in pieces], axis=0)
    scores = lax.dot_general(
        stacked, kv[:, :DH], (((1,), (1,)), ((), ())), preferred_element_type=jnp.float32
    ) * (DH ** (-0.5) * LOG2E)
    lane = lax.broadcasted_iota(jnp.int32, (1, length), 1)
    firsts = []
    for index in range(len(pieces)):
        step, other = index % GROUP, index // GROUP
        position = (part ^ step) * tokens + (head ^ other) * rows + lane
        one = jnp.where(selected_ref[me, 1] >= 0, 0, GROUP * tokens)
        two = jnp.where(selected_ref[me, 2] >= 0, 0, GROUP * tokens)
        firsts.append(jnp.where(lane < rows, position, jnp.where(lane < 2 * rows, one, two)))
    first = jnp.concatenate(firsts, axis=1)
    token = lax.broadcasted_iota(jnp.int32, (heads * tokens, 1), 0) % tokens
    scores = jnp.where(first <= part * tokens + token, scores, LOW)
    top = jnp.max(scores, axis=1, keepdims=True)
    weights = jnp.exp2(scores - top)
    total = jnp.sum(weights, axis=1, keepdims=True)
    out = jnp.dot(weights.astype(jnp.bfloat16), kv[:, DH:], preferred_element_type=jnp.float32) / total
    for h in range(heads):
        out_ref[:, h * DH : (h + 1) * DH] = out[h * tokens : (h + 1) * tokens].astype(out_ref.dtype)


def attend(where, selected, queries, pieces):
    smem = pl.BlockSpec(memory_space=pltpu.SMEM)
    vmem = pl.BlockSpec(memory_space=pltpu.VMEM)
    return pl.pallas_call(
        attend_kernel,
        out_shape=jax.ShapeDtypeStruct(queries.shape, queries.dtype),
        in_specs=[smem, smem] + [vmem] * (1 + len(pieces)),
        out_specs=vmem,
        name="attend",
    )(where, selected, queries, *pieces)


def shards(queries, keys_values, selected):
    blocks = lax.axis_size("seq") // GROUP
    me = lax.axis_index("seq").astype(jnp.int32)
    head = lax.axis_index("head").astype(jnp.int32)
    held = {0: keys_values}
    for step in range(blocks - 1, 0, -1):
        held[step] = swapped(keys_values, "seq", step * GROUP)
    own = pick(me[None], selected, [held[step] for step in range(blocks)])
    near = [own[0]] + [None] * (GROUP - 1)
    for step in (3, 1, 2):
        near[step] = swapped(own[step], "seq", step)
    far = [swapped(piece, "head", 1) for piece in near]
    return attend(jnp.stack([me, head]), selected, queries, near + far)


def solution(mesh):
    in_specs = (P("seq", "head"), P(("seq", "head"), None), P())
    out_specs = P("seq", "head")
    return jax.shard_map(shards, mesh=mesh, in_specs=in_specs, out_specs=out_specs, check_vma=False)
```

time: 55.9 us -> 27.8 us (0.50)
  starting transfers between devices: 21.9 us -> 9.11 us
  waiting for transfers between devices: 18.1 us -> 10.5 us
  Pallas kernels: 0 us -> 4.63 us
  other arithmetic: 3.75 us -> 0.61 us
  between operations: 2.77 us -> 0.08 us
  matrix products: 2.31 us -> 0 us
  blocking collectives: 2.06 us -> 0 us
  local copies, waits for them, and re-layouts: 4.54 us -> 2.62 us
    all_to_all x3 -> x0, starting transfers between devices: 18.3 us -> none  [the longest x1 8.31 us: shards(): lax.all_to_all(outgoing, 'seq', split_axis=0, concat_axis=0, tiled=True)]
    all_to_all x3 -> x0, waiting for transfers between devices: 13.8 us -> none  [the longest x1 8.07 us: shards(): lax.all_to_all(outputs, 'seq', split_axis=0, concat_axis=0, tiled=True)]
    ppermute x2 -> x10, waiting for transfers between devices: 4.25 us -> 10.5 us  [swapped(): return lax.ppermute(rows, axis, [(i, i ^ step) for i in range(count)])]
    ppermute x2 -> x10, starting transfers between devices: 3.59 us -> 9.11 us  [swapped(): return lax.ppermute(rows, axis, [(i, i ^ step) for i in range(count)])]
    pallas_call x0 -> x2, Pallas kernels: none -> 4.63 us  [the longest x1 2.76 us: attend(): pl.pallas_call(attend_kernel, out_shape=jax.ShapeDtypeStruct(queries.shap...]
    dot_general x4 -> x0, matrix products: 2.31 us -> none  [the longest x2 1.55 us: attend_rows(): jnp.einsum('nhd,kd->hnk', shaped, keys, preferred_element_type=jnp.float32)]
    convert_element_type x7 -> x0, local copies, waits for them, and re-layouts: 2.1 us -> none  [the longest x2 1.03 us: shards(): outputs = outputs.astype(jnp.bfloat16).reshape(senders, items, width)]
    all_gather x1 -> x0, blocking collectives: 2.06 us -> none  [shards(): kv_rows = lax.all_gather(keys_values, 'head', axis=0, tiled=True)]
  transfers between devices with their start and end apart: 5 -> 10, of which waited for: 4 -> 6; matrix products, arithmetic and copies ran while one was open for 7% -> 5% of each run, Pallas kernels for 0% -> 0%
where the time goes in v1:
time: 27.8 us; the launch traced here: 27.5 us
  waiting for transfers between devices  10.5 us (38%)
  starting transfers between devices  9.11 us (33%)
  Pallas kernels  4.63 us (17%)
  local copies, waits for them, and re-layouts  2.62 us (9%)
  other arithmetic  0.61 us (2%)
    ppermute x10, waiting for transfers between devices, swapped(): return lax.ppermute(rows, axis, [(i, i ^ step) for i in range(count)])  10.5 us
    ppermute x10, starting transfers between devices, swapped(): return lax.ppermute(rows, axis, [(i, i ^ step) for i in range(count)])  9.11 us
    pallas_call x1, Pallas kernels, attend(): pl.pallas_call(attend_kernel, out_shape=jax.ShapeDtypeStruct(queries.shap...  2.76 us
    unnamed x23, local copies, waits for them, and re-layouts  2.62 us
    pallas_call x1, Pallas kernels, pick(): pl.pallas_call(functools.partial(pick_kernel, len(held)), out_shape=[mess...  1.87 us
    another operation x1, other arithmetic, shards(): return attend(jnp.stack([me, head]), selected, queries, near + far)  0.61 us
  transfers between devices with their start and end apart: 10, of which 6 were waited for; matrix products, arithmetic and copies ran while one was open for 5% of the time, Pallas kernels for 0%

profile of v1, /device:TPU:0, one launch (start us, length us, event | category | flops | bytes accessed | tf_op | source)
XLA Modules:
  0.0 27.5 jit_solution(14601227586780339279)
XLA Ops:
  0.0 4.0 %collective-permute-start.1 = (bf16[64,256]{1,0:T(8,128)(2,1)}, bf16[64,256]{1,0:T(8,128)(2,1)S(1)}, u32[]{:S(2)}, u32[]{:S(2)}) collective-permute-start(bf16[64,256]{1,0:T(8,128)(2,1)} %refs_0_.1), channel_id=1, source_target_pairs={{0,16},{2,18},{4,20},{6,22},{8,24},{10,26},{12,28},{14,30},{16,0},... | collective-permute-start | bytes 98312 | tf_op jit(solution)/shard_map/ppermute | solution.py:19
  4.0 1.6 %collective-permute-start = (bf16[64,256]{1,0:T(8,128)(2,1)}, bf16[64,256]{1,0:T(8,128)(2,1)S(1)}, u32[]{:S(2)}, u32[]{:S(2)}) collective-permute-start(bf16[64,256]{1,0:T(8,128)(2,1)} %refs_0_.1), channel_id=1, source_target_pairs={{0,8},{2,10},{4,12},{6,14},{8,0},{10,2},{12,4},{14,6},{16,24},{18,... | collective-permute-start | bytes 98312 | tf_op jit(solution)/shard_map/ppermute | solution.py:19
  5.6 0.0 collective-permute-start.2
  5.6 0.7 %copy-done.10 = s32[16,3]{0,1:T(4,128)S(1)} copy-done((s32[16,3]{0,1:T(4,128)S(1)}, s32[16,3]{0,1:T(4,128)}, u32[]{:S(2)}) %copy-start.10) | copy-done | bytes 216
  6.3 0.7 %copy.5.selected_ref = s32[16,3]{1,0:T(8,128)} copy(s32[16,3]{0,1:T(4,128)S(1)} %copy-done.10) | data formatting | bytes 384 | tf_op args[2]
  7.0 0.0 collective-permute-done.1.refs_2_
  7.0 1.2 %collective-permute-done.refs_1_ = bf16[64,256]{1,0:T(8,128)(2,1)S(1)} collective-permute-done((bf16[64,256]{1,0:T(8,128)(2,1)}, bf16[64,256]{1,0:T(8,128)(2,1)S(1)}, u32[]{:S(2)}, u32[]{:S(2)}) %collective-permute-start) | collective-permute-done | bytes 32800 | tf_op jit(solution)/shard_map/ppermute | solution.py:19
  8.2 3.4 %collective-permute-done.2.refs_3_ = bf16[64,256]{1,0:T(8,128)(2,1)S(1)} collective-permute-done((bf16[64,256]{1,0:T(8,128)(2,1)}, bf16[64,256]{1,0:T(8,128)(2,1)S(1)}, u32[]{:S(2)}, u32[]{:S(2)}) %collective-permute-start.2) | collective-permute-done | bytes 32800 | tf_op jit(solution)/shard_map/ppermute | solution.py:19
  11.5 0.6 %copy-done.9 = bf16[64,256]{1,0:T(8,128)(2,1)} copy-done((bf16[64,256]{1,0:T(8,128)(2,1)}, bf16[64,256]{1,0:T(8,128)(2,1)S(1)}, u32[]{:S(2)}) %copy-start.9) | copy-done | bytes 32792
  12.1 1.9 %pick.1 = (bf16[192,256]{1,0:T(8,128)(2,1)}, bf16[192,256]{1,0:T(8,128)(2,1)}, bf16[192,256]{1,0:T(8,128)(2,1)}, bf16[192,256]{1,0:T(8,128)(2,1)}) custom-call(s32[1]{0:T(128)} %bitcast.me_ref, s32[16,3]{1,0:T(8,128)} %copy.5.selected_ref, bf16[64,256]{1,0:T(8,128)(2,1)} %refs_0_.1, bf16[64,256]{1,0:T(8,128)(2,1)} %copy-done.8, bf16[64,256]{1,0:T(8,128)(2,1)} %copy-done.7, ...), custom_call_target="tpu_custom_call" | custom-call | tf_op jit(solution)/shard_map/pick/pallas_call | solution.py:43
  14.0 1.5 %collective-permute-start.3 = (bf16[192,256]{1,0:T(8,128)(2,1)}, bf16[192,256]{1,0:T(8,128)(2,1)S(1)}, u32[]{:S(2)}, u32[]{:S(2)}) collective-permute-start(bf16[192,256]{1,0:T(8,128)(2,1)} %get-tuple-element.10), channel_id=1, source_target_pairs={{0,2},{2,0},{4,6},{6,4},{8,10},{10,8},{12,14},{14,12},{16,18},{18,... | collective-permute-start | bytes 294920 | tf_op jit(solution)/shard_map/ppermute | solution.py:19
  15.5 1.5 %collective-permute-start.4 = (bf16[192,256]{1,0:T(8,128)(2,1)}, bf16[192,256]{1,0:T(8,128)(2,1)S(1)}, u32[]{:S(2)}, u32[]{:S(2)}) collective-permute-start(bf16[192,256]{1,0:T(8,128)(2,1)} %get-tuple-element.11), channel_id=1, source_target_pairs={{0,4},{2,6},{4,0},{6,2},{8,12},{10,14},{12,8},{14,10},{16,20},{18,... | collective-permute-start | bytes 294920 | tf_op jit(solution)/shard_map/ppermute | solution.py:19
  17.0 0.5 %collective-permute-start.5 = (bf16[192,256]{1,0:T(8,128)(2,1)}, bf16[192,256]{1,0:T(8,128)(2,1)S(1)}, u32[]{:S(2)}, u32[]{:S(2)}) collective-permute-start(bf16[192,256]{1,0:T(8,128)(2,1)} %get-tuple-element.12), channel_id=1, source_target_pairs={{0,6},{2,4},{4,2},{6,0},{8,14},{10,12},{12,10},{14,8},{16,22},{18,... | collective-permute-start | bytes 294920 | tf_op jit(solution)/shard_map/ppermute | solution.py:19
  17.5 2.0 %collective-permute-done.3.refs_1_ = bf16[192,256]{1,0:T(8,128)(2,1)S(1)} collective-permute-done((bf16[192,256]{1,0:T(8,128)(2,1)}, bf16[192,256]{1,0:T(8,128)(2,1)S(1)}, u32[]{:S(2)}, u32[]{:S(2)}) %collective-permute-start.3) | collective-permute-done | bytes 98336 | tf_op jit(solution)/shard_map/ppermute | solution.py:19
  19.5 0.0 collective-permute-start.7
  19.6 1.2 %collective-permute-done.4.refs_2_ = bf16[192,256]{1,0:T(8,128)(2,1)S(1)} collective-permute-done((bf16[192,256]{1,0:T(8,128)(2,1)}, bf16[192,256]{1,0:T(8,128)(2,1)S(1)}, u32[]{:S(2)}, u32[]{:S(2)}) %collective-permute-start.4) | collective-permute-done | bytes 98336 | tf_op jit(solution)/shard_map/ppermute | solution.py:19
  20.8 0.0 collective-permute-start.8
  20.8 2.0 %collective-permute-done.5.refs_3_ = bf16[192,256]{1,0:T(8,128)(2,1)S(1)} collective-permute-done((bf16[192,256]{1,0:T(8,128)(2,1)}, bf16[192,256]{1,0:T(8,128)(2,1)S(1)}, u32[]{:S(2)}, u32[]{:S(2)}) %collective-permute-start.5) | collective-permute-done | bytes 98336 | tf_op jit(solution)/shard_map/ppermute | solution.py:19
  22.7 0.0 collective-permute-start.9
  22.8 0.6 %pad_add_fusion.where_ref = s32[2]{0:T(128)} fusion(s32[1]{0:T(128)} %bitcast.1, s32[1]{0:T(128)} %bitcast.me_ref), kind=kLoop, calls=%fused_computation | loop fusion | flops 2 | bytes 16 | tf_op jit(solution)/shard_map/stack | solution.py:109
  23.4 0.6 %collective-permute-done.9.refs_7_ = bf16[192,256]{1,0:T(8,128)(2,1)S(1)} collective-permute-done((bf16[192,256]{1,0:T(8,128)(2,1)S(1)}, bf16[192,256]{1,0:T(8,128)(2,1)S(1)}, u32[]{:S(2)}, u32[]{:S(2)}) %collective-permute-start.9) | collective-permute-done | bytes 98336 | tf_op jit(solution)/shard_map/ppermute | solution.py:19
  24.1 0.0 copy-done.5
  24.1 0.6 %copy-done.6 = bf16[192,256]{1,0:T(8,128)(2,1)} copy-done((bf16[192,256]{1,0:T(8,128)(2,1)}, bf16[192,256]{1,0:T(8,128)(2,1)S(1)}, u32[]{:S(2)}) %copy-start.6) | copy-done | bytes 98328
  24.7 2.8 %attend.1 = bf16[128,256]{1,0:T(8,128)(2,1)} custom-call(s32[2]{0:T(128)} %pad_add_fusion.where_ref, s32[16,3]{1,0:T(8,128)} %copy.5.selected_ref, bf16[128,256]{1,0:T(8,128)(2,1)} %queries_ref.1, bf16[192,256]{1,0:T(8,128)(2,1)} %get-tuple-element.9.refs_0_, bf16[192,256]{1,0:T(8,128)(2,1)} %copy-done, bf16[192,256]{1,0:T(8,128)(2,1)} %copy-done.1, ...), custom_call_target="tpu_custom_call" | custom-call | tf_op jit(solution)/shard_map/attend/pallas_call | solution.py:88
  (22 shorter events, 0.0 us)
Async XLA Ops:
  0.0 7.0 %collective-permute-start.1 = (bf16[64,256]{1,0:T(8,128)(2,1)}, bf16[64,256]{1,0:T(8,128)(2,1)S(1)}, u32[]{:S(2)}, u32[]{:S(2)}) collective-permute-start(bf16[64,256]{1,0:T(8,128)(2,1)} %refs_0_.1), channel_id=1, source_target_pairs={{0,16},{2,18},{4,20},{6,22},{8,24},{10,26},{12,28},{14,30},{16,0},... | collective-permute-start | bytes 98312 | tf_op jit(solution)/shard_map/ppermute | solution.py:19
  4.0 4.1 %collective-permute-start = (bf16[64,256]{1,0:T(8,128)(2,1)}, bf16[64,256]{1,0:T(8,128)(2,1)S(1)}, u32[]{:S(2)}, u32[]{:S(2)}) collective-permute-start(bf16[64,256]{1,0:T(8,128)(2,1)} %refs_0_.1), channel_id=1, source_target_pairs={{0,8},{2,10},{4,12},{6,14},{8,0},{10,2},{12,4},{14,6},{16,24},{18,... | collective-permute-start | bytes 98312 | tf_op jit(solution)/shard_map/ppermute | solution.py:19
  5.6 5.9 %collective-permute-start.2 = (bf16[64,256]{1,0:T(8,128)(2,1)}, bf16[64,256]{1,0:T(8,128)(2,1)S(1)}, u32[]{:S(2)}, u32[]{:S(2)}) collective-permute-start(bf16[64,256]{1,0:T(8,128)(2,1)} %refs_0_.1), channel_id=1, source_target_pairs={{0,24},{2,26},{4,28},{6,30},{8,16},{10,18},{12,20},{14,22},{16,8},... | collective-permute-start | bytes 98312 | tf_op jit(solution)/shard_map/ppermute | solution.py:19
  5.6 0.7 %copy-start.10 = (s32[16,3]{0,1:T(4,128)S(1)}, s32[16,3]{0,1:T(4,128)}, u32[]{:S(2)}) copy-start(s32[16,3]{0,1:T(4,128)} %param.5) | copy-start | bytes 580
  7.0 4.6 %copy-start.7 = (bf16[64,256]{1,0:T(8,128)(2,1)}, bf16[64,256]{1,0:T(8,128)(2,1)S(1)}, u32[]{:S(2)}) copy-start(bf16[64,256]{1,0:T(8,128)(2,1)S(1)} %collective-permute-done.1.refs_2_) | copy-start | bytes 98308
  8.2 3.4 %copy-start.8 = (bf16[64,256]{1,0:T(8,128)(2,1)}, bf16[64,256]{1,0:T(8,128)(2,1)S(1)}, u32[]{:S(2)}) copy-start(bf16[64,256]{1,0:T(8,128)(2,1)S(1)} %collective-permute-done.refs_1_) | copy-start | bytes 98308
  11.5 0.6 %copy-start.9 = (bf16[64,256]{1,0:T(8,128)(2,1)}, bf16[64,256]{1,0:T(8,128)(2,1)S(1)}, u32[]{:S(2)}) copy-start(bf16[64,256]{1,0:T(8,128)(2,1)S(1)} %collective-permute-done.2.refs_3_) | copy-start | bytes 98308
  14.0 5.5 %collective-permute-start.3 = (bf16[192,256]{1,0:T(8,128)(2,1)}, bf16[192,256]{1,0:T(8,128)(2,1)S(1)}, u32[]{:S(2)}, u32[]{:S(2)}) collective-permute-start(bf16[192,256]{1,0:T(8,128)(2,1)} %get-tuple-element.10), channel_id=1, source_target_pairs={{0,2},{2,0},{4,6},{6,4},{8,10},{10,8},{12,14},{14,12},{16,18},{18,... | collective-permute-start | bytes 294920 | tf_op jit(solution)/shard_map/ppermute | solution.py:19
  15.5 5.3 %collective-permute-start.4 = (bf16[192,256]{1,0:T(8,128)(2,1)}, bf16[192,256]{1,0:T(8,128)(2,1)S(1)}, u32[]{:S(2)}, u32[]{:S(2)}) collective-permute-start(bf16[192,256]{1,0:T(8,128)(2,1)} %get-tuple-element.11), channel_id=1, source_target_pairs={{0,4},{2,6},{4,0},{6,2},{8,12},{10,14},{12,8},{14,10},{16,20},{18,... | collective-permute-start | bytes 294920 | tf_op jit(solution)/shard_map/ppermute | solution.py:19
  17.0 5.7 %collective-permute-start.5 = (bf16[192,256]{1,0:T(8,128)(2,1)}, bf16[192,256]{1,0:T(8,128)(2,1)S(1)}, u32[]{:S(2)}, u32[]{:S(2)}) collective-permute-start(bf16[192,256]{1,0:T(8,128)(2,1)} %get-tuple-element.12), channel_id=1, source_target_pairs={{0,6},{2,4},{4,2},{6,0},{8,14},{10,12},{12,10},{14,8},{16,22},{18,... | collective-permute-start | bytes 294920 | tf_op jit(solution)/shard_map/ppermute | solution.py:19
  17.5 5.9 %collective-permute-start.6 = (bf16[192,256]{1,0:T(8,128)(2,1)}, bf16[192,256]{1,0:T(8,128)(2,1)S(1)}, u32[]{:S(2)}, u32[]{:S(2)}) collective-permute-start(bf16[192,256]{1,0:T(8,128)(2,1)} %get-tuple-element.9.refs_0_), channel_id=1, source_target_pairs={{0,1},{1,0},{2,3},{3,2},{4,5},{5,4},{6,7},{7,6},{8,9},{9,8},{10,11... | collective-permute-start | bytes 294920 | tf_op jit(solution)/shard_map/ppermute | solution.py:19
  19.5 4.5 %copy-start = (bf16[192,256]{1,0:T(8,128)(2,1)}, bf16[192,256]{1,0:T(8,128)(2,1)S(1)}, u32[]{:S(2)}) copy-start(bf16[192,256]{1,0:T(8,128)(2,1)S(1)} %collective-permute-done.3.refs_1_) | copy-start | bytes 294916
  19.5 3.8 %collective-permute-start.7 = (bf16[192,256]{1,0:T(8,128)(2,1)S(1)}, bf16[192,256]{1,0:T(8,128)(2,1)S(1)}, u32[]{:S(2)}, u32[]{:S(2)}) collective-permute-start(bf16[192,256]{1,0:T(8,128)(2,1)S(1)} %collective-permute-done.3.refs_1_), channel_id=1, source_target_pairs={{0,1},{1,0},{2,3},{3,2},{4,5},{5,4},{6,7},{7,6},{8,9},{9,8},{10,11... | collective-permute-start | bytes 294920 | tf_op jit(solution)/shard_map/ppermute | solution.py:19
  20.8 3.3 %copy-start.1 = (bf16[192,256]{1,0:T(8,128)(2,1)}, bf16[192,256]{1,0:T(8,128)(2,1)S(1)}, u32[]{:S(2)}) copy-start(bf16[192,256]{1,0:T(8,128)(2,1)S(1)} %collective-permute-done.4.refs_2_) | copy-start | bytes 294916
  20.8 2.6 %collective-permute-start.8 = (bf16[192,256]{1,0:T(8,128)(2,1)S(1)}, bf16[192,256]{1,0:T(8,128)(2,1)S(1)}, u32[]{:S(2)}, u32[]{:S(2)}) collective-permute-start(bf16[192,256]{1,0:T(8,128)(2,1)S(1)} %collective-permute-done.4.refs_2_), channel_id=1, source_target_pairs={{0,1},{1,0},{2,3},{3,2},{4,5},{5,4},{6,7},{7,6},{8,9},{9,8},{10,11... | collective-permute-start | bytes 294920 | tf_op jit(solution)/shard_map/ppermute | solution.py:19
  22.7 1.3 %copy-start.2 = (bf16[192,256]{1,0:T(8,128)(2,1)}, bf16[192,256]{1,0:T(8,128)(2,1)S(1)}, u32[]{:S(2)}) copy-start(bf16[192,256]{1,0:T(8,128)(2,1)S(1)} %collective-permute-done.5.refs_3_) | copy-start | bytes 294916
  22.7 1.3 %collective-permute-start.9 = (bf16[192,256]{1,0:T(8,128)(2,1)S(1)}, bf16[192,256]{1,0:T(8,128)(2,1)S(1)}, u32[]{:S(2)}, u32[]{:S(2)}) collective-permute-start(bf16[192,256]{1,0:T(8,128)(2,1)S(1)} %collective-permute-done.5.refs_3_), channel_id=1, source_target_pairs={{0,1},{1,0},{2,3},{3,2},{4,5},{5,4},{6,7},{7,6},{8,9},{9,8},{10,11... | collective-permute-start | bytes 294920 | tf_op jit(solution)/shard_map/ppermute | solution.py:19
  23.4 0.7 %copy-start.3 = (bf16[192,256]{1,0:T(8,128)(2,1)}, bf16[192,256]{1,0:T(8,128)(2,1)S(1)}, u32[]{:S(2)}) copy-start(bf16[192,256]{1,0:T(8,128)(2,1)S(1)} %collective-permute-done.6.refs_4_) | copy-start | bytes 294916
  23.4 0.7 %copy-start.4 = (bf16[192,256]{1,0:T(8,128)(2,1)}, bf16[192,256]{1,0:T(8,128)(2,1)S(1)}, u32[]{:S(2)}) copy-start(bf16[192,256]{1,0:T(8,128)(2,1)S(1)} %collective-permute-done.7.refs_5_) | copy-start | bytes 294916
  23.4 0.7 %copy-start.5 = (bf16[192,256]{1,0:T(8,128)(2,1)}, bf16[192,256]{1,0:T(8,128)(2,1)S(1)}, u32[]{:S(2)}) copy-start(bf16[192,256]{1,0:T(8,128)(2,1)S(1)} %collective-permute-done.8.refs_6_) | copy-start | bytes 294916
  24.1 0.6 %copy-start.6 = (bf16[192,256]{1,0:T(8,128)(2,1)}, bf16[192,256]{1,0:T(8,128)(2,1)S(1)}, u32[]{:S(2)}) copy-start(bf16[192,256]{1,0:T(8,128)(2,1)S(1)} %collective-permute-done.9.refs_7_) | copy-start | bytes 294916

commit v2 on v1

v2 whole, which is shorter than its diff:
```python
import functools

import jax
import jax.numpy as jnp
from jax import lax
from jax.experimental import pallas as pl
from jax.experimental.pallas import tpu as pltpu
from jax.sharding import PartitionSpec as P

DH = 128
GROUP = 4
TOPK = 3
LOG2E = 1.4426950408889634
LOW = -3e38
VMEM = 16 << 20


def swapped(rows, axis, step):
    count = lax.axis_size(axis)
    return lax.ppermute(rows, axis, [(i, i ^ step) for i in range(count)])


def kernel_call(body, out_shape, name, smem, vmem):
    return pl.pallas_call(
        body,
        out_shape=out_shape,
        in_specs=[pl.BlockSpec(memory_space=pltpu.SMEM)] * len(smem)
        + [pl.BlockSpec(memory_space=pltpu.VMEM)] * len(vmem),
        out_specs=jax.tree.map(lambda _: pl.BlockSpec(memory_space=pltpu.VMEM), out_shape),
        compiler_params=pltpu.CompilerParams(vmem_limit_bytes=VMEM),
        name=name,
    )(*smem, *vmem)


def pick_kernel(columns, blocks, selected_ref, *refs):
    held, messages = refs[:blocks], refs[blocks:]
    rows = held[0].shape[0]
    me = lax.axis_index("seq")
    mine = me // GROUP
    for step in range(GROUP):
        messages[step][0:rows, :] = held[0][...]
        for column in range(1, columns):
            wanted = selected_ref[me ^ step, column] ^ mine
            for index in range(1, blocks):

                @pl.when(wanted == index)
                def _():
                    messages[step][column * rows : (column + 1) * rows, :] = held[index][...]


def pick(columns, selected, held):
    rows, width = held[0].shape
    message = jax.ShapeDtypeStruct((columns * rows, width), held[0].dtype)
    body = functools.partial(pick_kernel, columns, len(held))
    return kernel_call(body, [message] * GROUP, f"pick_{columns}", [selected], held)


def attend_kernel(columns, queries_ref, *refs):
    pieces, out_ref = refs[:-1], refs[-1]
    tokens, width = queries_ref.shape
    heads = width // DH
    length = pieces[0].shape[0]
    rows = length // columns
    part = lax.axis_index("seq") % GROUP
    head = lax.axis_index("head")
    queries = queries_ref[...]
    stacked = jnp.concatenate([queries[:, h * DH : (h + 1) * DH] for h in range(heads)], axis=0)
    kv = jnp.concatenate([piece[...] for piece in pieces], axis=0)
    scores = lax.dot_general(
        stacked, kv[:, :DH], (((1,), (1,)), ((), ())), preferred_element_type=jnp.float32
    ) * (DH ** (-0.5) * LOG2E)
    lane = lax.broadcasted_iota(jnp.int32, (1, length), 1)
    positions = []
    for index in range(len(pieces)):
        step, other = index % GROUP, index // GROUP
        position = (part ^ step) * tokens + (head ^ other) * rows + lane
        positions.append(jnp.where(lane < rows, position, 0))
    position = jnp.concatenate(positions, axis=1)
    token = lax.broadcasted_iota(jnp.int32, (heads * tokens, 1), 0) % tokens
    scores = jnp.where(position <= part * tokens + token, scores, LOW)
    top = jnp.max(scores, axis=1, keepdims=True)
    weights = jnp.exp2(scores - top)
    total = jnp.sum(weights, axis=1, keepdims=True)
    out = jnp.dot(weights.astype(jnp.bfloat16), kv[:, DH:], preferred_element_type=jnp.float32) / total
    for h in range(heads):
        out_ref[:, h * DH : (h + 1) * DH] = out[h * tokens : (h + 1) * tokens].astype(out_ref.dtype)


def attend(columns, queries, pieces):
    out = jax.ShapeDtypeStruct(queries.shape, queries.dtype)
    body = functools.partial(attend_kernel, columns)
    return kernel_call(body, out, f"attend_{columns}", [], [queries] + pieces)


def plane(columns, queries, selected, held):
    own = [held[0]] * GROUP if columns == 1 else pick(columns, selected, held)
    near = [own[0]] + [None] * (GROUP - 1)
    for step in (3, 1, 2):
        near[step] = swapped(own[step], "seq", step)
    far = [swapped(piece, "head", 1) for piece in near]
    return attend(columns, queries, near + far)


def shards(queries, keys_values, selected):
    blocks = lax.axis_size("seq") // GROUP
    mine = lax.axis_index("seq") // GROUP
    held = {0: keys_values}
    for step in range(blocks - 1, 0, -1):
        held[step] = swapped(keys_values, "seq", step * GROUP)
    held = [held[step] for step in range(blocks)]
    branches = [functools.partial(plane, columns) for columns in range(1, TOPK + 1)]
    return lax.switch(jnp.minimum(mine, TOPK - 1), branches, queries, selected, held)


def solution(mesh):
    in_specs = (P("seq", "head"), P(("seq", "head"), None), P())
    out_specs = P("seq", "head")
    return jax.shard_map(shards, mesh=mesh, in_specs=in_specs, out_specs=out_specs, check_vma=False)
```

time: 27.8 us -> 21.7 us (0.78)
  Pallas kernels: 4.63 us -> 1.29 us
  local copies, waits for them, and re-layouts: 2.62 us -> 0.63 us
  other arithmetic: 0.61 us -> 0 us
    pallas_call x2 -> x1, Pallas kernels: 4.63 us -> 1.29 us  [kernel_call(): pl.pallas_call(body, out_shape=out_shape, in_specs=[pl.BlockSpec(memory_s...]
    unnamed x23 -> x6, local copies, waits for them, and re-layouts: 2.62 us -> 0.63 us
    another operation x1 -> x0, other arithmetic: 0.61 us -> none  [shards(): return attend(jnp.stack([me, head]), selected, queries, near + far)]
  transfers between devices with their start and end apart: 10 -> 10, of which waited for: 6 -> 8; matrix products, arithmetic and copies ran while one was open for 5% -> 0% of each run, Pallas kernels for 0% -> 0%
where the time goes in v2:
time: 21.7 us; the launch traced here: 21.6 us
  waiting for transfers between devices  10.5 us (48%)
  starting transfers between devices  9.12 us (42%)
  Pallas kernels  1.29 us (6%)
  local copies, waits for them, and re-layouts  0.63 us (3%)
    ppermute x10, waiting for transfers between devices, swapped(): return lax.ppermute(rows, axis, [(i, i ^ step) for i in range(count)])  10.5 us
    ppermute x10, starting transfers between devices, swapped(): return lax.ppermute(rows, axis, [(i, i ^ step) for i in range(count)])  9.12 us
    pallas_call x1, Pallas kernels, kernel_call(): pl.pallas_call(body, out_shape=out_shape, in_specs=[pl.BlockSpec(memory_s...  1.29 us
    unnamed x6, local copies, waits for them, and re-layouts  0.63 us
  transfers between devices with their start and end apart: 10, of which 8 were waited for; matrix products, arithmetic and copies ran while one was open for 0% of the time, Pallas kernels for 0%

profile of v2, /device:TPU:0, one launch (start us, length us, event | category | flops | bytes accessed | tf_op | source)
XLA Modules:
  0.0 21.6 jit_solution(15740971746151024280)
XLA Ops:
  0.0 4.0 %collective-permute-start.22 = (bf16[64,256]{1,0:T(8,128)(2,1)}, bf16[64,256]{1,0:T(8,128)(2,1)S(1)}, u32[]{:S(2)}, u32[]{:S(2)}) collective-permute-start(bf16[64,256]{1,0:T(8,128)(2,1)} %param.7), channel_id=1, source_target_pairs={{0,16},{2,18},{4,20},{6,22},{8,24},{10,26},{12,28},{14,30},{16,0},... | collective-permute-start | bytes 98312 | tf_op jit(solution)/shard_map/ppermute | solution.py:20
  4.0 1.6 %collective-permute-start.21 = (bf16[64,256]{1,0:T(8,128)(2,1)}, bf16[64,256]{1,0:T(8,128)(2,1)S(1)}, u32[]{:S(2)}, u32[]{:S(2)}) collective-permute-start(bf16[64,256]{1,0:T(8,128)(2,1)} %param.7), channel_id=1, source_target_pairs={{0,8},{2,10},{4,12},{6,14},{8,0},{10,2},{12,4},{14,6},{16,24},{18,... | collective-permute-start | bytes 98312 | tf_op jit(solution)/shard_map/ppermute | solution.py:20
  5.6 0.0 collective-permute-start.23
  5.6 1.1 %collective-permute-done.22 = bf16[64,256]{1,0:T(8,128)(2,1)S(1)} collective-permute-done((bf16[64,256]{1,0:T(8,128)(2,1)}, bf16[64,256]{1,0:T(8,128)(2,1)S(1)}, u32[]{:S(2)}, u32[]{:S(2)}) %collective-permute-start.22) | collective-permute-done | bytes 32800 | tf_op jit(solution)/shard_map/ppermute | solution.py:20
  6.7 1.5 %collective-permute-done.21 = bf16[64,256]{1,0:T(8,128)(2,1)S(1)} collective-permute-done((bf16[64,256]{1,0:T(8,128)(2,1)}, bf16[64,256]{1,0:T(8,128)(2,1)S(1)}, u32[]{:S(2)}, u32[]{:S(2)}) %collective-permute-start.21) | collective-permute-done | bytes 32800 | tf_op jit(solution)/shard_map/ppermute | solution.py:20
  8.2 3.4 %collective-permute-done.23 = bf16[64,256]{1,0:T(8,128)(2,1)S(1)} collective-permute-done((bf16[64,256]{1,0:T(8,128)(2,1)}, bf16[64,256]{1,0:T(8,128)(2,1)S(1)}, u32[]{:S(2)}, u32[]{:S(2)}) %collective-permute-start.23) | collective-permute-done | bytes 32800 | tf_op jit(solution)/shard_map/ppermute | solution.py:20
  11.5 9.4 %conditional.1 = (bf16[128,256]{1,0:T(8,128)(2,1)S(1)}) conditional(s32[]{:T(128)} %clamp.3, (bf16[64,256]{1,0:T(8,128)(2,1)S(1)}, bf16[128,256]{1,0:T(8,128)(2,1)}) %tuple.24, (s32[16,3]{0,1:T(4,128)S(1)}, bf16[64,256]{1,0:T(8,128)(2,1)S(1)}, bf16[64,256]{1,0:T(8,128)(2,1)S(1)}, bf16[64,256]{1,0:T(8,128)(2,1)S(1)}, ...), branch_computations={%region_0.1_spmd, %region_1.2_spmd, %region_2.3_spmd} | conditional | bytes 3015356 | solution.py:112
  11.5 2.4 %collective-permute-start.2 = (bf16[64,256]{1,0:T(8,128)(2,1)S(1)}, bf16[64,256]{1,0:T(8,128)(2,1)S(1)}, u32[]{:S(2)}, u32[]{:S(2)}) collective-permute-start(bf16[64,256]{1,0:T(8,128)(2,1)S(1)} %get-tuple-element.38.refs_0_), channel_id=1, source_target_pairs={{0,6},{2,4},{4,2},{6,0},{8,14},{10,12},{12,10},{14,8},{16,22},{18,... | collective-permute-start | bytes 98312 | tf_op jit(solution)/shard_map/cond/branch_0_fun/ppermute | solution.py:20
  14.0 0.5 %collective-permute-start.1 = (bf16[64,256]{1,0:T(8,128)(2,1)S(1)}, bf16[64,256]{1,0:T(8,128)(2,1)S(1)}, u32[]{:S(2)}, u32[]{:S(2)}) collective-permute-start(bf16[64,256]{1,0:T(8,128)(2,1)S(1)} %get-tuple-element.38.refs_0_), channel_id=1, source_target_pairs={{0,4},{2,6},{4,0},{6,2},{8,12},{10,14},{12,8},{14,10},{16,20},{18,... | collective-permute-start | bytes 98312 | tf_op jit(solution)/shard_map/cond/branch_0_fun/ppermute | solution.py:20
  14.5 0.5 %collective-permute-start = (bf16[64,256]{1,0:T(8,128)(2,1)S(1)}, bf16[64,256]{1,0:T(8,128)(2,1)S(1)}, u32[]{:S(2)}, u32[]{:S(2)}) collective-permute-start(bf16[64,256]{1,0:T(8,128)(2,1)S(1)} %get-tuple-element.38.refs_0_), channel_id=1, source_target_pairs={{0,2},{2,0},{4,6},{6,4},{8,10},{10,8},{12,14},{14,12},{16,18},{18,... | collective-permute-start | bytes 98312 | tf_op jit(solution)/shard_map/cond/branch_0_fun/ppermute | solution.py:20
  15.0 0.0 collective-permute-start.3
  15.0 1.4 %collective-permute-done.2.refs_3_ = bf16[64,256]{1,0:T(8,128)(2,1)S(1)} collective-permute-done((bf16[64,256]{1,0:T(8,128)(2,1)S(1)}, bf16[64,256]{1,0:T(8,128)(2,1)S(1)}, u32[]{:S(2)}, u32[]{:S(2)}) %collective-permute-start.2) | collective-permute-done | bytes 32800 | tf_op jit(solution)/shard_map/cond/branch_0_fun/ppermute | solution.py:20
  16.4 0.0 collective-permute-start.6
  16.4 1.5 %collective-permute-done.1.refs_2_ = bf16[64,256]{1,0:T(8,128)(2,1)S(1)} collective-permute-done((bf16[64,256]{1,0:T(8,128)(2,1)S(1)}, bf16[64,256]{1,0:T(8,128)(2,1)S(1)}, u32[]{:S(2)}, u32[]{:S(2)}) %collective-permute-start.1) | collective-permute-done | bytes 32800 | tf_op jit(solution)/shard_map/cond/branch_0_fun/ppermute | solution.py:20
  17.9 0.0 collective-permute-start.5
  17.9 0.5 %collective-permute-done.refs_1_ = bf16[64,256]{1,0:T(8,128)(2,1)S(1)} collective-permute-done((bf16[64,256]{1,0:T(8,128)(2,1)S(1)}, bf16[64,256]{1,0:T(8,128)(2,1)S(1)}, u32[]{:S(2)}, u32[]{:S(2)}) %collective-permute-start) | collective-permute-done | bytes 32800 | tf_op jit(solution)/shard_map/cond/branch_0_fun/ppermute | solution.py:20
  18.4 0.0 collective-permute-start.4
  18.4 0.0 collective-permute-done.3.refs_4_
  18.4 0.0 collective-permute-done.6.refs_7_
  18.4 0.7 %collective-permute-done.5.refs_6_ = bf16[64,256]{1,0:T(8,128)(2,1)S(1)} collective-permute-done((bf16[64,256]{1,0:T(8,128)(2,1)S(1)}, bf16[64,256]{1,0:T(8,128)(2,1)S(1)}, u32[]{:S(2)}, u32[]{:S(2)}) %collective-permute-start.5) | collective-permute-done | bytes 32800 | tf_op jit(solution)/shard_map/cond/branch_0_fun/ppermute | solution.py:20
  19.1 0.5 %collective-permute-done.4.refs_5_ = bf16[64,256]{1,0:T(8,128)(2,1)S(1)} collective-permute-done((bf16[64,256]{1,0:T(8,128)(2,1)S(1)}, bf16[64,256]{1,0:T(8,128)(2,1)S(1)}, u32[]{:S(2)}, u32[]{:S(2)}) %collective-permute-start.4) | collective-permute-done | bytes 32800 | tf_op jit(solution)/shard_map/cond/branch_0_fun/ppermute | solution.py:20
  19.6 1.3 %attend_1.1 = bf16[128,256]{1,0:T(8,128)(2,1)S(1)} custom-call(bf16[128,256]{1,0:T(8,128)(2,1)} %get-tuple-element.36.queries_ref, bf16[64,256]{1,0:T(8,128)(2,1)S(1)} %get-tuple-element.38.refs_0_, bf16[64,256]{1,0:T(8,128)(2,1)S(1)} %collective-permute-done.refs_1_, bf16[64,256]{1,0:T(8,128)(2,1)S(1)} %collective-permute-done.1.refs_2_, ...), custom_call_target="tpu_custom_call" | custom-call | tf_op jit(solution)/shard_map/cond/branch_0_fun/attend_1/pallas_call | solution.py:24
  20.9 0.0 copy-start.3
  20.9 0.6 %copy-done.3 = bf16[128,256]{1,0:T(8,128)(2,1)} copy-done((bf16[128,256]{1,0:T(8,128)(2,1)}, bf16[128,256]{1,0:T(8,128)(2,1)S(1)}, u32[]{:S(2)}) %copy-start.3) | copy-done | bytes 65560
  (4 shorter events, 0.0 us)
Async XLA Ops:
  0.0 11.5 %copy-start.2 = (bf16[64,256]{1,0:T(8,128)(2,1)S(1)}, bf16[64,256]{1,0:T(8,128)(2,1)}, u32[]{:S(2)}) copy-start(bf16[64,256]{1,0:T(8,128)(2,1)} %param.7) | copy-start | bytes 98308
  0.0 6.7 %collective-permute-start.22 = (bf16[64,256]{1,0:T(8,128)(2,1)}, bf16[64,256]{1,0:T(8,128)(2,1)S(1)}, u32[]{:S(2)}, u32[]{:S(2)}) collective-permute-start(bf16[64,256]{1,0:T(8,128)(2,1)} %param.7), channel_id=1, source_target_pairs={{0,16},{2,18},{4,20},{6,22},{8,24},{10,26},{12,28},{14,30},{16,0},... | collective-permute-start | bytes 98312 | tf_op jit(solution)/shard_map/ppermute | solution.py:20
  4.0 4.1 %collective-permute-start.21 = (bf16[64,256]{1,0:T(8,128)(2,1)}, bf16[64,256]{1,0:T(8,128)(2,1)S(1)}, u32[]{:S(2)}, u32[]{:S(2)}) collective-permute-start(bf16[64,256]{1,0:T(8,128)(2,1)} %param.7), channel_id=1, source_target_pairs={{0,8},{2,10},{4,12},{6,14},{8,0},{10,2},{12,4},{14,6},{16,24},{18,... | collective-permute-start | bytes 98312 | tf_op jit(solution)/shard_map/ppermute | solution.py:20
  5.6 5.9 %collective-permute-start.23 = (bf16[64,256]{1,0:T(8,128)(2,1)}, bf16[64,256]{1,0:T(8,128)(2,1)S(1)}, u32[]{:S(2)}, u32[]{:S(2)}) collective-permute-start(bf16[64,256]{1,0:T(8,128)(2,1)} %param.7), channel_id=1, source_target_pairs={{0,24},{2,26},{4,28},{6,30},{8,16},{10,18},{12,20},{14,22},{16,8},... | collective-permute-start | bytes 98312 | tf_op jit(solution)/shard_map/ppermute | solution.py:20
  5.6 5.9 %copy-start.4 = (s32[16,3]{0,1:T(4,128)S(1)}, s32[16,3]{0,1:T(4,128)}, u32[]{:S(2)}) copy-start(s32[16,3]{0,1:T(4,128)} %param.8) | copy-start | bytes 580
  11.5 4.9 %collective-permute-start.2 = (bf16[64,256]{1,0:T(8,128)(2,1)S(1)}, bf16[64,256]{1,0:T(8,128)(2,1)S(1)}, u32[]{:S(2)}, u32[]{:S(2)}) collective-permute-start(bf16[64,256]{1,0:T(8,128)(2,1)S(1)} %get-tuple-element.38.refs_0_), channel_id=1, source_target_pairs={{0,6},{2,4},{4,2},{6,0},{8,14},{10,12},{12,10},{14,8},{16,22},{18,... | collective-permute-start | bytes 98312 | tf_op jit(solution)/shard_map/cond/branch_0_fun/ppermute | solution.py:20
  14.0 3.9 %collective-permute-start.1 = (bf16[64,256]{1,0:T(8,128)(2,1)S(1)}, bf16[64,256]{1,0:T(8,128)(2,1)S(1)}, u32[]{:S(2)}, u32[]{:S(2)}) collective-permute-start(bf16[64,256]{1,0:T(8,128)(2,1)S(1)} %get-tuple-element.38.refs_0_), channel_id=1, source_target_pairs={{0,4},{2,6},{4,0},{6,2},{8,12},{10,14},{12,8},{14,10},{16,20},{18,... | collective-permute-start | bytes 98312 | tf_op jit(solution)/shard_map/cond/branch_0_fun/ppermute | solution.py:20
  14.5 3.9 %collective-permute-start = (bf16[64,256]{1,0:T(8,128)(2,1)S(1)}, bf16[64,256]{1,0:T(8,128)(2,1)S(1)}, u32[]{:S(2)}, u32[]{:S(2)}) collective-permute-start(bf16[64,256]{1,0:T(8,128)(2,1)S(1)} %get-tuple-element.38.refs_0_), channel_id=1, source_target_pairs={{0,2},{2,0},{4,6},{6,4},{8,10},{10,8},{12,14},{14,12},{16,18},{18,... | collective-permute-start | bytes 98312 | tf_op jit(solution)/shard_map/cond/branch_0_fun/ppermute | solution.py:20
  15.0 3.4 %collective-permute-start.3 = (bf16[64,256]{1,0:T(8,128)(2,1)S(1)}, bf16[64,256]{1,0:T(8,128)(2,1)S(1)}, u32[]{:S(2)}, u32[]{:S(2)}) collective-permute-start(bf16[64,256]{1,0:T(8,128)(2,1)S(1)} %get-tuple-element.38.refs_0_), channel_id=1, source_target_pairs={{0,1},{1,0},{2,3},{3,2},{4,5},{5,4},{6,7},{7,6},{8,9},{9,8},{10,11... | collective-permute-start | bytes 98312 | tf_op jit(solution)/shard_map/cond/branch_0_fun/ppermute | solution.py:20
  16.4 2.0 %collective-permute-start.6 = (bf16[64,256]{1,0:T(8,128)(2,1)S(1)}, bf16[64,256]{1,0:T(8,128)(2,1)S(1)}, u32[]{:S(2)}, u32[]{:S(2)}) collective-permute-start(bf16[64,256]{1,0:T(8,128)(2,1)S(1)} %collective-permute-done.2.refs_3_), channel_id=1, source_target_pairs={{0,1},{1,0},{2,3},{3,2},{4,5},{5,4},{6,7},{7,6},{8,9},{9,8},{10,11... | collective-permute-start | bytes 98312 | tf_op jit(solution)/shard_map/cond/branch_0_fun/ppermute | solution.py:20
  17.9 1.2 %collective-permute-start.5 = (bf16[64,256]{1,0:T(8,128)(2,1)S(1)}, bf16[64,256]{1,0:T(8,128)(2,1)S(1)}, u32[]{:S(2)}, u32[]{:S(2)}) collective-permute-start(bf16[64,256]{1,0:T(8,128)(2,1)S(1)} %collective-permute-done.1.refs_2_), channel_id=1, source_target_pairs={{0,1},{1,0},{2,3},{3,2},{4,5},{5,4},{6,7},{7,6},{8,9},{9,8},{10,11... | collective-permute-start | bytes 98312 | tf_op jit(solution)/shard_map/cond/branch_0_fun/ppermute | solution.py:20
  18.4 1.2 %collective-permute-start.4 = (bf16[64,256]{1,0:T(8,128)(2,1)S(1)}, bf16[64,256]{1,0:T(8,128)(2,1)S(1)}, u32[]{:S(2)}, u32[]{:S(2)}) collective-permute-start(bf16[64,256]{1,0:T(8,128)(2,1)S(1)} %collective-permute-done.refs_1_), channel_id=1, source_target_pairs={{0,1},{1,0},{2,3},{3,2},{4,5},{5,4},{6,7},{7,6},{8,9},{9,8},{10,11... | collective-permute-start | bytes 98312 | tf_op jit(solution)/shard_map/cond/branch_0_fun/ppermute | solution.py:20
  20.9 0.6 %copy-start.3 = (bf16[128,256]{1,0:T(8,128)(2,1)}, bf16[128,256]{1,0:T(8,128)(2,1)S(1)}, u32[]{:S(2)}) copy-start(bf16[128,256]{1,0:T(8,128)(2,1)S(1)} %get-tuple-element.127) | copy-start | bytes 196612

commit v3 on v2

--- a/solution.py
+++ b/solution.py
@@ -32,6 +32,18 @@
     )(*smem, *vmem)
 
 
+def join_kernel(*refs):
+    rows = refs[0].shape[0]
+    for index, piece in enumerate(refs[:-1]):
+        refs[-1][index * rows : (index + 1) * rows, :] = piece[...]
+
+
+def join(pieces):
+    rows, width = pieces[0].shape
+    out = jax.ShapeDtypeStruct((len(pieces) * rows, width), pieces[0].dtype)
+    return kernel_call(join_kernel, out, "join", [], pieces)
+
+
 def pick_kernel(columns, blocks, selected_ref, *refs):
     held, messages = refs[:blocks], refs[blocks:]
     rows = held[0].shape[0]
@@ -40,27 +52,29 @@
     for step in range(GROUP):
         messages[step][0:rows, :] = held[0][...]
         for column in range(1, columns):
+            start = column * rows
+            if columns == 2:
+                messages[step][start : start + rows, :] = held[1][...]
+                continue
             wanted = selected_ref[me ^ step, column] ^ mine
             for index in range(1, blocks):
 
                 @pl.when(wanted == index)
                 def _():
-                    messages[step][column * rows : (column + 1) * rows, :] = held[index][...]
+                    messages[step][start : start + rows, :] = held[index][...]
 
 
 def pick(columns, selected, held):
     rows, width = held[0].shape
-    message = jax.ShapeDtypeStruct((columns * rows, width), held[0].dtype)
+    messages = [jax.ShapeDtypeStruct((columns * rows, width), held[0].dtype)] * GROUP
     body = functools.partial(pick_kernel, columns, len(held))
-    return kernel_call(body, [message] * GROUP, f"pick_{columns}", [selected], held)
+    return kernel_call(body, messages, f"pick_{columns}", [selected], held)
 
 
-def attend_kernel(columns, queries_ref, *refs):
+def attend_kernel(rows, places, queries_ref, *refs):
     pieces, out_ref = refs[:-1], refs[-1]
     tokens, width = queries_ref.shape
     heads = width // DH
-    length = pieces[0].shape[0]
-    rows = length // columns
     part = lax.axis_index("seq") % GROUP
     head = lax.axis_index("head")
     queries = queries_ref[...]
@@ -69,10 +83,10 @@
     scores = lax.dot_general(
         stacked, kv[:, :DH], (((1,), (1,)), ((), ())), preferred_element_type=jnp.float32
     ) * (DH ** (-0.5) * LOG2E)
-    lane = lax.broadcasted_iota(jnp.int32, (1, length), 1)
     positions = []
-    for index in range(len(pieces)):
-        step, other = index % GROUP, index // GROUP
+    for piece, place in zip(pieces, places):
+        lane = lax.broadcasted_iota(jnp.int32, (1, piece.shape[0]), 1)
+        step, other = place
         position = (part ^ step) * tokens + (head ^ other) * rows + lane
         positions.append(jnp.where(lane < rows, position, 0))
     position = jnp.concatenate(positions, axis=1)
@@ -86,19 +100,37 @@
         out_ref[:, h * DH : (h + 1) * DH] = out[h * tokens : (h + 1) * tokens].astype(out_ref.dtype)
 
 
-def attend(columns, queries, pieces):
+def attend(rows, queries, placed):
     out = jax.ShapeDtypeStruct(queries.shape, queries.dtype)
-    body = functools.partial(attend_kernel, columns)
-    return kernel_call(body, out, f"attend_{columns}", [], [queries] + pieces)
+    places, pieces = zip(*placed)
+    body = functools.partial(attend_kernel, rows, places)
+    return kernel_call(body, out, f"attend_{len(pieces)}", [], [queries, *pieces])
 
 
-def plane(columns, queries, selected, held):
-    own = [held[0]] * GROUP if columns == 1 else pick(columns, selected, held)
+def first_block(queries, rows):
+    diagonal = swapped(rows, "seq", 3)
+    beside = swapped(rows, "seq", 1)
+    diagonal, again = lax.optimization_barrier((diagonal, rows))
+    near = join([rows, beside, swapped(again, "seq", 2), diagonal])
+    far = swapped(near, "head", 1)
+    length = rows.shape[0]
+    placed = []
+    for other, piece in enumerate((near, far)):
+        for step in range(GROUP):
+            placed.append(((step, other), piece[step * length : (step + 1) * length]))
+    return attend(length, queries, placed)
+
+
+def later_block(columns, queries, selected, held):
+    own = pick(columns, selected, held)
     near = [own[0]] + [None] * (GROUP - 1)
     for step in (3, 1, 2):
         near[step] = swapped(own[step], "seq", step)
     far = [swapped(piece, "head", 1) for piece in near]
-    return attend(columns, queries, near + far)
+    placed = []
+    for step in range(GROUP):
+        placed += [((step, 0), near[step]), ((step, 1), far[step])]
+    return attend(held[0].shape[0], queries, placed)
 
 
 def shards(queries, keys_values, selected):
@@ -108,8 +140,14 @@
     for step in range(blocks - 1, 0, -1):
         held[step] = swapped(keys_values, "seq", step * GROUP)
     held = [held[step] for step in range(blocks)]
-    branches = [functools.partial(plane, columns) for columns in range(1, TOPK + 1)]
-    return lax.switch(jnp.minimum(mine, TOPK - 1), branches, queries, selected, held)
+    level = jnp.minimum(mine, TOPK - 1)
+    first = lax.cond(
+        level == 0,
+        lambda: first_block(queries, keys_values),
+        lambda: jnp.zeros_like(queries),
+    )
+    branches = [functools.partial(later_block, columns) for columns in range(2, TOPK + 1)]
+    return lax.switch(level, [lambda *_: first] + branches, queries, selected, held)
 
 
 def solution(mesh):

time: 21.7 us -> 19.7 us (0.908)
  the two profiles are of different devices: /device:TPU:0 before, /device:TPU:25 now
where the time goes in v3:
time: 19.7 us; the launch traced here: 19.5 us
  starting transfers between devices  14 us (71%)
  waiting for transfers between devices  2.97 us (15%)
  Pallas kernels  1.73 us (9%)
  local copies, waits for them, and re-layouts  0.73 us (4%)
    ppermute x10, starting transfers between devices, swapped(): return lax.ppermute(rows, axis, [(i, i ^ step) for i in range(count)])  14 us
    ppermute x10, waiting for transfers between devices, swapped(): return lax.ppermute(rows, axis, [(i, i ^ step) for i in range(count)])  2.97 us
    pallas_call x2, Pallas kernels, kernel_call(): pl.pallas_call(body, out_shape=out_shape, in_specs=[pl.BlockSpec(memory_s...  1.73 us
    unnamed x6, local copies, waits for them, and re-layouts  0.63 us
  transfers between devices with their start and end apart: 10, of which 3 were waited for; matrix products, arithmetic and copies ran while one was open for 0% of the time, Pallas kernels for 0%

profile of v3, /device:TPU:25, one launch (start us, length us, event | category | flops | bytes accessed | tf_op | source)
XLA Modules:
  0.0 19.5 jit_solution(8933235695264393707)
XLA Ops:
  0.0 0.1 collective-permute-start.19
  0.1 0.2 collective-permute-start.18
  0.2 3.3 %collective-permute-start.20 = (bf16[64,256]{1,0:T(8,128)(2,1)}, bf16[64,256]{1,0:T(8,128)(2,1)S(1)}, u32[]{:S(2)}, u32[]{:S(2)}) collective-permute-start(bf16[64,256]{1,0:T(8,128)(2,1)} %param.9), channel_id=1, source_target_pairs={{0,24},{2,26},{4,28},{6,30},{8,16},{10,18},{12,20},{14,22},{16,8},... | collective-permute-start | bytes 98312 | tf_op jit(solution)/shard_map/ppermute | solution.py:20
  3.6 0.5 %collective-permute-done.19 = bf16[64,256]{1,0:T(8,128)(2,1)S(1)} collective-permute-done((bf16[64,256]{1,0:T(8,128)(2,1)}, bf16[64,256]{1,0:T(8,128)(2,1)S(1)}, u32[]{:S(2)}, u32[]{:S(2)}) %collective-permute-start.19) | collective-permute-done | bytes 32800 | tf_op jit(solution)/shard_map/ppermute | solution.py:20
  4.1 0.0 collective-permute-done.18
  4.1 1.5 %collective-permute-done.20 = bf16[64,256]{1,0:T(8,128)(2,1)S(1)} collective-permute-done((bf16[64,256]{1,0:T(8,128)(2,1)}, bf16[64,256]{1,0:T(8,128)(2,1)S(1)}, u32[]{:S(2)}, u32[]{:S(2)}) %collective-permute-start.20) | collective-permute-done | bytes 32800 | tf_op jit(solution)/shard_map/ppermute | solution.py:20
  5.6 13.3 %conditional.3 = (bf16[128,256]{1,0:T(8,128)(2,1)S(1)}) conditional(s32[]{:T(128)} %clamp.3, bf16[128,256]{1,0:T(8,128)(2,1)S(1)} %get-tuple-element.93, (s32[16,3]{0,1:T(4,128)S(1)}, bf16[64,256]{1,0:T(8,128)(2,1)S(1)}, bf16[64,256]{1,0:T(8,128)(2,1)S(1)}, bf16[64,256]{1,0:T(8,128)(2,1)S(1)}, bf16[64,256]{1,0:T(8,128)(2,1)S(1)}, ...), branch_computations={%region_2.3_spmd, %region_3.4_spmd, %region_4.5_spmd} | conditional | bytes 3015356 | solution.py:150
  5.6 0.1 copy.10.selected_ref
  5.7 0.8 %pick_3.1 = (bf16[192,256]{1,0:T(8,128)(2,1)S(1)}, bf16[192,256]{1,0:T(8,128)(2,1)S(1)}, bf16[192,256]{1,0:T(8,128)(2,1)S(1)}, bf16[192,256]{1,0:T(8,128)(2,1)S(1)}) custom-call(s32[16,3]{1,0:T(8,128)S(1)} %copy.10.selected_ref, bf16[64,256]{1,0:T(8,128)(2,1)S(1)} %get-tuple-element.57.refs_0_, bf16[64,256]{1,0:T(8,128)(2,1)S(1)} %get-tuple-element.58.refs_1_, ...), custom_call_target="tpu_custom_call" | custom-call | tf_op jit(solution)/shard_map/cond/branch_2_fun/pick_3/pallas_call | solution.py:24
  6.5 1.3 %collective-permute-start.8 = (bf16[192,256]{1,0:T(8,128)(2,1)S(1)}, bf16[192,256]{1,0:T(8,128)(2,1)S(1)}, u32[]{:S(2)}, u32[]{:S(2)}) collective-permute-start(bf16[192,256]{1,0:T(8,128)(2,1)S(1)} %get-tuple-element.62), channel_id=1, source_target_pairs={{0,2},{2,0},{4,6},{6,4},{8,10},{10,8},{12,14},{14,12},{16,18},{18,... | collective-permute-start | bytes 294920 | tf_op jit(solution)/shard_map/cond/branch_2_fun/ppermute | solution.py:20
  7.8 1.2 %collective-permute-start.10 = (bf16[192,256]{1,0:T(8,128)(2,1)S(1)}, bf16[192,256]{1,0:T(8,128)(2,1)S(1)}, u32[]{:S(2)}, u32[]{:S(2)}) collective-permute-start(bf16[192,256]{1,0:T(8,128)(2,1)S(1)} %get-tuple-element.63), channel_id=1, source_target_pairs={{0,4},{2,6},{4,0},{6,2},{8,12},{10,14},{12,8},{14,10},{16,20},{18,... | collective-permute-start | bytes 294920 | tf_op jit(solution)/shard_map/cond/branch_2_fun/ppermute | solution.py:20
  9.0 0.2 %collective-permute-start.12 = (bf16[192,256]{1,0:T(8,128)(2,1)S(1)}, bf16[192,256]{1,0:T(8,128)(2,1)S(1)}, u32[]{:S(2)}, u32[]{:S(2)}) collective-permute-start(bf16[192,256]{1,0:T(8,128)(2,1)S(1)} %get-tuple-element.64), channel_id=1, source_target_pairs={{0,6},{2,4},{4,2},{6,0},{8,14},{10,12},{12,10},{14,8},{16,22},{18,... | collective-permute-start | bytes 294920 | tf_op jit(solution)/shard_map/cond/branch_2_fun/ppermute | solution.py:20
  9.2 2.8 %collective-permute-start.7 = (bf16[192,256]{1,0:T(8,128)(2,1)S(1)}, bf16[192,256]{1,0:T(8,128)(2,1)S(1)}, u32[]{:S(2)}, u32[]{:S(2)}) collective-permute-start(bf16[192,256]{1,0:T(8,128)(2,1)S(1)} %get-tuple-element.61.refs_0_), channel_id=1, source_target_pairs={{0,1},{1,0},{2,3},{3,2},{4,5},{5,4},{6,7},{7,6},{8,9},{9,8},{10,11... | collective-permute-start | bytes 294920 | tf_op jit(solution)/shard_map/cond/branch_2_fun/ppermute | solution.py:20
  12.0 0.0 collective-permute-done.8.refs_2_
  12.0 2.2 %collective-permute-start.9 = (bf16[192,256]{1,0:T(8,128)(2,1)S(1)}, bf16[192,256]{1,0:T(8,128)(2,1)S(1)}, u32[]{:S(2)}, u32[]{:S(2)}) collective-permute-start(bf16[192,256]{1,0:T(8,128)(2,1)S(1)} %collective-permute-done.8.refs_2_), channel_id=1, source_target_pairs={{0,1},{1,0},{2,3},{3,2},{4,5},{5,4},{6,7},{7,6},{8,9},{9,8},{10,11... | collective-permute-start | bytes 294920 | tf_op jit(solution)/shard_map/cond/branch_2_fun/ppermute | solution.py:20
  14.2 0.0 collective-permute-done.10.refs_4_
  14.2 1.3 %collective-permute-start.11 = (bf16[192,256]{1,0:T(8,128)(2,1)S(1)}, bf16[192,256]{1,0:T(8,128)(2,1)S(1)}, u32[]{:S(2)}, u32[]{:S(2)}) collective-permute-start(bf16[192,256]{1,0:T(8,128)(2,1)S(1)} %collective-permute-done.10.refs_4_), channel_id=1, source_target_pairs={{0,1},{1,0},{2,3},{3,2},{4,5},{5,4},{6,7},{7,6},{8,9},{9,8},{10,11... | collective-permute-start | bytes 294920 | tf_op jit(solution)/shard_map/cond/branch_2_fun/ppermute | solution.py:20
  15.4 0.0 collective-permute-done.12.refs_6_
  15.4 1.6 %collective-permute-start.13 = (bf16[192,256]{1,0:T(8,128)(2,1)S(1)}, bf16[192,256]{1,0:T(8,128)(2,1)S(1)}, u32[]{:S(2)}, u32[]{:S(2)}) collective-permute-start(bf16[192,256]{1,0:T(8,128)(2,1)S(1)} %collective-permute-done.12.refs_6_), channel_id=1, source_target_pairs={{0,1},{1,0},{2,3},{3,2},{4,5},{5,4},{6,7},{7,6},{8,9},{9,8},{10,11... | collective-permute-start | bytes 294920 | tf_op jit(solution)/shard_map/cond/branch_2_fun/ppermute | solution.py:20
  17.0 0.0 collective-permute-done.7.refs_1_
  17.0 0.9 %collective-permute-done.13.refs_7_ = bf16[192,256]{1,0:T(8,128)(2,1)S(1)} collective-permute-done((bf16[192,256]{1,0:T(8,128)(2,1)S(1)}, bf16[192,256]{1,0:T(8,128)(2,1)S(1)}, u32[]{:S(2)}, u32[]{:S(2)}) %collective-permute-start.13) | collective-permute-done | bytes 98336 | tf_op jit(solution)/shard_map/cond/branch_2_fun/ppermute | solution.py:20
  18.0 0.9 %attend_8.5 = bf16[128,256]{1,0:T(8,128)(2,1)S(1)} custom-call(bf16[128,256]{1,0:T(8,128)(2,1)S(1)} %copy-done.2, bf16[192,256]{1,0:T(8,128)(2,1)S(1)} %get-tuple-element.61.refs_0_, bf16[192,256]{1,0:T(8,128)(2,1)S(1)} %collective-permute-done.7.refs_1_, bf16[192,256]{1,0:T(8,128)(2,1)S(1)} %collective-permute-done.8.refs_2_, ...), custom_call_target="tpu_custom_call" | custom-call | tf_op jit(solution)/shard_map/cond/branch_2_fun/attend_8/pallas_call | solution.py:24
  18.9 0.0 copy-start.4
  18.9 0.6 %copy-done.4 = bf16[128,256]{1,0:T(8,128)(2,1)} copy-done((bf16[128,256]{1,0:T(8,128)(2,1)}, bf16[128,256]{1,0:T(8,128)(2,1)S(1)}, u32[]{:S(2)}) %copy-start.4) | copy-done | bytes 65560
  (10 shorter events, 0.0 us)
Async XLA Ops:
  0.0 3.6 %copy-start.3 = (bf16[64,256]{1,0:T(8,128)(2,1)S(1)}, bf16[64,256]{1,0:T(8,128)(2,1)}, u32[]{:S(2)}) copy-start(bf16[64,256]{1,0:T(8,128)(2,1)} %param.9) | copy-start | bytes 98308
  0.0 4.1 %collective-permute-start.19 = (bf16[64,256]{1,0:T(8,128)(2,1)}, bf16[64,256]{1,0:T(8,128)(2,1)S(1)}, u32[]{:S(2)}, u32[]{:S(2)}) collective-permute-start(bf16[64,256]{1,0:T(8,128)(2,1)} %param.9), channel_id=1, source_target_pairs={{0,16},{2,18},{4,20},{6,22},{8,24},{10,26},{12,28},{14,30},{16,0},... | collective-permute-start | bytes 98312 | tf_op jit(solution)/shard_map/ppermute | solution.py:20
  0.1 4.1 %collective-permute-start.18 = (bf16[64,256]{1,0:T(8,128)(2,1)}, bf16[64,256]{1,0:T(8,128)(2,1)S(1)}, u32[]{:S(2)}, u32[]{:S(2)}) collective-permute-start(bf16[64,256]{1,0:T(8,128)(2,1)} %param.9), channel_id=1, source_target_pairs={{0,8},{2,10},{4,12},{6,14},{8,0},{10,2},{12,4},{14,6},{16,24},{18,... | collective-permute-start | bytes 98312 | tf_op jit(solution)/shard_map/ppermute | solution.py:20
  0.2 5.4 %collective-permute-start.20 = (bf16[64,256]{1,0:T(8,128)(2,1)}, bf16[64,256]{1,0:T(8,128)(2,1)S(1)}, u32[]{:S(2)}, u32[]{:S(2)}) collective-permute-start(bf16[64,256]{1,0:T(8,128)(2,1)} %param.9), channel_id=1, source_target_pairs={{0,24},{2,26},{4,28},{6,30},{8,16},{10,18},{12,20},{14,22},{16,8},... | collective-permute-start | bytes 98312 | tf_op jit(solution)/shard_map/ppermute | solution.py:20
  3.6 2.0 %copy-start.5 = (s32[16,3]{0,1:T(4,128)S(1)}, s32[16,3]{0,1:T(4,128)}, u32[]{:S(2)}) copy-start(s32[16,3]{0,1:T(4,128)} %param.10) | copy-start | bytes 580
  5.7 12.3 %copy-start.2 = (bf16[128,256]{1,0:T(8,128)(2,1)S(1)}, bf16[128,256]{1,0:T(8,128)(2,1)}, u32[]{:S(2)}) copy-start(bf16[128,256]{1,0:T(8,128)(2,1)} %get-tuple-element.55.queries_ref) | copy-start | bytes 196612 | tf_op jit(solution)/shard_map/cond
  6.5 5.5 %collective-permute-start.8 = (bf16[192,256]{1,0:T(8,128)(2,1)S(1)}, bf16[192,256]{1,0:T(8,128)(2,1)S(1)}, u32[]{:S(2)}, u32[]{:S(2)}) collective-permute-start(bf16[192,256]{1,0:T(8,128)(2,1)S(1)} %get-tuple-element.62), channel_id=1, source_target_pairs={{0,2},{2,0},{4,6},{6,4},{8,10},{10,8},{12,14},{14,12},{16,18},{18,... | collective-permute-start | bytes 294920 | tf_op jit(solution)/shard_map/cond/branch_2_fun/ppermute | solution.py:20
  7.8 6.4 %collective-permute-start.10 = (bf16[192,256]{1,0:T(8,128)(2,1)S(1)}, bf16[192,256]{1,0:T(8,128)(2,1)S(1)}, u32[]{:S(2)}, u32[]{:S(2)}) collective-permute-start(bf16[192,256]{1,0:T(8,128)(2,1)S(1)} %get-tuple-element.63), channel_id=1, source_target_pairs={{0,4},{2,6},{4,0},{6,2},{8,12},{10,14},{12,8},{14,10},{16,20},{18,... | collective-permute-start | bytes 294920 | tf_op jit(solution)/shard_map/cond/branch_2_fun/ppermute | solution.py:20
  9.0 6.4 %collective-permute-start.12 = (bf16[192,256]{1,0:T(8,128)(2,1)S(1)}, bf16[192,256]{1,0:T(8,128)(2,1)S(1)}, u32[]{:S(2)}, u32[]{:S(2)}) collective-permute-start(bf16[192,256]{1,0:T(8,128)(2,1)S(1)} %get-tuple-element.64), channel_id=1, source_target_pairs={{0,6},{2,4},{4,2},{6,0},{8,14},{10,12},{12,10},{14,8},{16,22},{18,... | collective-permute-start | bytes 294920 | tf_op jit(solution)/shard_map/cond/branch_2_fun/ppermute | solution.py:20
  9.2 7.8 %collective-permute-start.7 = (bf16[192,256]{1,0:T(8,128)(2,1)S(1)}, bf16[192,256]{1,0:T(8,128)(2,1)S(1)}, u32[]{:S(2)}, u32[]{:S(2)}) collective-permute-start(bf16[192,256]{1,0:T(8,128)(2,1)S(1)} %get-tuple-element.61.refs_0_), channel_id=1, source_target_pairs={{0,1},{1,0},{2,3},{3,2},{4,5},{5,4},{6,7},{7,6},{8,9},{9,8},{10,11... | collective-permute-start | bytes 294920 | tf_op jit(solution)/shard_map/cond/branch_2_fun/ppermute | solution.py:20
  12.0 5.0 %collective-permute-start.9 = (bf16[192,256]{1,0:T(8,128)(2,1)S(1)}, bf16[192,256]{1,0:T(8,128)(2,1)S(1)}, u32[]{:S(2)}, u32[]{:S(2)}) collective-permute-start(bf16[192,256]{1,0:T(8,128)(2,1)S(1)} %collective-permute-done.8.refs_2_), channel_id=1, source_target_pairs={{0,1},{1,0},{2,3},{3,2},{4,5},{5,4},{6,7},{7,6},{8,9},{9,8},{10,11... | collective-permute-start | bytes 294920 | tf_op jit(solution)/shard_map/cond/branch_2_fun/ppermute | solution.py:20
  14.2 2.9 %collective-permute-start.11 = (bf16[192,256]{1,0:T(8,128)(2,1)S(1)}, bf16[192,256]{1,0:T(8,128)(2,1)S(1)}, u32[]{:S(2)}, u32[]{:S(2)}) collective-permute-start(bf16[192,256]{1,0:T(8,128)(2,1)S(1)} %collective-permute-done.10.refs_4_), channel_id=1, source_target_pairs={{0,1},{1,0},{2,3},{3,2},{4,5},{5,4},{6,7},{7,6},{8,9},{9,8},{10,11... | collective-permute-start | bytes 294920 | tf_op jit(solution)/shard_map/cond/branch_2_fun/ppermute | solution.py:20
  15.4 2.6 %collective-permute-start.13 = (bf16[192,256]{1,0:T(8,128)(2,1)S(1)}, bf16[192,256]{1,0:T(8,128)(2,1)S(1)}, u32[]{:S(2)}, u32[]{:S(2)}) collective-permute-start(bf16[192,256]{1,0:T(8,128)(2,1)S(1)} %collective-permute-done.12.refs_6_), channel_id=1, source_target_pairs={{0,1},{1,0},{2,3},{3,2},{4,5},{5,4},{6,7},{7,6},{8,9},{9,8},{10,11... | collective-permute-start | bytes 294920 | tf_op jit(solution)/shard_map/cond/branch_2_fun/ppermute | solution.py:20
  18.9 0.6 %copy-start.4 = (bf16[128,256]{1,0:T(8,128)(2,1)}, bf16[128,256]{1,0:T(8,128)(2,1)S(1)}, u32[]{:S(2)}) copy-start(bf16[128,256]{1,0:T(8,128)(2,1)S(1)} %get-tuple-element.136) | copy-start | bytes 196612

commit v4 on v3

v4 whole, which is shorter than its diff:
```python
import functools

import jax
import jax.numpy as jnp
from jax import lax
from jax.experimental import pallas as pl
from jax.experimental.pallas import tpu as pltpu
from jax.sharding import PartitionSpec as P

DH = 128
GROUP = 4
TOPK = 3
LOG2E = 1.4426950408889634
LOW = -3e38
VMEM = 16 << 20


def swapped(rows, axis, step):
    count = lax.axis_size(axis)
    return lax.ppermute(rows, axis, [(i, i ^ step) for i in range(count)])


def kernel_call(body, out_shape, name, arrays):
    vmem = pl.BlockSpec(memory_space=pltpu.VMEM)
    return pl.pallas_call(
        body,
        out_shape=out_shape,
        in_specs=[vmem] * len(arrays),
        out_specs=jax.tree.map(lambda _: vmem, out_shape),
        compiler_params=pltpu.CompilerParams(vmem_limit_bytes=VMEM),
        name=name,
    )(*arrays)


def join_kernel(*refs):
    rows = refs[0].shape[0]
    for index, piece in enumerate(refs[:-1]):
        refs[-1][index * rows : (index + 1) * rows, :] = piece[...]


def join(pieces):
    rows, width = pieces[0].shape
    out = jax.ShapeDtypeStruct((len(pieces) * rows, width), pieces[0].dtype)
    return kernel_call(join_kernel, out, "join", pieces)


def pick_kernel(columns, blocks, selected_ref, *refs):
    held, messages = refs[:blocks], refs[blocks:]
    rows = held[0].shape[0]
    me = lax.axis_index("seq")
    mine = me // GROUP
    for step in range(GROUP):
        messages[step][0:rows, :] = held[0][...]
        for column in range(1, columns):
            picked = held[1][...]
            if columns > 2:
                wanted = selected_ref[pl.ds(me ^ step, 1), column : column + 1] ^ mine
                wanted = jnp.broadcast_to(wanted, picked.shape)
                for index in range(2, blocks):
                    picked = jnp.where(wanted == index, held[index][...], picked)
            messages[step][column * rows : (column + 1) * rows, :] = picked


def pick(columns, selected, held):
    rows, width = held[0].shape
    messages = [jax.ShapeDtypeStruct((columns * rows, width), held[0].dtype)] * GROUP
    body = functools.partial(pick_kernel, columns, len(held))
    return kernel_call(body, messages, f"pick_{columns}", [selected, *held])


def attend_kernel(rows, places, resumed, last, queries_ref, *refs):
    pieces, rest = refs[: len(places)], refs[len(places) :]
    state, outs = (rest[:3], rest[3:]) if resumed else ((), rest)
    tokens, width = queries_ref.shape
    heads = width // DH
    part = lax.axis_index("seq") % GROUP
    head = lax.axis_index("head")
    queries = queries_ref[...]
    stacked = jnp.concatenate([queries[:, h * DH : (h + 1) * DH] for h in range(heads)], axis=0)
    parts = [piece[:rows, :] for piece in pieces]
    parts += [piece[rows:, :] for piece in pieces if piece.shape[0] > rows]
    kv = jnp.concatenate(parts, axis=0)
    scores = lax.dot_general(
        stacked, kv[:, :DH], (((1,), (1,)), ((), ())), preferred_element_type=jnp.float32
    ) * (DH ** (-0.5) * LOG2E)
    edge = min(-(-len(pieces) * rows // DH) * DH, kv.shape[0])
    lane = lax.broadcasted_iota(jnp.int32, (1, edge), 1)
    position = jnp.zeros_like(lane)
    for index, (step, other) in enumerate(places):
        start = (part ^ step) * tokens + (head ^ other) * rows - index * rows
        inside = (lane >= index * rows) & (lane < (index + 1) * rows)
        position = jnp.where(inside, start + lane, position)
    token = lax.broadcasted_iota(jnp.int32, (heads * tokens, 1), 0) % tokens
    own = jnp.where(position <= part * tokens + token, scores[:, :edge], LOW)
    scores = jnp.concatenate([own, scores[:, edge:]], axis=1) if edge < kv.shape[0] else own
    top = jnp.max(scores, axis=1, keepdims=True)
    if resumed:
        before = state[0][:, :1]
        top = jnp.maximum(top, before)
    weights = jnp.exp2(scores - top)
    total = jnp.sum(weights, axis=1, keepdims=True)
    out = jnp.dot(weights.astype(jnp.bfloat16), kv[:, DH:], preferred_element_type=jnp.float32)
    if resumed:
        scale = jnp.exp2(before - top)
        total += scale * state[1][:, :1]
        out += scale * state[2][...]
    if not last:
        outs[0][...] = jnp.broadcast_to(top, outs[0].shape)
        outs[1][...] = jnp.broadcast_to(total, outs[1].shape)
        outs[2][...] = out
        return
    out /= total
    for h in range(heads):
        outs[0][:, h * DH : (h + 1) * DH] = out[h * tokens : (h + 1) * tokens].astype(outs[0].dtype)


def attend(rows, queries, placed, state=(), last=True):
    tokens, width = queries.shape
    running = jax.ShapeDtypeStruct((tokens * width // DH, DH), jnp.float32)
    out = jax.ShapeDtypeStruct(queries.shape, queries.dtype) if last else [running] * 3
    places, pieces = zip(*placed)
    body = functools.partial(attend_kernel, rows, places, bool(state), last)
    return kernel_call(body, out, f"attend_{len(pieces)}", [queries, *pieces, *state])


def first_block(queries, rows):
    diagonal = swapped(rows, "seq", 3)
    beside = swapped(rows, "seq", 1)
    diagonal, again = lax.optimization_barrier((diagonal, rows))
    near = join([rows, beside, swapped(again, "seq", 2), diagonal])
    far = swapped(near, "head", 1)
    length = rows.shape[0]
    placed = []
    for other, piece in enumerate((near, far)):
        for step in range(GROUP):
            placed.append(((step, other), piece[step * length : (step + 1) * length]))
    return attend(length, queries, placed)


def later_block(columns, queries, selected, held):
    own = pick(columns, selected, held)
    near = [own[0]] + [None] * (GROUP - 1)
    for step in (3, 1, 2):
        near[step] = swapped(own[step], "seq", step)
    far = [swapped(piece, "head", 1) for piece in near]
    length = held[0].shape[0]
    placed = []
    for step in (0, 3, 1, 2):
        placed += [((step, 0), near[step]), ((step, 1), far[step])]
    state = attend(length, queries, placed[:4], last=False)
    state = attend(length, queries, placed[4:7], state, last=False)
    return attend(length, queries, placed[7:], state)


def shards(queries, keys_values, selected):
    blocks = lax.axis_size("seq") // GROUP
    mine = lax.axis_index("seq") // GROUP
    held = {0: keys_values}
    for step in range(blocks - 1, 0, -1):
        held[step] = swapped(keys_values, "seq", step * GROUP)
    held = [held[step] for step in range(blocks)]
    level = jnp.minimum(mine, TOPK - 1)
    first = lax.cond(
        level == 0,
        lambda: first_block(queries, keys_values),
        lambda: jnp.zeros_like(queries),
    )
    branches = [functools.partial(later_block, columns) for columns in range(2, TOPK + 1)]
    return lax.switch(level, [lambda *_: first] + branches, queries, selected, held)


def solution(mesh):
    in_specs = (P("seq", "head"), P(("seq", "head"), None), P())
    out_specs = P("seq", "head")
    return jax.shard_map(shards, mesh=mesh, in_specs=in_specs, out_specs=out_specs, check_vma=False)
```

time: 19.7 us -> 18.1 us (0.919)
  waiting for transfers between devices: 2.97 us -> 1.87 us
  starting transfers between devices: 14 us -> 13.3 us
  Pallas kernels: 1.73 us -> 2 us
    ppermute x10, waiting for transfers between devices: 2.97 us -> 1.87 us  [swapped(): return lax.ppermute(rows, axis, [(i, i ^ step) for i in range(count)])]
    ppermute x10, starting transfers between devices: 14 us -> 13.3 us  [swapped(): return lax.ppermute(rows, axis, [(i, i ^ step) for i in range(count)])]
    pallas_call x2 -> x4, Pallas kernels: 1.73 us -> 2 us  [kernel_call(): pl.pallas_call(body, out_shape=out_shape, in_specs=[vmem] * len(arrays),...]
  transfers between devices with their start and end apart: 10 -> 10, of which waited for: 3 -> 2; matrix products, arithmetic and copies ran while one was open for 0% -> 0% of each run, Pallas kernels for 0% -> 7%
where the time goes in v4:
time: 18.1 us; the launch traced here: 18 us
  starting transfers between devices  13.3 us (73%)
  Pallas kernels  2 us (11%)
  waiting for transfers between devices  1.87 us (10%)
  local copies, waits for them, and re-layouts  0.73 us (4%)
    ppermute x10, starting transfers between devices, swapped(): return lax.ppermute(rows, axis, [(i, i ^ step) for i in range(count)])  13.3 us
    pallas_call x4, Pallas kernels, kernel_call(): pl.pallas_call(body, out_shape=out_shape, in_specs=[vmem] * len(arrays),...  2 us
    ppermute x10, waiting for transfers between devices, swapped(): return lax.ppermute(rows, axis, [(i, i ^ step) for i in range(count)])  1.87 us
    unnamed x6, local copies, waits for them, and re-layouts  0.63 us
  transfers between devices with their start and end apart: 10, of which 2 were waited for; matrix products, arithmetic and copies ran while one was open for 0% of the time, Pallas kernels for 7%

profile of v4, /device:TPU:25, one launch (start us, length us, event | category | flops | bytes accessed | tf_op | source)
XLA Modules:
  0.0 18.0 jit_solution(15637304560098510363)
XLA Ops:
  0.0 0.2 collective-permute-start.18
  0.2 3.4 %collective-permute-start.20 = (bf16[64,256]{1,0:T(8,128)(2,1)}, bf16[64,256]{1,0:T(8,128)(2,1)S(1)}, u32[]{:S(2)}, u32[]{:S(2)}) collective-permute-start(bf16[64,256]{1,0:T(8,128)(2,1)} %param.9), channel_id=1, source_target_pairs={{0,24},{2,26},{4,28},{6,30},{8,16},{10,18},{12,20},{14,22},{16,8},... | collective-permute-start | bytes 98312 | tf_op jit(solution)/shard_map/ppermute | solution.py:20
  3.6 0.0 collective-permute-done.18
  3.6 0.5 %collective-permute-done.19 = bf16[64,256]{1,0:T(8,128)(2,1)S(1)} collective-permute-done((bf16[64,256]{1,0:T(8,128)(2,1)}, bf16[64,256]{1,0:T(8,128)(2,1)S(1)}, u32[]{:S(2)}, u32[]{:S(2)}) %collective-permute-start.19) | collective-permute-done | bytes 32800 | tf_op jit(solution)/shard_map/ppermute | solution.py:20
  4.1 1.4 %collective-permute-done.20 = bf16[64,256]{1,0:T(8,128)(2,1)S(1)} collective-permute-done((bf16[64,256]{1,0:T(8,128)(2,1)}, bf16[64,256]{1,0:T(8,128)(2,1)S(1)}, u32[]{:S(2)}, u32[]{:S(2)}) %collective-permute-start.20) | collective-permute-done | bytes 32800 | tf_op jit(solution)/shard_map/ppermute | solution.py:20
  5.4 11.9 %conditional.3 = (bf16[128,256]{1,0:T(8,128)(2,1)S(1)}) conditional(s32[]{:T(128)} %clamp.3, bf16[128,256]{1,0:T(8,128)(2,1)S(1)} %get-tuple-element.105, (s32[16,3]{0,1:T(4,128)S(1)}, bf16[64,256]{1,0:T(8,128)(2,1)S(1)}, bf16[64,256]{1,0:T(8,128)(2,1)S(1)}, bf16[64,256]{1,0:T(8,128)(2,1)S(1)}, bf16[64,256]{1,0:T(8,128)(2,1)S(1)}, ...), branch_computations={%region_2.3_spmd, %region_3.4_spmd, %region_4.5_spmd} | conditional | bytes 3015356 | solution.py:169
  5.4 0.1 copy.10.selected_ref
  5.5 0.1 pick_3.1
  5.7 2.2 %collective-permute-start.12 = (bf16[192,256]{1,0:T(8,128)(2,1)S(1)}, bf16[192,256]{1,0:T(8,128)(2,1)S(1)}, u32[]{:S(2)}, u32[]{:S(2)}) collective-permute-start(bf16[192,256]{1,0:T(8,128)(2,1)S(1)} %get-tuple-element.70), channel_id=1, source_target_pairs={{0,6},{2,4},{4,2},{6,0},{8,14},{10,12},{12,10},{14,8},{16,22},{18,... | collective-permute-start | bytes 294920 | tf_op jit(solution)/shard_map/cond/branch_2_fun/ppermute | solution.py:20
  7.9 0.3 %collective-permute-start.9 = (bf16[192,256]{1,0:T(8,128)(2,1)S(1)}, bf16[192,256]{1,0:T(8,128)(2,1)S(1)}, u32[]{:S(2)}, u32[]{:S(2)}) collective-permute-start(bf16[192,256]{1,0:T(8,128)(2,1)S(1)} %get-tuple-element.68), channel_id=1, source_target_pairs={{0,2},{2,0},{4,6},{6,4},{8,10},{10,8},{12,14},{14,12},{16,18},{18,... | collective-permute-start | bytes 294920 | tf_op jit(solution)/shard_map/cond/branch_2_fun/ppermute | solution.py:20
  8.2 0.2 %collective-permute-start.7 = (bf16[192,256]{1,0:T(8,128)(2,1)S(1)}, bf16[192,256]{1,0:T(8,128)(2,1)S(1)}, u32[]{:S(2)}, u32[]{:S(2)}) collective-permute-start(bf16[192,256]{1,0:T(8,128)(2,1)S(1)} %get-tuple-element.67), channel_id=1, source_target_pairs={{0,4},{2,6},{4,0},{6,2},{8,12},{10,14},{12,8},{14,10},{16,20},{18,... | collective-permute-start | bytes 294920 | tf_op jit(solution)/shard_map/cond/branch_2_fun/ppermute | solution.py:20
  8.4 2.9 %collective-permute-start.11 = (bf16[192,256]{1,0:T(8,128)(2,1)S(1)}, bf16[192,256]{1,0:T(8,128)(2,1)S(1)}, u32[]{:S(2)}, u32[]{:S(2)}) collective-permute-start(bf16[192,256]{1,0:T(8,128)(2,1)S(1)} %get-tuple-element.69.refs_0_), channel_id=1, source_target_pairs={{0,1},{1,0},{2,3},{3,2},{4,5},{5,4},{6,7},{7,6},{8,9},{9,8},{10,11... | collective-permute-start | bytes 294920 | tf_op jit(solution)/shard_map/cond/branch_2_fun/ppermute | solution.py:20
  11.3 0.0 collective-permute-done.12.refs_2_
  11.3 2.1 %collective-permute-start.13 = (bf16[192,256]{1,0:T(8,128)(2,1)S(1)}, bf16[192,256]{1,0:T(8,128)(2,1)S(1)}, u32[]{:S(2)}, u32[]{:S(2)}) collective-permute-start(bf16[192,256]{1,0:T(8,128)(2,1)S(1)} %collective-permute-done.12.refs_2_), channel_id=1, source_target_pairs={{0,1},{1,0},{2,3},{3,2},{4,5},{5,4},{6,7},{7,6},{8,9},{9,8},{10,11... | collective-permute-start | bytes 294920 | tf_op jit(solution)/shard_map/cond/branch_2_fun/ppermute | solution.py:20
  13.4 0.0 collective-permute-done.9.refs_0_
  13.4 1.5 %collective-permute-start.10 = (bf16[192,256]{1,0:T(8,128)(2,1)S(1)}, bf16[192,256]{1,0:T(8,128)(2,1)S(1)}, u32[]{:S(2)}, u32[]{:S(2)}) collective-permute-start(bf16[192,256]{1,0:T(8,128)(2,1)S(1)} %collective-permute-done.9.refs_0_), channel_id=1, source_target_pairs={{0,1},{1,0},{2,3},{3,2},{4,5},{5,4},{6,7},{7,6},{8,9},{9,8},{10,11... | collective-permute-start | bytes 294920 | tf_op jit(solution)/shard_map/cond/branch_2_fun/ppermute | solution.py:20
  14.9 0.0 collective-permute-done.7.refs_2_
  14.9 0.5 %collective-permute-start.8 = (bf16[192,256]{1,0:T(8,128)(2,1)S(1)}, bf16[192,256]{1,0:T(8,128)(2,1)S(1)}, u32[]{:S(2)}, u32[]{:S(2)}) collective-permute-start(bf16[192,256]{1,0:T(8,128)(2,1)S(1)} %collective-permute-done.7.refs_2_), channel_id=1, source_target_pairs={{0,1},{1,0},{2,3},{3,2},{4,5},{5,4},{6,7},{7,6},{8,9},{9,8},{10,11... | collective-permute-start | bytes 294920 | tf_op jit(solution)/shard_map/cond/branch_2_fun/ppermute | solution.py:20
  15.4 0.0 collective-permute-done.13.refs_3_
  15.4 0.6 %attend_4.3 = (f32[256,128]{1,0:T(8,128)S(1)}, f32[256,128]{1,0:T(8,128)S(1)}, f32[256,128]{1,0:T(8,128)S(1)}) custom-call(bf16[128,256]{1,0:T(8,128)(2,1)S(1)} %copy-done.2, bf16[192,256]{1,0:T(8,128)(2,1)S(1)} %get-tuple-element.69.refs_0_, bf16[192,256]{1,0:T(8,128)(2,1)S(1)} %collective-permute-done.11.refs_1_, ...), custom_call_target="tpu_custom_call" | custom-call | tf_op jit(solution)/shard_map/cond/branch_2_fun/attend_4/pallas_call | solution.py:25
  16.1 0.7 %attend_3.3 = (f32[256,128]{1,0:T(8,128)S(1)}, f32[256,128]{1,0:T(8,128)S(1)}, f32[256,128]{1,0:T(8,128)S(1)}) custom-call(bf16[128,256]{1,0:T(8,128)(2,1)S(1)} %copy-done.2, bf16[192,256]{1,0:T(8,128)(2,1)S(1)} %collective-permute-done.9.refs_0_, bf16[192,256]{1,0:T(8,128)(2,1)S(1)} %collective-permute-done.10.refs_1_, ...), custom_call_target="tpu_custom_call" | custom-call | tf_op jit(solution)/shard_map/cond/branch_2_fun/attend_3/pallas_call | solution.py:25
  16.8 0.5 %attend_1.3 = bf16[128,256]{1,0:T(8,128)(2,1)S(1)} custom-call(bf16[128,256]{1,0:T(8,128)(2,1)S(1)} %copy-done.2, bf16[192,256]{1,0:T(8,128)(2,1)S(1)} %collective-permute-done.8.refs_0_, f32[256,128]{1,0:T(8,128)S(1)} %get-tuple-element.74.refs_1_, f32[256,128]{1,0:T(8,128)S(1)} %get-tuple-element.75.refs_2_, f32[256,128]{1,0:T(8,128)S(1)} %get-tuple-element.76.refs_3_), custom_call_target="tpu_custom_call" | custom-call | tf_op jit(solution)/shard_map/cond/branch_2_fun/attend_1/pallas_call | solution.py:25
  17.3 0.0 copy-start.4
  17.3 0.6 %copy-done.4 = bf16[128,256]{1,0:T(8,128)(2,1)} copy-done((bf16[128,256]{1,0:T(8,128)(2,1)}, bf16[128,256]{1,0:T(8,128)(2,1)S(1)}, u32[]{:S(2)}) %copy-start.4) | copy-done | bytes 65560
  (12 shorter events, 0.0 us)
Async XLA Ops:
  0.0 3.6 %copy-start.3 = (bf16[64,256]{1,0:T(8,128)(2,1)S(1)}, bf16[64,256]{1,0:T(8,128)(2,1)}, u32[]{:S(2)}) copy-start(bf16[64,256]{1,0:T(8,128)(2,1)} %param.9) | copy-start | bytes 98308
  0.0 3.6 %collective-permute-start.18 = (bf16[64,256]{1,0:T(8,128)(2,1)}, bf16[64,256]{1,0:T(8,128)(2,1)S(1)}, u32[]{:S(2)}, u32[]{:S(2)}) collective-permute-start(bf16[64,256]{1,0:T(8,128)(2,1)} %param.9), channel_id=1, source_target_pairs={{0,8},{2,10},{4,12},{6,14},{8,0},{10,2},{12,4},{14,6},{16,24},{18,... | collective-permute-start | bytes 98312 | tf_op jit(solution)/shard_map/ppermute | solution.py:20
  0.2 3.9 %collective-permute-start.19 = (bf16[64,256]{1,0:T(8,128)(2,1)}, bf16[64,256]{1,0:T(8,128)(2,1)S(1)}, u32[]{:S(2)}, u32[]{:S(2)}) collective-permute-start(bf16[64,256]{1,0:T(8,128)(2,1)} %param.9), channel_id=1, source_target_pairs={{0,16},{2,18},{4,20},{6,22},{8,24},{10,26},{12,28},{14,30},{16,0},... | collective-permute-start | bytes 98312 | tf_op jit(solution)/shard_map/ppermute | solution.py:20
  0.2 5.3 %collective-permute-start.20 = (bf16[64,256]{1,0:T(8,128)(2,1)}, bf16[64,256]{1,0:T(8,128)(2,1)S(1)}, u32[]{:S(2)}, u32[]{:S(2)}) collective-permute-start(bf16[64,256]{1,0:T(8,128)(2,1)} %param.9), channel_id=1, source_target_pairs={{0,24},{2,26},{4,28},{6,30},{8,16},{10,18},{12,20},{14,22},{16,8},... | collective-permute-start | bytes 98312 | tf_op jit(solution)/shard_map/ppermute | solution.py:20
  3.6 1.9 %copy-start.5 = (s32[16,3]{0,1:T(4,128)S(1)}, s32[16,3]{0,1:T(4,128)}, u32[]{:S(2)}) copy-start(s32[16,3]{0,1:T(4,128)} %param.10) | copy-start | bytes 580
  5.5 9.9 %copy-start.2 = (bf16[128,256]{1,0:T(8,128)(2,1)S(1)}, bf16[128,256]{1,0:T(8,128)(2,1)}, u32[]{:S(2)}) copy-start(bf16[128,256]{1,0:T(8,128)(2,1)} %get-tuple-element.61.queries_ref) | copy-start | bytes 196612 | tf_op jit(solution)/shard_map/cond
  5.7 5.6 %collective-permute-start.12 = (bf16[192,256]{1,0:T(8,128)(2,1)S(1)}, bf16[192,256]{1,0:T(8,128)(2,1)S(1)}, u32[]{:S(2)}, u32[]{:S(2)}) collective-permute-start(bf16[192,256]{1,0:T(8,128)(2,1)S(1)} %get-tuple-element.70), channel_id=1, source_target_pairs={{0,6},{2,4},{4,2},{6,0},{8,14},{10,12},{12,10},{14,8},{16,22},{18,... | collective-permute-start | bytes 294920 | tf_op jit(solution)/shard_map/cond/branch_2_fun/ppermute | solution.py:20
  7.9 5.5 %collective-permute-start.9 = (bf16[192,256]{1,0:T(8,128)(2,1)S(1)}, bf16[192,256]{1,0:T(8,128)(2,1)S(1)}, u32[]{:S(2)}, u32[]{:S(2)}) collective-permute-start(bf16[192,256]{1,0:T(8,128)(2,1)S(1)} %get-tuple-element.68), channel_id=1, source_target_pairs={{0,2},{2,0},{4,6},{6,4},{8,10},{10,8},{12,14},{14,12},{16,18},{18,... | collective-permute-start | bytes 294920 | tf_op jit(solution)/shard_map/cond/branch_2_fun/ppermute | solution.py:20
  8.2 6.7 %collective-permute-start.7 = (bf16[192,256]{1,0:T(8,128)(2,1)S(1)}, bf16[192,256]{1,0:T(8,128)(2,1)S(1)}, u32[]{:S(2)}, u32[]{:S(2)}) collective-permute-start(bf16[192,256]{1,0:T(8,128)(2,1)S(1)} %get-tuple-element.67), channel_id=1, source_target_pairs={{0,4},{2,6},{4,0},{6,2},{8,12},{10,14},{12,8},{14,10},{16,20},{18,... | collective-permute-start | bytes 294920 | tf_op jit(solution)/shard_map/cond/branch_2_fun/ppermute | solution.py:20
  8.4 7.0 %collective-permute-start.11 = (bf16[192,256]{1,0:T(8,128)(2,1)S(1)}, bf16[192,256]{1,0:T(8,128)(2,1)S(1)}, u32[]{:S(2)}, u32[]{:S(2)}) collective-permute-start(bf16[192,256]{1,0:T(8,128)(2,1)S(1)} %get-tuple-element.69.refs_0_), channel_id=1, source_target_pairs={{0,1},{1,0},{2,3},{3,2},{4,5},{5,4},{6,7},{7,6},{8,9},{9,8},{10,11... | collective-permute-start | bytes 294920 | tf_op jit(solution)/shard_map/cond/branch_2_fun/ppermute | solution.py:20
  11.3 4.1 %collective-permute-start.13 = (bf16[192,256]{1,0:T(8,128)(2,1)S(1)}, bf16[192,256]{1,0:T(8,128)(2,1)S(1)}, u32[]{:S(2)}, u32[]{:S(2)}) collective-permute-start(bf16[192,256]{1,0:T(8,128)(2,1)S(1)} %collective-permute-done.12.refs_2_), channel_id=1, source_target_pairs={{0,1},{1,0},{2,3},{3,2},{4,5},{5,4},{6,7},{7,6},{8,9},{9,8},{10,11... | collective-permute-start | bytes 294920 | tf_op jit(solution)/shard_map/cond/branch_2_fun/ppermute | solution.py:20
  13.4 2.7 %collective-permute-start.10 = (bf16[192,256]{1,0:T(8,128)(2,1)S(1)}, bf16[192,256]{1,0:T(8,128)(2,1)S(1)}, u32[]{:S(2)}, u32[]{:S(2)}) collective-permute-start(bf16[192,256]{1,0:T(8,128)(2,1)S(1)} %collective-permute-done.9.refs_0_), channel_id=1, source_target_pairs={{0,1},{1,0},{2,3},{3,2},{4,5},{5,4},{6,7},{7,6},{8,9},{9,8},{10,11... | collective-permute-start | bytes 294920 | tf_op jit(solution)/shard_map/cond/branch_2_fun/ppermute | solution.py:20
  14.9 1.9 %collective-permute-start.8 = (bf16[192,256]{1,0:T(8,128)(2,1)S(1)}, bf16[192,256]{1,0:T(8,128)(2,1)S(1)}, u32[]{:S(2)}, u32[]{:S(2)}) collective-permute-start(bf16[192,256]{1,0:T(8,128)(2,1)S(1)} %collective-permute-done.7.refs_2_), channel_id=1, source_target_pairs={{0,1},{1,0},{2,3},{3,2},{4,5},{5,4},{6,7},{7,6},{8,9},{9,8},{10,11... | collective-permute-start | bytes 294920 | tf_op jit(solution)/shard_map/cond/branch_2_fun/ppermute | solution.py:20
  17.3 0.6 %copy-start.4 = (bf16[128,256]{1,0:T(8,128)(2,1)}, bf16[128,256]{1,0:T(8,128)(2,1)S(1)}, u32[]{:S(2)}) copy-start(bf16[128,256]{1,0:T(8,128)(2,1)S(1)} %get-tuple-element.148) | copy-start | bytes 196612

commit v5 on v4

--- a/solution.py
+++ b/solution.py
@@ -13,11 +13,46 @@
 LOG2E = 1.4426950408889634
 LOW = -3e38
 VMEM = 16 << 20
-
-
-def swapped(rows, axis, step):
-    count = lax.axis_size(axis)
-    return lax.ppermute(rows, axis, [(i, i ^ step) for i in range(count)])
+LF, CF, ZF = 1, 0, ((1, 1), (0, 1), (1, 1))
+
+
+def own(part, head):
+    return 0, 0
+
+
+def across(part, head):
+    return 3, CF
+
+
+def lane(part, head):
+    return head ^ (((part ^ (part >> 1)) & 1) if LF else 0)
+
+
+def beside(part, head):
+    return 1 + lane(part, head), LF
+
+
+def other_beside(part, head):
+    return 2 - lane(part, head), LF
+
+
+def swapped(rows, route):
+    seq, head = lax.axis_size("seq"), lax.axis_size("head")
+    routes = []
+    for i in range(seq):
+        for h in range(head):
+            step, flip = route(i, h)
+            routes.append((i * head + h, (i ^ step) * head + (h ^ flip)))
+    return lax.ppermute(rows, ("seq", "head"), routes)
+
+
+def earlier_block(step, place, head):
+    lower = min(place, place ^ step * GROUP) // GROUP
+    return step * GROUP, ZF[min(step, 3) - 1][lower & 1]
+
+
+def other_core(part, head):
+    return 0, 1
 
 
 def kernel_call(body, out_shape, name, arrays):
@@ -49,16 +84,17 @@
     rows = held[0].shape[0]
     me = lax.axis_index("seq")
     mine = me // GROUP
-    for step in range(GROUP):
-        messages[step][0:rows, :] = held[0][...]
+    for index, route in enumerate((own, across, beside, other_beside)):
+        step, _ = route(me % GROUP, lax.axis_index("head"))
+        messages[index][0:rows, :] = held[0][...]
         for column in range(1, columns):
             picked = held[1][...]
             if columns > 2:
                 wanted = selected_ref[pl.ds(me ^ step, 1), column : column + 1] ^ mine
                 wanted = jnp.broadcast_to(wanted, picked.shape)
-                for index in range(2, blocks):
-                    picked = jnp.where(wanted == index, held[index][...], picked)
-            messages[step][column * rows : (column + 1) * rows, :] = picked
+                for other in range(2, blocks):
+                    picked = jnp.where(wanted == other, held[other][...], picked)
+            messages[index][column * rows : (column + 1) * rows, :] = picked
 
 
 def pick(columns, selected, held):
@@ -86,27 +122,30 @@
     edge = min(-(-len(pieces) * rows // DH) * DH, kv.shape[0])
     lane = lax.broadcasted_iota(jnp.int32, (1, edge), 1)
     position = jnp.zeros_like(lane)
-    for index, (step, other) in enumerate(places):
-        start = (part ^ step) * tokens + (head ^ other) * rows - index * rows
+    for index, (route, relayed) in enumerate(places):
+        step, flip = route(part, head ^ relayed)
+        start = (part ^ step) * tokens + (head ^ relayed ^ flip) * rows - index * rows
         inside = (lane >= index * rows) & (lane < (index + 1) * rows)
         position = jnp.where(inside, start + lane, position)
     token = lax.broadcasted_iota(jnp.int32, (heads * tokens, 1), 0) % tokens
     own = jnp.where(position <= part * tokens + token, scores[:, :edge], LOW)
     scores = jnp.concatenate([own, scores[:, edge:]], axis=1) if edge < kv.shape[0] else own
-    top = jnp.max(scores, axis=1, keepdims=True)
+    top = jnp.broadcast_to(jnp.max(scores, axis=1, keepdims=True), (heads * tokens, DH))
     if resumed:
-        before = state[0][:, :1]
+        before = state[0][...]
         top = jnp.maximum(top, before)
-    weights = jnp.exp2(scores - top)
-    total = jnp.sum(weights, axis=1, keepdims=True)
-    out = jnp.dot(weights.astype(jnp.bfloat16), kv[:, DH:], preferred_element_type=jnp.float32)
+    columns = [scores[:, start : start + DH] for start in range(0, scores.shape[1], DH)]
+    weights = jnp.concatenate([jnp.exp2(c - top[:, : c.shape[1]]).astype(jnp.bfloat16) for c in columns], axis=1)
+    values = jnp.concatenate([kv[:, DH:], jnp.ones_like(kv[:, DH:])], axis=1)
+    sums = jnp.dot(weights, values, preferred_element_type=jnp.float32)
+    out, total = sums[:, :DH], sums[:, DH:]
     if resumed:
         scale = jnp.exp2(before - top)
-        total += scale * state[1][:, :1]
+        total += scale * state[1][...]
         out += scale * state[2][...]
     if not last:
-        outs[0][...] = jnp.broadcast_to(top, outs[0].shape)
-        outs[1][...] = jnp.broadcast_to(total, outs[1].shape)
+        outs[0][...] = top
+        outs[1][...] = total
         outs[2][...] = out
         return
     out /= total
@@ -124,32 +163,28 @@
 
 
 def first_block(queries, rows):
-    diagonal = swapped(rows, "seq", 3)
-    beside = swapped(rows, "seq", 1)
+    diagonal = swapped(rows, across)
+    first = swapped(rows, beside)
     diagonal, again = lax.optimization_barrier((diagonal, rows))
-    near = join([rows, beside, swapped(again, "seq", 2), diagonal])
-    far = swapped(near, "head", 1)
+    near = join([rows, first, swapped(again, other_beside), diagonal])
+    far = swapped(near, other_core)
     length = rows.shape[0]
     placed = []
-    for other, piece in enumerate((near, far)):
-        for step in range(GROUP):
-            placed.append(((step, other), piece[step * length : (step + 1) * length]))
+    for relayed, piece in enumerate((near, far)):
+        for index, route in enumerate((own, beside, other_beside, across)):
+            placed.append(((route, relayed), piece[index * length : (index + 1) * length]))
     return attend(length, queries, placed)
 
 
 def later_block(columns, queries, selected, held):
-    own = pick(columns, selected, held)
-    near = [own[0]] + [None] * (GROUP - 1)
-    for step in (3, 1, 2):
-        near[step] = swapped(own[step], "seq", step)
-    far = [swapped(piece, "head", 1) for piece in near]
     length = held[0].shape[0]
-    placed = []
-    for step in (0, 3, 1, 2):
-        placed += [((step, 0), near[step]), ((step, 1), far[step])]
-    state = attend(length, queries, placed[:4], last=False)
-    state = attend(length, queries, placed[4:7], state, last=False)
-    return attend(length, queries, placed[7:], state)
+    messages = pick(columns, selected, held)
+    near = [messages[0]] + [swapped(m, route) for m, route in zip(messages[1:], (across, beside, other_beside))]
+    far = [swapped(piece, other_core) for piece in near]
+    placed = [((own, 0), near[0]), ((own, 1), far[0]), ((across, 0), near[1]), ((across, 1), far[1]), ((beside, 0), near[2]), ((other_beside, 0), near[3])]
+    state = attend(length, queries, placed, last=False)
+    placed = [((beside, 1), far[2]), ((other_beside, 1), far[3])]
+    return attend(length, queries, placed, state)
 
 
 def shards(queries, keys_values, selected):
@@ -157,8 +192,10 @@
     mine = lax.axis_index("seq") // GROUP
     held = {0: keys_values}
     for step in range(blocks - 1, 0, -1):
-        held[step] = swapped(keys_values, "seq", step * GROUP)
+        held[step] = swapped(keys_values, functools.partial(earlier_block, step))
     held = [held[step] for step in range(blocks)]
+    held[2], held[1] = lax.optimization_barrier((held[2], held[1]))
+    held[3], held[2] = lax.optimization_barrier((held[3], held[2]))
     level = jnp.minimum(mine, TOPK - 1)
     first = lax.cond(
         level == 0,

time: 18.1 us -> 17.5 us (0.967)
  the two profiles are of different devices: /device:TPU:25 before, /device:TPU:21 now
where the time goes in v5:
time: 17.5 us; the launch traced here: 17.4 us
  starting transfers between devices  8.68 us (50%)
  waiting for transfers between devices  6.28 us (36%)
  Pallas kernels  1.64 us (9%)
  local copies, waits for them, and re-layouts  0.73 us (4%)
    ppermute x10, starting transfers between devices, swapped(): return lax.ppermute(rows, ('seq', 'head'), routes)  8.68 us
    ppermute x10, waiting for transfers between devices, swapped(): return lax.ppermute(rows, ('seq', 'head'), routes)  6.28 us
    pallas_call x3, Pallas kernels, kernel_call(): pl.pallas_call(body, out_shape=out_shape, in_specs=[vmem] * len(arrays),...  1.64 us
    unnamed x6, local copies, waits for them, and re-layouts  0.63 us
  transfers between devices with their start and end apart: 10, of which 5 were waited for; matrix products, arithmetic and copies ran while one was open for 0% of the time, Pallas kernels for 6%

profile of v5, /device:TPU:21, one launch (start us, length us, event | category | flops | bytes accessed | tf_op | source)
XLA Modules:
  0.0 17.4 jit_solution(9385978367612763904)
XLA Ops:
  0.0 0.1 collective-permute-start.18
  0.1 1.9 %collective-permute-start.19 = (bf16[64,256]{1,0:T(8,128)(2,1)}, bf16[64,256]{1,0:T(8,128)(2,1)S(1)}, u32[]{:S(2)}, u32[]{:S(2)}) collective-permute-start(bf16[64,256]{1,0:T(8,128)(2,1)} %param.9), channel_id=1, source_target_pairs={{0,9},{1,8},{2,11},{3,10},{4,13},{5,12},{6,15},{7,14},{8,1},{9,0},... | collective-permute-start | bytes 98312 | tf_op jit(solution)/shard_map/ppermute | solution.py:46
  1.9 1.0 %collective-permute-start.20 = (bf16[64,256]{1,0:T(8,128)(2,1)}, bf16[64,256]{1,0:T(8,128)(2,1)S(1)}, u32[]{:S(2)}, u32[]{:S(2)}) collective-permute-start(bf16[64,256]{1,0:T(8,128)(2,1)} %param.9), channel_id=1, source_target_pairs={{0,25},{1,24},{2,27},{3,26},{4,29},{5,28},{6,31},{7,30},{8,17},{9,... | collective-permute-start | bytes 98312 | tf_op jit(solution)/shard_map/ppermute | solution.py:46
  3.0 0.9 %collective-permute-done.18 = bf16[64,256]{1,0:T(8,128)(2,1)S(1)} collective-permute-done((bf16[64,256]{1,0:T(8,128)(2,1)}, bf16[64,256]{1,0:T(8,128)(2,1)S(1)}, u32[]{:S(2)}, u32[]{:S(2)}) %collective-permute-start.18) | collective-permute-done | bytes 32800 | tf_op jit(solution)/shard_map/ppermute | solution.py:46
  3.9 0.6 %collective-permute-done.19 = bf16[64,256]{1,0:T(8,128)(2,1)S(1)} collective-permute-done((bf16[64,256]{1,0:T(8,128)(2,1)}, bf16[64,256]{1,0:T(8,128)(2,1)S(1)}, u32[]{:S(2)}, u32[]{:S(2)}) %collective-permute-start.19) | collective-permute-done | bytes 32800 | tf_op jit(solution)/shard_map/ppermute | solution.py:46
  4.5 2.1 %collective-permute-done.20 = bf16[64,256]{1,0:T(8,128)(2,1)S(1)} collective-permute-done((bf16[64,256]{1,0:T(8,128)(2,1)}, bf16[64,256]{1,0:T(8,128)(2,1)S(1)}, u32[]{:S(2)}, u32[]{:S(2)}) %collective-permute-start.20) | collective-permute-done | bytes 32800 | tf_op jit(solution)/shard_map/ppermute | solution.py:46
  6.6 10.2 %conditional.3 = (bf16[128,256]{1,0:T(8,128)(2,1)S(1)}) conditional(s32[]{:T(128)} %clamp.3, bf16[128,256]{1,0:T(8,128)(2,1)S(1)} %get-tuple-element.107, (s32[16,3]{0,1:T(4,128)S(1)}, bf16[64,256]{1,0:T(8,128)(2,1)S(1)}, bf16[64,256]{1,0:T(8,128)(2,1)S(1)}, bf16[64,256]{1,0:T(8,128)(2,1)S(1)}, bf16[64,256]{1,0:T(8,128)(2,1)S(1)}, ...), branch_computations={%region_2.3_spmd, %region_3.4_spmd, %region_4.5_spmd} | conditional | bytes 3015356 | solution.py:206
  6.6 0.1 copy.10.selected_ref
  6.7 0.1 pick_3.1
  6.8 1.2 %collective-permute-start.12 = (bf16[192,256]{1,0:T(8,128)(2,1)S(1)}, bf16[192,256]{1,0:T(8,128)(2,1)S(1)}, u32[]{:S(2)}, u32[]{:S(2)}) collective-permute-start(bf16[192,256]{1,0:T(8,128)(2,1)S(1)} %get-tuple-element.67), channel_id=1, source_target_pairs={{0,6},{1,7},{2,4},{3,5},{4,2},{5,3},{6,0},{7,1},{8,14},{9,15},{10,... | collective-permute-start | bytes 294920 | tf_op jit(solution)/shard_map/cond/branch_2_fun/ppermute | solution.py:46
  8.0 1.8 %collective-permute-start.9 = (bf16[192,256]{1,0:T(8,128)(2,1)S(1)}, bf16[192,256]{1,0:T(8,128)(2,1)S(1)}, u32[]{:S(2)}, u32[]{:S(2)}) collective-permute-start(bf16[192,256]{1,0:T(8,128)(2,1)S(1)} %get-tuple-element.65), channel_id=1, source_target_pairs={{0,5},{1,2},{2,1},{3,6},{4,7},{5,0},{6,3},{7,4},{8,13},{9,10},{10,... | collective-permute-start | bytes 294920 | tf_op jit(solution)/shard_map/cond/branch_2_fun/ppermute | solution.py:46
  9.8 0.0 collective-permute-start.7
  9.8 0.6 %collective-permute-start.11 = (bf16[192,256]{1,0:T(8,128)(2,1)S(1)}, bf16[192,256]{1,0:T(8,128)(2,1)S(1)}, u32[]{:S(2)}, u32[]{:S(2)}) collective-permute-start(bf16[192,256]{1,0:T(8,128)(2,1)S(1)} %get-tuple-element.66.refs_0_), channel_id=1, source_target_pairs={{0,1},{1,0},{2,3},{3,2},{4,5},{5,4},{6,7},{7,6},{8,9},{9,8},{10,11... | collective-permute-start | bytes 294920 | tf_op jit(solution)/shard_map/cond/branch_2_fun/ppermute | solution.py:46
  10.5 1.3 %collective-permute-done.12.refs_2_ = bf16[192,256]{1,0:T(8,128)(2,1)S(1)} collective-permute-done((bf16[192,256]{1,0:T(8,128)(2,1)S(1)}, bf16[192,256]{1,0:T(8,128)(2,1)S(1)}, u32[]{:S(2)}, u32[]{:S(2)}) %collective-permute-start.12) | collective-permute-done | bytes 98336 | tf_op jit(solution)/shard_map/cond/branch_2_fun/ppermute | solution.py:46
  11.8 1.6 %collective-permute-start.13 = (bf16[192,256]{1,0:T(8,128)(2,1)S(1)}, bf16[192,256]{1,0:T(8,128)(2,1)S(1)}, u32[]{:S(2)}, u32[]{:S(2)}) collective-permute-start(bf16[192,256]{1,0:T(8,128)(2,1)S(1)} %collective-permute-done.12.refs_2_), channel_id=1, source_target_pairs={{0,1},{1,0},{2,3},{3,2},{4,5},{5,4},{6,7},{7,6},{8,9},{9,8},{10,11... | collective-permute-start | bytes 294920 | tf_op jit(solution)/shard_map/cond/branch_2_fun/ppermute | solution.py:46
  13.3 1.4 %collective-permute-done.9.refs_5_ = bf16[192,256]{1,0:T(8,128)(2,1)S(1)} collective-permute-done((bf16[192,256]{1,0:T(8,128)(2,1)S(1)}, bf16[192,256]{1,0:T(8,128)(2,1)S(1)}, u32[]{:S(2)}, u32[]{:S(2)}) %collective-permute-start.9) | collective-permute-done | bytes 98336 | tf_op jit(solution)/shard_map/cond/branch_2_fun/ppermute | solution.py:46
  14.7 0.0 collective-permute-start.10
  14.7 0.5 %collective-permute-start.8 = (bf16[192,256]{1,0:T(8,128)(2,1)S(1)}, bf16[192,256]{1,0:T(8,128)(2,1)S(1)}, u32[]{:S(2)}, u32[]{:S(2)}) collective-permute-start(bf16[192,256]{1,0:T(8,128)(2,1)S(1)} %collective-permute-done.7.refs_4_), channel_id=1, source_target_pairs={{0,1},{1,0},{2,3},{3,2},{4,5},{5,4},{6,7},{7,6},{8,9},{9,8},{10,11... | collective-permute-start | bytes 294920 | tf_op jit(solution)/shard_map/cond/branch_2_fun/ppermute | solution.py:46
  15.2 1.0 %attend_6.3 = (f32[256,128]{1,0:T(8,128)S(1)}, f32[256,128]{1,0:T(8,128)S(1)}, f32[256,128]{1,0:T(8,128)S(1)}) custom-call(bf16[128,256]{1,0:T(8,128)(2,1)S(1)} %copy-done.2, bf16[192,256]{1,0:T(8,128)(2,1)S(1)} %get-tuple-element.66.refs_0_, bf16[192,256]{1,0:T(8,128)(2,1)S(1)} %collective-permute-done.11.refs_1_, ...), custom_call_target="tpu_custom_call" | custom-call | tf_op jit(solution)/shard_map/cond/branch_2_fun/attend_6/pallas_call | solution.py:60
  16.2 0.0 collective-permute-done.10.refs_1_
  16.2 0.0 collective-permute-done.8.refs_0_
  16.2 0.5 %attend_2.3 = bf16[128,256]{1,0:T(8,128)(2,1)S(1)} custom-call(bf16[128,256]{1,0:T(8,128)(2,1)S(1)} %copy-done.2, bf16[192,256]{1,0:T(8,128)(2,1)S(1)} %collective-permute-done.8.refs_0_, bf16[192,256]{1,0:T(8,128)(2,1)S(1)} %collective-permute-done.10.refs_1_, f32[256,128]{1,0:T(8,128)S(1)} %get-tuple-element.68.refs_2_, ...), custom_call_target="tpu_custom_call" | custom-call | tf_op jit(solution)/shard_map/cond/branch_2_fun/attend_2/pallas_call | solution.py:60
  16.8 0.0 copy-start.4
  16.8 0.6 %copy-done.4 = bf16[128,256]{1,0:T(8,128)(2,1)} copy-done((bf16[128,256]{1,0:T(8,128)(2,1)}, bf16[128,256]{1,0:T(8,128)(2,1)S(1)}, u32[]{:S(2)}) %copy-start.4) | copy-done | bytes 65560
  (11 shorter events, 0.0 us)
Async XLA Ops:
  0.0 2.9 %copy-start.3 = (bf16[64,256]{1,0:T(8,128)(2,1)S(1)}, bf16[64,256]{1,0:T(8,128)(2,1)}, u32[]{:S(2)}) copy-start(bf16[64,256]{1,0:T(8,128)(2,1)} %param.9) | copy-start | bytes 98308
  0.0 3.9 %collective-permute-start.18 = (bf16[64,256]{1,0:T(8,128)(2,1)}, bf16[64,256]{1,0:T(8,128)(2,1)S(1)}, u32[]{:S(2)}, u32[]{:S(2)}) collective-permute-start(bf16[64,256]{1,0:T(8,128)(2,1)} %param.9), channel_id=1, source_target_pairs={{0,16},{1,17},{2,18},{3,19},{4,20},{5,21},{6,22},{7,23},{8,25},{9,... | collective-permute-start | bytes 98312 | tf_op jit(solution)/shard_map/ppermute | solution.py:46
  0.1 4.5 %collective-permute-start.19 = (bf16[64,256]{1,0:T(8,128)(2,1)}, bf16[64,256]{1,0:T(8,128)(2,1)S(1)}, u32[]{:S(2)}, u32[]{:S(2)}) collective-permute-start(bf16[64,256]{1,0:T(8,128)(2,1)} %param.9), channel_id=1, source_target_pairs={{0,9},{1,8},{2,11},{3,10},{4,13},{5,12},{6,15},{7,14},{8,1},{9,0},... | collective-permute-start | bytes 98312 | tf_op jit(solution)/shard_map/ppermute | solution.py:46
  1.9 4.6 %collective-permute-start.20 = (bf16[64,256]{1,0:T(8,128)(2,1)}, bf16[64,256]{1,0:T(8,128)(2,1)S(1)}, u32[]{:S(2)}, u32[]{:S(2)}) collective-permute-start(bf16[64,256]{1,0:T(8,128)(2,1)} %param.9), channel_id=1, source_target_pairs={{0,25},{1,24},{2,27},{3,26},{4,29},{5,28},{6,31},{7,30},{8,17},{9,... | collective-permute-start | bytes 98312 | tf_op jit(solution)/shard_map/ppermute | solution.py:46
  2.9 3.7 %copy-start.5 = (s32[16,3]{0,1:T(4,128)S(1)}, s32[16,3]{0,1:T(4,128)}, u32[]{:S(2)}) copy-start(s32[16,3]{0,1:T(4,128)} %param.10) | copy-start | bytes 580
  6.7 8.6 %copy-start.2 = (bf16[128,256]{1,0:T(8,128)(2,1)S(1)}, bf16[128,256]{1,0:T(8,128)(2,1)}, u32[]{:S(2)}) copy-start(bf16[128,256]{1,0:T(8,128)(2,1)} %get-tuple-element.58.queries_ref) | copy-start | bytes 196612 | tf_op jit(solution)/shard_map/cond
  6.8 4.9 %collective-permute-start.12 = (bf16[192,256]{1,0:T(8,128)(2,1)S(1)}, bf16[192,256]{1,0:T(8,128)(2,1)S(1)}, u32[]{:S(2)}, u32[]{:S(2)}) collective-permute-start(bf16[192,256]{1,0:T(8,128)(2,1)S(1)} %get-tuple-element.67), channel_id=1, source_target_pairs={{0,6},{1,7},{2,4},{3,5},{4,2},{5,3},{6,0},{7,1},{8,14},{9,15},{10,... | collective-permute-start | bytes 294920 | tf_op jit(solution)/shard_map/cond/branch_2_fun/ppermute | solution.py:46
  8.0 6.7 %collective-permute-start.9 = (bf16[192,256]{1,0:T(8,128)(2,1)S(1)}, bf16[192,256]{1,0:T(8,128)(2,1)S(1)}, u32[]{:S(2)}, u32[]{:S(2)}) collective-permute-start(bf16[192,256]{1,0:T(8,128)(2,1)S(1)} %get-tuple-element.65), channel_id=1, source_target_pairs={{0,5},{1,2},{2,1},{3,6},{4,7},{5,0},{6,3},{7,4},{8,13},{9,10},{10,... | collective-permute-start | bytes 294920 | tf_op jit(solution)/shard_map/cond/branch_2_fun/ppermute | solution.py:46
  9.8 4.9 %collective-permute-start.7 = (bf16[192,256]{1,0:T(8,128)(2,1)S(1)}, bf16[192,256]{1,0:T(8,128)(2,1)S(1)}, u32[]{:S(2)}, u32[]{:S(2)}) collective-permute-start(bf16[192,256]{1,0:T(8,128)(2,1)S(1)} %get-tuple-element.64), channel_id=1, source_target_pairs={{0,3},{1,4},{2,7},{3,0},{4,1},{5,6},{6,5},{7,2},{8,11},{9,12},{10,... | collective-permute-start | bytes 294920 | tf_op jit(solution)/shard_map/cond/branch_2_fun/ppermute | solution.py:46
  9.8 5.4 %collective-permute-start.11 = (bf16[192,256]{1,0:T(8,128)(2,1)S(1)}, bf16[192,256]{1,0:T(8,128)(2,1)S(1)}, u32[]{:S(2)}, u32[]{:S(2)}) collective-permute-start(bf16[192,256]{1,0:T(8,128)(2,1)S(1)} %get-tuple-element.66.refs_0_), channel_id=1, source_target_pairs={{0,1},{1,0},{2,3},{3,2},{4,5},{5,4},{6,7},{7,6},{8,9},{9,8},{10,11... | collective-permute-start | bytes 294920 | tf_op jit(solution)/shard_map/cond/branch_2_fun/ppermute | solution.py:46
  11.8 3.5 %collective-permute-start.13 = (bf16[192,256]{1,0:T(8,128)(2,1)S(1)}, bf16[192,256]{1,0:T(8,128)(2,1)S(1)}, u32[]{:S(2)}, u32[]{:S(2)}) collective-permute-start(bf16[192,256]{1,0:T(8,128)(2,1)S(1)} %collective-permute-done.12.refs_2_), channel_id=1, source_target_pairs={{0,1},{1,0},{2,3},{3,2},{4,5},{5,4},{6,7},{7,6},{8,9},{9,8},{10,11... | collective-permute-start | bytes 294920 | tf_op jit(solution)/shard_map/cond/branch_2_fun/ppermute | solution.py:46
  14.7 1.5 %collective-permute-start.10 = (bf16[192,256]{1,0:T(8,128)(2,1)S(1)}, bf16[192,256]{1,0:T(8,128)(2,1)S(1)}, u32[]{:S(2)}, u32[]{:S(2)}) collective-permute-start(bf16[192,256]{1,0:T(8,128)(2,1)S(1)} %collective-permute-done.9.refs_5_), channel_id=1, source_target_pairs={{0,1},{1,0},{2,3},{3,2},{4,5},{5,4},{6,7},{7,6},{8,9},{9,8},{10,11... | collective-permute-start | bytes 294920 | tf_op jit(solution)/shard_map/cond/branch_2_fun/ppermute | solution.py:46
  14.7 1.5 %collective-permute-start.8 = (bf16[192,256]{1,0:T(8,128)(2,1)S(1)}, bf16[192,256]{1,0:T(8,128)(2,1)S(1)}, u32[]{:S(2)}, u32[]{:S(2)}) collective-permute-start(bf16[192,256]{1,0:T(8,128)(2,1)S(1)} %collective-permute-done.7.refs_4_), channel_id=1, source_target_pairs={{0,1},{1,0},{2,3},{3,2},{4,5},{5,4},{6,7},{7,6},{8,9},{9,8},{10,11... | collective-permute-start | bytes 294920 | tf_op jit(solution)/shard_map/cond/branch_2_fun/ppermute | solution.py:46
  16.8 0.6 %copy-start.4 = (bf16[128,256]{1,0:T(8,128)(2,1)}, bf16[128,256]{1,0:T(8,128)(2,1)S(1)}, u32[]{:S(2)}) copy-start(bf16[128,256]{1,0:T(8,128)(2,1)S(1)} %get-tuple-element.150) | copy-start | bytes 196612

commit v6 on v5

--- a/solution.py
+++ b/solution.py
@@ -13,46 +13,46 @@
 LOG2E = 1.4426950408889634
 LOW = -3e38
 VMEM = 16 << 20
-LF, CF, ZF = 1, 0, ((1, 1), (0, 1), (1, 1))
-
-
-def own(part, head):
+CROSSES = ((1, 1, 1, 1), (0, 1, 0, 0), (1, 0, 0, 0))
+
+
+def own(place, head):
     return 0, 0
 
 
-def across(part, head):
-    return 3, CF
-
-
-def lane(part, head):
-    return head ^ (((part ^ (part >> 1)) & 1) if LF else 0)
-
-
-def beside(part, head):
-    return 1 + lane(part, head), LF
-
-
-def other_beside(part, head):
-    return 2 - lane(part, head), LF
+def across(place, head):
+    return 3, place // GROUP & 1
+
+
+def lane(place, head):
+    return head ^ ((place ^ place >> 1) & 1)
+
+
+def beside(place, head):
+    return 1 + lane(place, head), 1
+
+
+def other_beside(place, head):
+    return 2 - lane(place, head), 1
+
+
+def other_core(place, head):
+    return 0, 1
+
+
+def block_away(step, place, head):
+    lower = min(place, place ^ step * GROUP) // GROUP
+    return step * GROUP, CROSSES[min(step, 3) - 1][lower & 3]
 
 
 def swapped(rows, route):
     seq, head = lax.axis_size("seq"), lax.axis_size("head")
-    routes = []
+    pairs = []
     for i in range(seq):
         for h in range(head):
             step, flip = route(i, h)
-            routes.append((i * head + h, (i ^ step) * head + (h ^ flip)))
-    return lax.ppermute(rows, ("seq", "head"), routes)
-
-
-def earlier_block(step, place, head):
-    lower = min(place, place ^ step * GROUP) // GROUP
-    return step * GROUP, ZF[min(step, 3) - 1][lower & 1]
-
-
-def other_core(part, head):
-    return 0, 1
+            pairs.append((i * head + h, (i ^ step) * head + (h ^ flip)))
+    return lax.ppermute(rows, ("seq", "head"), pairs)
 
 
 def kernel_call(body, out_shape, name, arrays):
@@ -85,7 +85,7 @@
     me = lax.axis_index("seq")
     mine = me // GROUP
     for index, route in enumerate((own, across, beside, other_beside)):
-        step, _ = route(me % GROUP, lax.axis_index("head"))
+        step, _ = route(me, lax.axis_index("head"))
         messages[index][0:rows, :] = held[0][...]
         for column in range(1, columns):
             picked = held[1][...]
@@ -109,7 +109,7 @@
     state, outs = (rest[:3], rest[3:]) if resumed else ((), rest)
     tokens, width = queries_ref.shape
     heads = width // DH
-    part = lax.axis_index("seq") % GROUP
+    me = lax.axis_index("seq")
     head = lax.axis_index("head")
     queries = queries_ref[...]
     stacked = jnp.concatenate([queries[:, h * DH : (h + 1) * DH] for h in range(heads)], axis=0)
@@ -123,12 +123,12 @@
     lane = lax.broadcasted_iota(jnp.int32, (1, edge), 1)
     position = jnp.zeros_like(lane)
     for index, (route, relayed) in enumerate(places):
-        step, flip = route(part, head ^ relayed)
-        start = (part ^ step) * tokens + (head ^ relayed ^ flip) * rows - index * rows
+        step, flip = route(me, head ^ relayed)
+        start = ((me ^ step) % GROUP) * tokens + (head ^ relayed ^ flip) * rows - index * rows
         inside = (lane >= index * rows) & (lane < (index + 1) * rows)
         position = jnp.where(inside, start + lane, position)
     token = lax.broadcasted_iota(jnp.int32, (heads * tokens, 1), 0) % tokens
-    own = jnp.where(position <= part * tokens + token, scores[:, :edge], LOW)
+    own = jnp.where(position <= (me % GROUP) * tokens + token, scores[:, :edge], LOW)
     scores = jnp.concatenate([own, scores[:, edge:]], axis=1) if edge < kv.shape[0] else own
     top = jnp.broadcast_to(jnp.max(scores, axis=1, keepdims=True), (heads * tokens, DH))
     if resumed:
@@ -192,7 +192,7 @@
     mine = lax.axis_index("seq") // GROUP
     held = {0: keys_values}
     for step in range(blocks - 1, 0, -1):
-        held[step] = swapped(keys_values, functools.partial(earlier_block, step))
+        held[step] = swapped(keys_values, functools.partial(block_away, step))
     held = [held[step] for step in range(blocks)]
     held[2], held[1] = lax.optimization_barrier((held[2], held[1]))
     held[3], held[2] = lax.optimization_barrier((held[3], held[2]))

time: 17.5 us -> 17.4 us (level)
  waiting for transfers between devices: 6.28 us -> 5.38 us
  starting transfers between devices: 8.68 us -> 9.43 us
    ppermute x10, waiting for transfers between devices: 6.28 us -> 5.38 us  [swapped(): return lax.ppermute(rows, ('seq', 'head'), pairs)]
    ppermute x10, starting transfers between devices: 8.68 us -> 9.43 us  [swapped(): return lax.ppermute(rows, ('seq', 'head'), pairs)]
where the time goes in v6:
time: 17.4 us; the launch traced here: 17.2 us
  starting transfers between devices  9.43 us (54%)
  waiting for transfers between devices  5.38 us (31%)
  Pallas kernels  1.65 us (9%)
  local copies, waits for them, and re-layouts  0.73 us (4%)
    ppermute x10, starting transfers between devices, swapped(): return lax.ppermute(rows, ('seq', 'head'), pairs)  9.43 us
    ppermute x10, waiting for transfers between devices, swapped(): return lax.ppermute(rows, ('seq', 'head'), pairs)  5.38 us
    pallas_call x3, Pallas kernels, kernel_call(): pl.pallas_call(body, out_shape=out_shape, in_specs=[vmem] * len(arrays),...  1.65 us
    unnamed x6, local copies, waits for them, and re-layouts  0.63 us
  transfers between devices with their start and end apart: 10, of which 5 were waited for; matrix products, arithmetic and copies ran while one was open for 0% of the time, Pallas kernels for 6%

profile of v6, /device:TPU:21, one launch (start us, length us, event | category | flops | bytes accessed | tf_op | source)
XLA Modules:
  0.0 17.2 jit_solution(10581905602074711375)
XLA Ops:
  0.0 0.1 collective-permute-start.18
  0.1 1.9 %collective-permute-start.19 = (bf16[64,256]{1,0:T(8,128)(2,1)}, bf16[64,256]{1,0:T(8,128)(2,1)S(1)}, u32[]{:S(2)}, u32[]{:S(2)}) collective-permute-start(bf16[64,256]{1,0:T(8,128)(2,1)} %param.9), channel_id=1, source_target_pairs={{0,9},{1,8},{2,11},{3,10},{4,13},{5,12},{6,15},{7,14},{8,1},{9,0},... | collective-permute-start | bytes 98312 | tf_op jit(solution)/shard_map/ppermute | solution.py:55
  1.9 1.5 %collective-permute-start.20 = (bf16[64,256]{1,0:T(8,128)(2,1)}, bf16[64,256]{1,0:T(8,128)(2,1)S(1)}, u32[]{:S(2)}, u32[]{:S(2)}) collective-permute-start(bf16[64,256]{1,0:T(8,128)(2,1)} %param.9), channel_id=1, source_target_pairs={{0,25},{1,24},{2,27},{3,26},{4,29},{5,28},{6,31},{7,30},{8,16},{9,... | collective-permute-start | bytes 98312 | tf_op jit(solution)/shard_map/ppermute | solution.py:55
  3.5 0.4 %collective-permute-done.18 = bf16[64,256]{1,0:T(8,128)(2,1)S(1)} collective-permute-done((bf16[64,256]{1,0:T(8,128)(2,1)}, bf16[64,256]{1,0:T(8,128)(2,1)S(1)}, u32[]{:S(2)}, u32[]{:S(2)}) %collective-permute-start.18) | collective-permute-done | bytes 32800 | tf_op jit(solution)/shard_map/ppermute | solution.py:55
  3.9 0.6 %collective-permute-done.19 = bf16[64,256]{1,0:T(8,128)(2,1)S(1)} collective-permute-done((bf16[64,256]{1,0:T(8,128)(2,1)}, bf16[64,256]{1,0:T(8,128)(2,1)S(1)}, u32[]{:S(2)}, u32[]{:S(2)}) %collective-permute-start.19) | collective-permute-done | bytes 32800 | tf_op jit(solution)/shard_map/ppermute | solution.py:55
  4.5 1.9 %collective-permute-done.20 = bf16[64,256]{1,0:T(8,128)(2,1)S(1)} collective-permute-done((bf16[64,256]{1,0:T(8,128)(2,1)}, bf16[64,256]{1,0:T(8,128)(2,1)S(1)}, u32[]{:S(2)}, u32[]{:S(2)}) %collective-permute-start.20) | collective-permute-done | bytes 32800 | tf_op jit(solution)/shard_map/ppermute | solution.py:55
  6.4 10.2 %conditional.3 = (bf16[128,256]{1,0:T(8,128)(2,1)S(1)}) conditional(s32[]{:T(128)} %clamp.3, bf16[128,256]{1,0:T(8,128)(2,1)S(1)} %get-tuple-element.107, (s32[16,3]{0,1:T(4,128)S(1)}, bf16[64,256]{1,0:T(8,128)(2,1)S(1)}, bf16[64,256]{1,0:T(8,128)(2,1)S(1)}, bf16[64,256]{1,0:T(8,128)(2,1)S(1)}, bf16[64,256]{1,0:T(8,128)(2,1)S(1)}, ...), branch_computations={%region_2.3_spmd, %region_3.4_spmd, %region_4.5_spmd} | conditional | bytes 3015356 | solution.py:206
  6.4 0.1 copy.10.selected_ref
  6.5 0.1 pick_3.1
  6.7 1.2 %collective-permute-start.12 = (bf16[192,256]{1,0:T(8,128)(2,1)S(1)}, bf16[192,256]{1,0:T(8,128)(2,1)S(1)}, u32[]{:S(2)}, u32[]{:S(2)}) collective-permute-start(bf16[192,256]{1,0:T(8,128)(2,1)S(1)} %get-tuple-element.67), channel_id=1, source_target_pairs={{0,6},{1,7},{2,4},{3,5},{4,2},{5,3},{6,0},{7,1},{8,15},{9,14},{10,... | collective-permute-start | bytes 294920 | tf_op jit(solution)/shard_map/cond/branch_2_fun/ppermute | solution.py:55
  7.9 2.0 %collective-permute-start.9 = (bf16[192,256]{1,0:T(8,128)(2,1)S(1)}, bf16[192,256]{1,0:T(8,128)(2,1)S(1)}, u32[]{:S(2)}, u32[]{:S(2)}) collective-permute-start(bf16[192,256]{1,0:T(8,128)(2,1)S(1)} %get-tuple-element.65), channel_id=1, source_target_pairs={{0,5},{1,2},{2,1},{3,6},{4,7},{5,0},{6,3},{7,4},{8,13},{9,10},{10,... | collective-permute-start | bytes 294920 | tf_op jit(solution)/shard_map/cond/branch_2_fun/ppermute | solution.py:55
  9.9 0.6 %collective-permute-start.11 = (bf16[192,256]{1,0:T(8,128)(2,1)S(1)}, bf16[192,256]{1,0:T(8,128)(2,1)S(1)}, u32[]{:S(2)}, u32[]{:S(2)}) collective-permute-start(bf16[192,256]{1,0:T(8,128)(2,1)S(1)} %get-tuple-element.66.refs_0_), channel_id=1, source_target_pairs={{0,1},{1,0},{2,3},{3,2},{4,5},{5,4},{6,7},{7,6},{8,9},{9,8},{10,11... | collective-permute-start | bytes 294920 | tf_op jit(solution)/shard_map/cond/branch_2_fun/ppermute | solution.py:55
  10.5 0.9 %collective-permute-done.12.refs_2_ = bf16[192,256]{1,0:T(8,128)(2,1)S(1)} collective-permute-done((bf16[192,256]{1,0:T(8,128)(2,1)S(1)}, bf16[192,256]{1,0:T(8,128)(2,1)S(1)}, u32[]{:S(2)}, u32[]{:S(2)}) %collective-permute-start.12) | collective-permute-done | bytes 98336 | tf_op jit(solution)/shard_map/cond/branch_2_fun/ppermute | solution.py:55
  11.4 1.6 %collective-permute-start.13 = (bf16[192,256]{1,0:T(8,128)(2,1)S(1)}, bf16[192,256]{1,0:T(8,128)(2,1)S(1)}, u32[]{:S(2)}, u32[]{:S(2)}) collective-permute-start(bf16[192,256]{1,0:T(8,128)(2,1)S(1)} %collective-permute-done.12.refs_2_), channel_id=1, source_target_pairs={{0,1},{1,0},{2,3},{3,2},{4,5},{5,4},{6,7},{7,6},{8,9},{9,8},{10,11... | collective-permute-start | bytes 294920 | tf_op jit(solution)/shard_map/cond/branch_2_fun/ppermute | solution.py:55
  13.0 1.5 %collective-permute-done.9.refs_5_ = bf16[192,256]{1,0:T(8,128)(2,1)S(1)} collective-permute-done((bf16[192,256]{1,0:T(8,128)(2,1)S(1)}, bf16[192,256]{1,0:T(8,128)(2,1)S(1)}, u32[]{:S(2)}, u32[]{:S(2)}) %collective-permute-start.9) | collective-permute-done | bytes 98336 | tf_op jit(solution)/shard_map/cond/branch_2_fun/ppermute | solution.py:55
  14.5 0.0 collective-permute-start.10
  14.6 0.0 collective-permute-done.7.refs_4_
  14.6 0.5 %collective-permute-start.8 = (bf16[192,256]{1,0:T(8,128)(2,1)S(1)}, bf16[192,256]{1,0:T(8,128)(2,1)S(1)}, u32[]{:S(2)}, u32[]{:S(2)}) collective-permute-start(bf16[192,256]{1,0:T(8,128)(2,1)S(1)} %collective-permute-done.7.refs_4_), channel_id=1, source_target_pairs={{0,1},{1,0},{2,3},{3,2},{4,5},{5,4},{6,7},{7,6},{8,9},{9,8},{10,11... | collective-permute-start | bytes 294920 | tf_op jit(solution)/shard_map/cond/branch_2_fun/ppermute | solution.py:55
  15.1 0.0 collective-permute-done.11.refs_1_
  15.1 0.0 collective-permute-done.13.refs_3_
  15.1 1.0 %attend_6.3 = (f32[256,128]{1,0:T(8,128)S(1)}, f32[256,128]{1,0:T(8,128)S(1)}, f32[256,128]{1,0:T(8,128)S(1)}) custom-call(bf16[128,256]{1,0:T(8,128)(2,1)S(1)} %copy-done.2, bf16[192,256]{1,0:T(8,128)(2,1)S(1)} %get-tuple-element.66.refs_0_, bf16[192,256]{1,0:T(8,128)(2,1)S(1)} %collective-permute-done.11.refs_1_, ...), custom_call_target="tpu_custom_call" | custom-call | tf_op jit(solution)/shard_map/cond/branch_2_fun/attend_6/pallas_call | solution.py:60
  16.1 0.5 %attend_2.3 = bf16[128,256]{1,0:T(8,128)(2,1)S(1)} custom-call(bf16[128,256]{1,0:T(8,128)(2,1)S(1)} %copy-done.2, bf16[192,256]{1,0:T(8,128)(2,1)S(1)} %collective-permute-done.8.refs_0_, bf16[192,256]{1,0:T(8,128)(2,1)S(1)} %collective-permute-done.10.refs_1_, f32[256,128]{1,0:T(8,128)S(1)} %get-tuple-element.68.refs_2_, ...), custom_call_target="tpu_custom_call" | custom-call | tf_op jit(solution)/shard_map/cond/branch_2_fun/attend_2/pallas_call | solution.py:60
  16.6 0.0 copy-start.4
  16.6 0.6 %copy-done.4 = bf16[128,256]{1,0:T(8,128)(2,1)} copy-done((bf16[128,256]{1,0:T(8,128)(2,1)}, bf16[128,256]{1,0:T(8,128)(2,1)S(1)}, u32[]{:S(2)}) %copy-start.4) | copy-done | bytes 65560
  (11 shorter events, 0.0 us)
Async XLA Ops:
  0.0 3.5 %copy-start.3 = (bf16[64,256]{1,0:T(8,128)(2,1)S(1)}, bf16[64,256]{1,0:T(8,128)(2,1)}, u32[]{:S(2)}) copy-start(bf16[64,256]{1,0:T(8,128)(2,1)} %param.9) | copy-start | bytes 98308
  0.0 3.9 %collective-permute-start.18 = (bf16[64,256]{1,0:T(8,128)(2,1)}, bf16[64,256]{1,0:T(8,128)(2,1)S(1)}, u32[]{:S(2)}, u32[]{:S(2)}) collective-permute-start(bf16[64,256]{1,0:T(8,128)(2,1)} %param.9), channel_id=1, source_target_pairs={{0,16},{1,17},{2,18},{3,19},{4,20},{5,21},{6,22},{7,23},{8,25},{9,... | collective-permute-start | bytes 98312 | tf_op jit(solution)/shard_map/ppermute | solution.py:55
  0.1 4.5 %collective-permute-start.19 = (bf16[64,256]{1,0:T(8,128)(2,1)}, bf16[64,256]{1,0:T(8,128)(2,1)S(1)}, u32[]{:S(2)}, u32[]{:S(2)}) collective-permute-start(bf16[64,256]{1,0:T(8,128)(2,1)} %param.9), channel_id=1, source_target_pairs={{0,9},{1,8},{2,11},{3,10},{4,13},{5,12},{6,15},{7,14},{8,1},{9,0},... | collective-permute-start | bytes 98312 | tf_op jit(solution)/shard_map/ppermute | solution.py:55
  1.9 4.5 %collective-permute-start.20 = (bf16[64,256]{1,0:T(8,128)(2,1)}, bf16[64,256]{1,0:T(8,128)(2,1)S(1)}, u32[]{:S(2)}, u32[]{:S(2)}) collective-permute-start(bf16[64,256]{1,0:T(8,128)(2,1)} %param.9), channel_id=1, source_target_pairs={{0,25},{1,24},{2,27},{3,26},{4,29},{5,28},{6,31},{7,30},{8,16},{9,... | collective-permute-start | bytes 98312 | tf_op jit(solution)/shard_map/ppermute | solution.py:55
  3.5 2.9 %copy-start.5 = (s32[16,3]{0,1:T(4,128)S(1)}, s32[16,3]{0,1:T(4,128)}, u32[]{:S(2)}) copy-start(s32[16,3]{0,1:T(4,128)} %param.10) | copy-start | bytes 580
  6.5 8.6 %copy-start.2 = (bf16[128,256]{1,0:T(8,128)(2,1)S(1)}, bf16[128,256]{1,0:T(8,128)(2,1)}, u32[]{:S(2)}) copy-start(bf16[128,256]{1,0:T(8,128)(2,1)} %get-tuple-element.58.queries_ref) | copy-start | bytes 196612 | tf_op jit(solution)/shard_map/cond
  6.7 4.8 %collective-permute-start.12 = (bf16[192,256]{1,0:T(8,128)(2,1)S(1)}, bf16[192,256]{1,0:T(8,128)(2,1)S(1)}, u32[]{:S(2)}, u32[]{:S(2)}) collective-permute-start(bf16[192,256]{1,0:T(8,128)(2,1)S(1)} %get-tuple-element.67), channel_id=1, source_target_pairs={{0,6},{1,7},{2,4},{3,5},{4,2},{5,3},{6,0},{7,1},{8,15},{9,14},{10,... | collective-permute-start | bytes 294920 | tf_op jit(solution)/shard_map/cond/branch_2_fun/ppermute | solution.py:55
  7.9 6.7 %collective-permute-start.9 = (bf16[192,256]{1,0:T(8,128)(2,1)S(1)}, bf16[192,256]{1,0:T(8,128)(2,1)S(1)}, u32[]{:S(2)}, u32[]{:S(2)}) collective-permute-start(bf16[192,256]{1,0:T(8,128)(2,1)S(1)} %get-tuple-element.65), channel_id=1, source_target_pairs={{0,5},{1,2},{2,1},{3,6},{4,7},{5,0},{6,3},{7,4},{8,13},{9,10},{10,... | collective-permute-start | bytes 294920 | tf_op jit(solution)/shard_map/cond/branch_2_fun/ppermute | solution.py:55
  9.9 4.7 %collective-permute-start.7 = (bf16[192,256]{1,0:T(8,128)(2,1)S(1)}, bf16[192,256]{1,0:T(8,128)(2,1)S(1)}, u32[]{:S(2)}, u32[]{:S(2)}) collective-permute-start(bf16[192,256]{1,0:T(8,128)(2,1)S(1)} %get-tuple-element.64), channel_id=1, source_target_pairs={{0,3},{1,4},{2,7},{3,0},{4,1},{5,6},{6,5},{7,2},{8,11},{9,12},{10,... | collective-permute-start | bytes 294920 | tf_op jit(solution)/shard_map/cond/branch_2_fun/ppermute | solution.py:55
  9.9 5.2 %collective-permute-start.11 = (bf16[192,256]{1,0:T(8,128)(2,1)S(1)}, bf16[192,256]{1,0:T(8,128)(2,1)S(1)}, u32[]{:S(2)}, u32[]{:S(2)}) collective-permute-start(bf16[192,256]{1,0:T(8,128)(2,1)S(1)} %get-tuple-element.66.refs_0_), channel_id=1, source_target_pairs={{0,1},{1,0},{2,3},{3,2},{4,5},{5,4},{6,7},{7,6},{8,9},{9,8},{10,11... | collective-permute-start | bytes 294920 | tf_op jit(solution)/shard_map/cond/branch_2_fun/ppermute | solution.py:55
  11.4 3.6 %collective-permute-start.13 = (bf16[192,256]{1,0:T(8,128)(2,1)S(1)}, bf16[192,256]{1,0:T(8,128)(2,1)S(1)}, u32[]{:S(2)}, u32[]{:S(2)}) collective-permute-start(bf16[192,256]{1,0:T(8,128)(2,1)S(1)} %collective-permute-done.12.refs_2_), channel_id=1, source_target_pairs={{0,1},{1,0},{2,3},{3,2},{4,5},{5,4},{6,7},{7,6},{8,9},{9,8},{10,11... | collective-permute-start | bytes 294920 | tf_op jit(solution)/shard_map/cond/branch_2_fun/ppermute | solution.py:55
  14.5 1.5 %collective-permute-start.10 = (bf16[192,256]{1,0:T(8,128)(2,1)S(1)}, bf16[192,256]{1,0:T(8,128)(2,1)S(1)}, u32[]{:S(2)}, u32[]{:S(2)}) collective-permute-start(bf16[192,256]{1,0:T(8,128)(2,1)S(1)} %collective-permute-done.9.refs_5_), channel_id=1, source_target_pairs={{0,1},{1,0},{2,3},{3,2},{4,5},{5,4},{6,7},{7,6},{8,9},{9,8},{10,11... | collective-permute-start | bytes 294920 | tf_op jit(solution)/shard_map/cond/branch_2_fun/ppermute | solution.py:55
  14.6 1.5 %collective-permute-start.8 = (bf16[192,256]{1,0:T(8,128)(2,1)S(1)}, bf16[192,256]{1,0:T(8,128)(2,1)S(1)}, u32[]{:S(2)}, u32[]{:S(2)}) collective-permute-start(bf16[192,256]{1,0:T(8,128)(2,1)S(1)} %collective-permute-done.7.refs_4_), channel_id=1, source_target_pairs={{0,1},{1,0},{2,3},{3,2},{4,5},{5,4},{6,7},{7,6},{8,9},{9,8},{10,11... | collective-permute-start | bytes 294920 | tf_op jit(solution)/shard_map/cond/branch_2_fun/ppermute | solution.py:55
  16.6 0.6 %copy-start.4 = (bf16[128,256]{1,0:T(8,128)(2,1)}, bf16[128,256]{1,0:T(8,128)(2,1)S(1)}, u32[]{:S(2)}) copy-start(bf16[128,256]{1,0:T(8,128)(2,1)S(1)} %get-tuple-element.150) | copy-start | bytes 196612

commit v7 on v6

--- a/solution.py
+++ b/solution.py
@@ -79,19 +79,27 @@
     return kernel_call(join_kernel, out, "join", pieces)
 
 
-def pick_kernel(columns, blocks, selected_ref, *refs):
+def plan_kernel(selected_ref, wanted_ref):
+    me = lax.axis_index("seq")
+    for index, route in enumerate((own, across, beside, other_beside)):
+        step, _ = route(me, lax.axis_index("head"))
+        for column in range(1, TOPK):
+            wanted = selected_ref[pl.ds(me ^ step, 1), column : column + 1] ^ (me // GROUP)
+            row = index * (TOPK - 1) + column - 1
+            wanted_ref[row : row + 1, :] = jnp.broadcast_to(wanted, (1, DH))
+
+
+def pick_kernel(columns, blocks, wanted_ref, *refs):
     held, messages = refs[:blocks], refs[blocks:]
     rows = held[0].shape[0]
-    me = lax.axis_index("seq")
-    mine = me // GROUP
-    for index, route in enumerate((own, across, beside, other_beside)):
-        step, _ = route(me, lax.axis_index("head"))
+    for index in range(GROUP):
         messages[index][0:rows, :] = held[0][...]
         for column in range(1, columns):
             picked = held[1][...]
             if columns > 2:
-                wanted = selected_ref[pl.ds(me ^ step, 1), column : column + 1] ^ mine
-                wanted = jnp.broadcast_to(wanted, picked.shape)
+                row = index * (TOPK - 1) + column - 1
+                wanted = jnp.broadcast_to(wanted_ref[row : row + 1, :], (rows, DH))
+                wanted = jnp.concatenate([wanted, wanted], axis=1)
                 for other in range(2, blocks):
                     picked = jnp.where(wanted == other, held[other][...], picked)
             messages[index][column * rows : (column + 1) * rows, :] = picked
@@ -196,6 +204,7 @@
     held = [held[step] for step in range(blocks)]
     held[2], held[1] = lax.optimization_barrier((held[2], held[1]))
     held[3], held[2] = lax.optimization_barrier((held[3], held[2]))
+    selected = kernel_call(plan_kernel, jax.ShapeDtypeStruct((2 * GROUP, DH), jnp.int32), "plan", [selected])
     level = jnp.minimum(mine, TOPK - 1)
     first = lax.cond(
         level == 0,

time: 17.4 us -> 17.2 us (0.989)
  the two profiles are of different devices: /device:TPU:21 before, /device:TPU:0 now
where the time goes in v7:
time: 17.2 us; the launch traced here: 17.1 us
  starting transfers between devices  8.38 us (49%)
  waiting for transfers between devices  6.53 us (38%)
  local copies, waits for them, and re-layouts  1.42 us (8%)
  Pallas kernels  0.65 us (4%)
    ppermute x7, starting transfers between devices, swapped(): return lax.ppermute(rows, ('seq', 'head'), pairs)  8.38 us
    ppermute x7, waiting for transfers between devices, swapped(): return lax.ppermute(rows, ('seq', 'head'), pairs)  6.53 us
    unnamed x7, local copies, waits for them, and re-layouts  1.39 us
    pallas_call x3, Pallas kernels, kernel_call(): pl.pallas_call(body, out_shape=out_shape, in_specs=[vmem] * len(arrays),...  0.65 us
  transfers between devices with their start and end apart: 7, of which 4 were waited for; matrix products, arithmetic and copies ran while one was open for 1% of the time, Pallas kernels for 4%

profile of v7, /device:TPU:0, one launch (start us, length us, event | category | flops | bytes accessed | tf_op | source)
XLA Modules:
  0.0 17.1 jit_solution(3666464601972919185)
XLA Ops:
  0.0 4.0 %collective-permute-start.18 = (bf16[64,256]{1,0:T(8,128)(2,1)}, bf16[64,256]{1,0:T(8,128)(2,1)S(1)}, u32[]{:S(2)}, u32[]{:S(2)}) collective-permute-start(bf16[64,256]{1,0:T(8,128)(2,1)} %param.9), channel_id=1, source_target_pairs={{0,16},{1,17},{2,18},{3,19},{4,20},{5,21},{6,22},{7,23},{8,25},{9,... | collective-permute-start | bytes 98312 | tf_op jit(solution)/shard_map/ppermute | solution.py:55
  4.0 1.3 %collective-permute-start.19 = (bf16[64,256]{1,0:T(8,128)(2,1)}, bf16[64,256]{1,0:T(8,128)(2,1)S(1)}, u32[]{:S(2)}, u32[]{:S(2)}) collective-permute-start(bf16[64,256]{1,0:T(8,128)(2,1)} %param.9), channel_id=1, source_target_pairs={{0,9},{1,8},{2,11},{3,10},{4,13},{5,12},{6,15},{7,14},{8,1},{9,0},... | collective-permute-start | bytes 98312 | tf_op jit(solution)/shard_map/ppermute | solution.py:55
  5.3 0.0 collective-permute-start.20
  5.3 0.7 %copy-done.5 = s32[16,3]{0,1:T(4,128)S(1)} copy-done((s32[16,3]{0,1:T(4,128)S(1)}, s32[16,3]{0,1:T(4,128)}, u32[]{:S(2)}) %copy-start.5) | copy-done | bytes 216
  6.0 0.1 copy.7.selected_ref
  6.1 0.0 copy-done.3
  6.1 0.1 plan.1
  6.2 10.2 %conditional.2 = (bf16[128,256]{1,0:T(8,128)(2,1)S(1)}) conditional(s32[]{:T(128)} %convert_element_type.3, () %tuple.23, (bf16[64,256]{1,0:T(8,128)(2,1)S(1)}, bf16[128,256]{1,0:T(8,128)(2,1)}) %tuple.43), branch_computations={%region_0.1_spmd, %region_1.2_spmd} | conditional | bytes 1704132 | solution.py:209
  6.2 2.7 %collective-permute-start.15 = (bf16[64,256]{1,0:T(8,128)(2,1)S(1)}, bf16[64,256]{1,0:T(8,128)(2,1)S(1)}, u32[]{:S(2)}, u32[]{:S(2)}) collective-permute-start(bf16[64,256]{1,0:T(8,128)(2,1)S(1)} %get-tuple-element.43.refs_0_), channel_id=1, source_target_pairs={{0,6},{1,7},{2,4},{3,5},{4,2},{5,3},{6,0},{7,1},{8,15},{9,14},{10,... | collective-permute-start | bytes 98312 | tf_op jit(solution)/shard_map/cond/branch_1_fun/ppermute | solution.py:55
  8.9 0.0 collective-permute-start.14
  8.9 2.1 %collective-permute-done.15.refs_3_ = bf16[64,256]{1,0:T(8,128)(2,1)S(1)} collective-permute-done((bf16[64,256]{1,0:T(8,128)(2,1)S(1)}, bf16[64,256]{1,0:T(8,128)(2,1)S(1)}, u32[]{:S(2)}, u32[]{:S(2)}) %collective-permute-start.15) | collective-permute-done | bytes 32800 | tf_op jit(solution)/shard_map/cond/branch_1_fun/ppermute | solution.py:55
  11.0 0.0 collective-permute-start.16
  11.0 1.2 %collective-permute-done.14.refs_1_ = bf16[64,256]{1,0:T(8,128)(2,1)S(1)} collective-permute-done((bf16[64,256]{1,0:T(8,128)(2,1)S(1)}, bf16[64,256]{1,0:T(8,128)(2,1)S(1)}, u32[]{:S(2)}, u32[]{:S(2)}) %collective-permute-start.14) | collective-permute-done | bytes 32800 | tf_op jit(solution)/shard_map/cond/branch_1_fun/ppermute | solution.py:55
  12.2 2.1 %collective-permute-done.16.refs_2_ = bf16[64,256]{1,0:T(8,128)(2,1)S(1)} collective-permute-done((bf16[64,256]{1,0:T(8,128)(2,1)S(1)}, bf16[64,256]{1,0:T(8,128)(2,1)S(1)}, u32[]{:S(2)}, u32[]{:S(2)}) %collective-permute-start.16) | collective-permute-done | bytes 32800 | tf_op jit(solution)/shard_map/cond/branch_1_fun/ppermute | solution.py:55
  14.4 0.3 %collective-permute-start.17 = (bf16[256,256]{1,0:T(8,128)(2,1)S(1)}, bf16[256,256]{1,0:T(8,128)(2,1)S(1)}, u32[]{:S(2)}, u32[]{:S(2)}) collective-permute-start(bf16[256,256]{1,0:T(8,128)(2,1)S(1)} %join.1), channel_id=1, source_target_pairs={{0,1},{1,0},{2,3},{3,2},{4,5},{5,4},{6,7},{7,6},{8,9},{9,8},{10,11... | collective-permute-start | bytes 393224 | tf_op jit(solution)/shard_map/cond/branch_1_fun/ppermute | solution.py:55
  14.7 0.0 copy-start
  14.8 1.0 %collective-permute-done.17 = bf16[256,256]{1,0:T(8,128)(2,1)S(1)} collective-permute-done((bf16[256,256]{1,0:T(8,128)(2,1)S(1)}, bf16[256,256]{1,0:T(8,128)(2,1)S(1)}, u32[]{:S(2)}, u32[]{:S(2)}) %collective-permute-start.17) | collective-permute-done | bytes 131104 | tf_op jit(solution)/shard_map/cond/branch_1_fun/ppermute | solution.py:55
  15.8 0.0 copy-done
  15.8 0.6 %attend_8.1 = bf16[128,256]{1,0:T(8,128)(2,1)S(1)} custom-call(bf16[128,256]{1,0:T(8,128)(2,1)S(1)} %copy-done, bf16[64,256]{1,0:T(8,128)(2,1)S(1)} %get-tuple-element.87.refs_0_, bf16[64,256]{1,0:T(8,128)(2,1)S(1)} %get-tuple-element.86.refs_1_, bf16[64,256]{1,0:T(8,128)(2,1)S(1)} %get-tuple-element.85.refs_2_, ...), custom_call_target="tpu_custom_call" | custom-call | tf_op jit(solution)/shard_map/cond/branch_1_fun/attend_8/pallas_call | solution.py:60
  16.4 0.0 collective-permute-done.18
  16.4 0.0 collective-permute-done.19
  16.4 0.0 collective-permute-done.20
  16.4 0.0 copy-start.4
  16.5 0.6 %copy-done.4 = bf16[128,256]{1,0:T(8,128)(2,1)} copy-done((bf16[128,256]{1,0:T(8,128)(2,1)}, bf16[128,256]{1,0:T(8,128)(2,1)S(1)}, u32[]{:S(2)}) %copy-start.4) | copy-done | bytes 65560
  (6 shorter events, 0.0 us)
Async XLA Ops:
  0.0 6.1 %copy-start.3 = (bf16[64,256]{1,0:T(8,128)(2,1)S(1)}, bf16[64,256]{1,0:T(8,128)(2,1)}, u32[]{:S(2)}) copy-start(bf16[64,256]{1,0:T(8,128)(2,1)} %param.9) | copy-start | bytes 98308
  0.0 16.4 %collective-permute-start.18 = (bf16[64,256]{1,0:T(8,128)(2,1)}, bf16[64,256]{1,0:T(8,128)(2,1)S(1)}, u32[]{:S(2)}, u32[]{:S(2)}) collective-permute-start(bf16[64,256]{1,0:T(8,128)(2,1)} %param.9), channel_id=1, source_target_pairs={{0,16},{1,17},{2,18},{3,19},{4,20},{5,21},{6,22},{7,23},{8,25},{9,... | collective-permute-start | bytes 98312 | tf_op jit(solution)/shard_map/ppermute | solution.py:55
  4.0 12.4 %collective-permute-start.19 = (bf16[64,256]{1,0:T(8,128)(2,1)}, bf16[64,256]{1,0:T(8,128)(2,1)S(1)}, u32[]{:S(2)}, u32[]{:S(2)}) collective-permute-start(bf16[64,256]{1,0:T(8,128)(2,1)} %param.9), channel_id=1, source_target_pairs={{0,9},{1,8},{2,11},{3,10},{4,13},{5,12},{6,15},{7,14},{8,1},{9,0},... | collective-permute-start | bytes 98312 | tf_op jit(solution)/shard_map/ppermute | solution.py:55
  5.3 11.1 %collective-permute-start.20 = (bf16[64,256]{1,0:T(8,128)(2,1)}, bf16[64,256]{1,0:T(8,128)(2,1)S(1)}, u32[]{:S(2)}, u32[]{:S(2)}) collective-permute-start(bf16[64,256]{1,0:T(8,128)(2,1)} %param.9), channel_id=1, source_target_pairs={{0,25},{1,24},{2,27},{3,26},{4,29},{5,28},{6,31},{7,30},{8,16},{9,... | collective-permute-start | bytes 98312 | tf_op jit(solution)/shard_map/ppermute | solution.py:55
  5.3 0.7 %copy-start.5 = (s32[16,3]{0,1:T(4,128)S(1)}, s32[16,3]{0,1:T(4,128)}, u32[]{:S(2)}) copy-start(s32[16,3]{0,1:T(4,128)} %param.10) | copy-start | bytes 580
  6.2 4.8 %collective-permute-start.15 = (bf16[64,256]{1,0:T(8,128)(2,1)S(1)}, bf16[64,256]{1,0:T(8,128)(2,1)S(1)}, u32[]{:S(2)}, u32[]{:S(2)}) collective-permute-start(bf16[64,256]{1,0:T(8,128)(2,1)S(1)} %get-tuple-element.43.refs_0_), channel_id=1, source_target_pairs={{0,6},{1,7},{2,4},{3,5},{4,2},{5,3},{6,0},{7,1},{8,15},{9,14},{10,... | collective-permute-start | bytes 98312 | tf_op jit(solution)/shard_map/cond/branch_1_fun/ppermute | solution.py:55
  8.9 3.3 %collective-permute-start.14 = (bf16[64,256]{1,0:T(8,128)(2,1)S(1)}, bf16[64,256]{1,0:T(8,128)(2,1)S(1)}, u32[]{:S(2)}, u32[]{:S(2)}) collective-permute-start(bf16[64,256]{1,0:T(8,128)(2,1)S(1)} %get-tuple-element.43.refs_0_), channel_id=1, source_target_pairs={{0,3},{1,4},{2,7},{3,0},{4,1},{5,6},{6,5},{7,2},{8,11},{9,12},{10,... | collective-permute-start | bytes 98312 | tf_op jit(solution)/shard_map/cond/branch_1_fun/ppermute | solution.py:55
  11.0 3.3 %collective-permute-start.16 = (bf16[64,256]{1,0:T(8,128)(2,1)S(1)}, bf16[64,256]{1,0:T(8,128)(2,1)S(1)}, u32[]{:S(2)}, u32[]{:S(2)}) collective-permute-start(bf16[64,256]{1,0:T(8,128)(2,1)S(1)} %get-tuple-element.43.refs_0_), channel_id=1, source_target_pairs={{0,5},{1,2},{2,1},{3,6},{4,7},{5,0},{6,3},{7,4},{8,13},{9,10},{10,... | collective-permute-start | bytes 98312 | tf_op jit(solution)/shard_map/cond/branch_1_fun/ppermute | solution.py:55
  14.4 1.4 %collective-permute-start.17 = (bf16[256,256]{1,0:T(8,128)(2,1)S(1)}, bf16[256,256]{1,0:T(8,128)(2,1)S(1)}, u32[]{:S(2)}, u32[]{:S(2)}) collective-permute-start(bf16[256,256]{1,0:T(8,128)(2,1)S(1)} %join.1), channel_id=1, source_target_pairs={{0,1},{1,0},{2,3},{3,2},{4,5},{5,4},{6,7},{7,6},{8,9},{9,8},{10,11... | collective-permute-start | bytes 393224 | tf_op jit(solution)/shard_map/cond/branch_1_fun/ppermute | solution.py:55
  14.7 1.1 %copy-start = (bf16[128,256]{1,0:T(8,128)(2,1)S(1)}, bf16[128,256]{1,0:T(8,128)(2,1)}, u32[]{:S(2)}) copy-start(bf16[128,256]{1,0:T(8,128)(2,1)} %get-tuple-element.40.queries_ref) | copy-start | bytes 196612 | tf_op jit(solution)/shard_map/cond
  16.4 0.6 %copy-start.4 = (bf16[128,256]{1,0:T(8,128)(2,1)}, bf16[128,256]{1,0:T(8,128)(2,1)S(1)}, u32[]{:S(2)}) copy-start(bf16[128,256]{1,0:T(8,128)(2,1)S(1)} %get-tuple-element.134) | copy-start | bytes 196612

commit v8 on v7

--- a/solution.py
+++ b/solution.py
@@ -12,6 +12,7 @@
 TOPK = 3
 LOG2E = 1.4426950408889634
 LOW = -3e38
+SCALE = DH ** (-0.5) * LOG2E
 VMEM = 16 << 20
 CROSSES = ((1, 1, 1, 1), (0, 1, 0, 0), (1, 0, 0, 0))
 
@@ -126,7 +127,7 @@
     kv = jnp.concatenate(parts, axis=0)
     scores = lax.dot_general(
         stacked, kv[:, :DH], (((1,), (1,)), ((), ())), preferred_element_type=jnp.float32
-    ) * (DH ** (-0.5) * LOG2E)
+    )
     edge = min(-(-len(pieces) * rows // DH) * DH, kv.shape[0])
     lane = lax.broadcasted_iota(jnp.int32, (1, edge), 1)
     position = jnp.zeros_like(lane)
@@ -143,12 +144,12 @@
         before = state[0][...]
         top = jnp.maximum(top, before)
     columns = [scores[:, start : start + DH] for start in range(0, scores.shape[1], DH)]
-    weights = jnp.concatenate([jnp.exp2(c - top[:, : c.shape[1]]).astype(jnp.bfloat16) for c in columns], axis=1)
+    weights = jnp.concatenate([jnp.exp2((c - top[:, : c.shape[1]]) * SCALE).astype(jnp.bfloat16) for c in columns], axis=1)
     values = jnp.concatenate([kv[:, DH:], jnp.ones_like(kv[:, DH:])], axis=1)
     sums = jnp.dot(weights, values, preferred_element_type=jnp.float32)
     out, total = sums[:, :DH], sums[:, DH:]
     if resumed:
-        scale = jnp.exp2(before - top)
+        scale = jnp.exp2((before - top) * SCALE)
         total += scale * state[1][...]
         out += scale * state[2][...]
     if not last:
@@ -188,9 +189,11 @@
     length = held[0].shape[0]
     messages = pick(columns, selected, held)
     near = [messages[0]] + [swapped(m, route) for m, route in zip(messages[1:], (across, beside, other_beside))]
+    state = attend(length, queries, [((own, 0), near[0]), ((across, 0), near[1])], last=False)
+    near[3], *state = lax.optimization_barrier((near[3], *state))
     far = [swapped(piece, other_core) for piece in near]
-    placed = [((own, 0), near[0]), ((own, 1), far[0]), ((across, 0), near[1]), ((across, 1), far[1]), ((beside, 0), near[2]), ((other_beside, 0), near[3])]
-    state = attend(length, queries, placed, last=False)
+    placed = [((own, 1), far[0]), ((across, 1), far[1]), ((beside, 0), near[2]), ((other_beside, 0), near[3])]
+    state = attend(length, queries, placed, state, last=False)
     placed = [((beside, 1), far[2]), ((other_beside, 1), far[3])]
     return attend(length, queries, placed, state)
 

time: 17.2 us -> 17.2 us (level)
  no operation moved by 1% of the time
where the time goes in v8:
time: 17.2 us; the launch traced here: 17.1 us
  starting transfers between devices  8.38 us (49%)
  waiting for transfers between devices  6.53 us (38%)
  local copies, waits for them, and re-layouts  1.42 us (8%)
  Pallas kernels  0.65 us (4%)
    ppermute x7, starting transfers between devices, swapped(): return lax.ppermute(rows, ('seq', 'head'), pairs)  8.38 us
    ppermute x7, waiting for transfers between devices, swapped(): return lax.ppermute(rows, ('seq', 'head'), pairs)  6.53 us
    unnamed x7, local copies, waits for them, and re-layouts  1.39 us
    pallas_call x3, Pallas kernels, kernel_call(): pl.pallas_call(body, out_shape=out_shape, in_specs=[vmem] * len(arrays),...  0.65 us
  transfers between devices with their start and end apart: 7, of which 4 were waited for; matrix products, arithmetic and copies ran while one was open for 1% of the time, Pallas kernels for 4%

profile of v8, /device:TPU:0, one launch (start us, length us, event | category | flops | bytes accessed | tf_op | source)
XLA Modules:
  0.0 17.1 jit_solution(6944018793570006108)
XLA Ops:
  0.0 4.0 %collective-permute-start.18 = (bf16[64,256]{1,0:T(8,128)(2,1)}, bf16[64,256]{1,0:T(8,128)(2,1)S(1)}, u32[]{:S(2)}, u32[]{:S(2)}) collective-permute-start(bf16[64,256]{1,0:T(8,128)(2,1)} %param.9), channel_id=1, source_target_pairs={{0,16},{1,17},{2,18},{3,19},{4,20},{5,21},{6,22},{7,23},{8,25},{9,... | collective-permute-start | bytes 98312 | tf_op jit(solution)/shard_map/ppermute | solution.py:56
  4.0 1.3 %collective-permute-start.19 = (bf16[64,256]{1,0:T(8,128)(2,1)}, bf16[64,256]{1,0:T(8,128)(2,1)S(1)}, u32[]{:S(2)}, u32[]{:S(2)}) collective-permute-start(bf16[64,256]{1,0:T(8,128)(2,1)} %param.9), channel_id=1, source_target_pairs={{0,9},{1,8},{2,11},{3,10},{4,13},{5,12},{6,15},{7,14},{8,1},{9,0},... | collective-permute-start | bytes 98312 | tf_op jit(solution)/shard_map/ppermute | solution.py:56
  5.3 0.0 collective-permute-start.20
  5.3 0.7 %copy-done.5 = s32[16,3]{0,1:T(4,128)S(1)} copy-done((s32[16,3]{0,1:T(4,128)S(1)}, s32[16,3]{0,1:T(4,128)}, u32[]{:S(2)}) %copy-start.5) | copy-done | bytes 216
  6.0 0.1 copy.7.selected_ref
  6.1 0.0 copy-done.3
  6.1 0.1 plan.1
  6.2 10.2 %conditional.2 = (bf16[128,256]{1,0:T(8,128)(2,1)S(1)}) conditional(s32[]{:T(128)} %convert_element_type.3, () %tuple.25, (bf16[64,256]{1,0:T(8,128)(2,1)S(1)}, bf16[128,256]{1,0:T(8,128)(2,1)}) %tuple.45), branch_computations={%region_0.1_spmd, %region_1.2_spmd} | conditional | bytes 1704132 | solution.py:212
  6.2 2.7 %collective-permute-start.15 = (bf16[64,256]{1,0:T(8,128)(2,1)S(1)}, bf16[64,256]{1,0:T(8,128)(2,1)S(1)}, u32[]{:S(2)}, u32[]{:S(2)}) collective-permute-start(bf16[64,256]{1,0:T(8,128)(2,1)S(1)} %get-tuple-element.43.refs_0_), channel_id=1, source_target_pairs={{0,6},{1,7},{2,4},{3,5},{4,2},{5,3},{6,0},{7,1},{8,15},{9,14},{10,... | collective-permute-start | bytes 98312 | tf_op jit(solution)/shard_map/cond/branch_1_fun/ppermute | solution.py:56
  8.9 0.0 collective-permute-start.14
  8.9 2.1 %collective-permute-done.15.refs_3_ = bf16[64,256]{1,0:T(8,128)(2,1)S(1)} collective-permute-done((bf16[64,256]{1,0:T(8,128)(2,1)S(1)}, bf16[64,256]{1,0:T(8,128)(2,1)S(1)}, u32[]{:S(2)}, u32[]{:S(2)}) %collective-permute-start.15) | collective-permute-done | bytes 32800 | tf_op jit(solution)/shard_map/cond/branch_1_fun/ppermute | solution.py:56
  11.0 0.0 collective-permute-start.16
  11.0 1.2 %collective-permute-done.14.refs_1_ = bf16[64,256]{1,0:T(8,128)(2,1)S(1)} collective-permute-done((bf16[64,256]{1,0:T(8,128)(2,1)S(1)}, bf16[64,256]{1,0:T(8,128)(2,1)S(1)}, u32[]{:S(2)}, u32[]{:S(2)}) %collective-permute-start.14) | collective-permute-done | bytes 32800 | tf_op jit(solution)/shard_map/cond/branch_1_fun/ppermute | solution.py:56
  12.2 2.1 %collective-permute-done.16.refs_2_ = bf16[64,256]{1,0:T(8,128)(2,1)S(1)} collective-permute-done((bf16[64,256]{1,0:T(8,128)(2,1)S(1)}, bf16[64,256]{1,0:T(8,128)(2,1)S(1)}, u32[]{:S(2)}, u32[]{:S(2)}) %collective-permute-start.16) | collective-permute-done | bytes 32800 | tf_op jit(solution)/shard_map/cond/branch_1_fun/ppermute | solution.py:56
  14.4 0.3 %collective-permute-start.17 = (bf16[256,256]{1,0:T(8,128)(2,1)S(1)}, bf16[256,256]{1,0:T(8,128)(2,1)S(1)}, u32[]{:S(2)}, u32[]{:S(2)}) collective-permute-start(bf16[256,256]{1,0:T(8,128)(2,1)S(1)} %join.1), channel_id=1, source_target_pairs={{0,1},{1,0},{2,3},{3,2},{4,5},{5,4},{6,7},{7,6},{8,9},{9,8},{10,11... | collective-permute-start | bytes 393224 | tf_op jit(solution)/shard_map/cond/branch_1_fun/ppermute | solution.py:56
  14.7 0.0 copy-start
  14.8 1.0 %collective-permute-done.17 = bf16[256,256]{1,0:T(8,128)(2,1)S(1)} collective-permute-done((bf16[256,256]{1,0:T(8,128)(2,1)S(1)}, bf16[256,256]{1,0:T(8,128)(2,1)S(1)}, u32[]{:S(2)}, u32[]{:S(2)}) %collective-permute-start.17) | collective-permute-done | bytes 131104 | tf_op jit(solution)/shard_map/cond/branch_1_fun/ppermute | solution.py:56
  15.8 0.0 copy-done
  15.8 0.6 %attend_8.1 = bf16[128,256]{1,0:T(8,128)(2,1)S(1)} custom-call(bf16[128,256]{1,0:T(8,128)(2,1)S(1)} %copy-done, bf16[64,256]{1,0:T(8,128)(2,1)S(1)} %get-tuple-element.101.refs_0_, bf16[64,256]{1,0:T(8,128)(2,1)S(1)} %get-tuple-element.100.refs_1_, bf16[64,256]{1,0:T(8,128)(2,1)S(1)} %get-tuple-element.99.refs_2_, ...), custom_call_target="tpu_custom_call" | custom-call | tf_op jit(solution)/shard_map/cond/branch_1_fun/attend_8/pallas_call | solution.py:61
  16.4 0.0 collective-permute-done.18
  16.4 0.0 collective-permute-done.19
  16.4 0.0 collective-permute-done.20
  16.4 0.0 copy-start.4
  16.5 0.6 %copy-done.4 = bf16[128,256]{1,0:T(8,128)(2,1)} copy-done((bf16[128,256]{1,0:T(8,128)(2,1)}, bf16[128,256]{1,0:T(8,128)(2,1)S(1)}, u32[]{:S(2)}) %copy-start.4) | copy-done | bytes 65560
  (6 shorter events, 0.0 us)
Async XLA Ops:
  0.0 6.1 %copy-start.3 = (bf16[64,256]{1,0:T(8,128)(2,1)S(1)}, bf16[64,256]{1,0:T(8,128)(2,1)}, u32[]{:S(2)}) copy-start(bf16[64,256]{1,0:T(8,128)(2,1)} %param.9) | copy-start | bytes 98308
  0.0 16.4 %collective-permute-start.18 = (bf16[64,256]{1,0:T(8,128)(2,1)}, bf16[64,256]{1,0:T(8,128)(2,1)S(1)}, u32[]{:S(2)}, u32[]{:S(2)}) collective-permute-start(bf16[64,256]{1,0:T(8,128)(2,1)} %param.9), channel_id=1, source_target_pairs={{0,16},{1,17},{2,18},{3,19},{4,20},{5,21},{6,22},{7,23},{8,25},{9,... | collective-permute-start | bytes 98312 | tf_op jit(solution)/shard_map/ppermute | solution.py:56
  4.0 12.4 %collective-permute-start.19 = (bf16[64,256]{1,0:T(8,128)(2,1)}, bf16[64,256]{1,0:T(8,128)(2,1)S(1)}, u32[]{:S(2)}, u32[]{:S(2)}) collective-permute-start(bf16[64,256]{1,0:T(8,128)(2,1)} %param.9), channel_id=1, source_target_pairs={{0,9},{1,8},{2,11},{3,10},{4,13},{5,12},{6,15},{7,14},{8,1},{9,0},... | collective-permute-start | bytes 98312 | tf_op jit(solution)/shard_map/ppermute | solution.py:56
  5.3 11.1 %collective-permute-start.20 = (bf16[64,256]{1,0:T(8,128)(2,1)}, bf16[64,256]{1,0:T(8,128)(2,1)S(1)}, u32[]{:S(2)}, u32[]{:S(2)}) collective-permute-start(bf16[64,256]{1,0:T(8,128)(2,1)} %param.9), channel_id=1, source_target_pairs={{0,25},{1,24},{2,27},{3,26},{4,29},{5,28},{6,31},{7,30},{8,16},{9,... | collective-permute-start | bytes 98312 | tf_op jit(solution)/shard_map/ppermute | solution.py:56
  5.3 0.7 %copy-start.5 = (s32[16,3]{0,1:T(4,128)S(1)}, s32[16,3]{0,1:T(4,128)}, u32[]{:S(2)}) copy-start(s32[16,3]{0,1:T(4,128)} %param.10) | copy-start | bytes 580
  6.2 4.8 %collective-permute-start.15 = (bf16[64,256]{1,0:T(8,128)(2,1)S(1)}, bf16[64,256]{1,0:T(8,128)(2,1)S(1)}, u32[]{:S(2)}, u32[]{:S(2)}) collective-permute-start(bf16[64,256]{1,0:T(8,128)(2,1)S(1)} %get-tuple-element.43.refs_0_), channel_id=1, source_target_pairs={{0,6},{1,7},{2,4},{3,5},{4,2},{5,3},{6,0},{7,1},{8,15},{9,14},{10,... | collective-permute-start | bytes 98312 | tf_op jit(solution)/shard_map/cond/branch_1_fun/ppermute | solution.py:56
  8.9 3.3 %collective-permute-start.14 = (bf16[64,256]{1,0:T(8,128)(2,1)S(1)}, bf16[64,256]{1,0:T(8,128)(2,1)S(1)}, u32[]{:S(2)}, u32[]{:S(2)}) collective-permute-start(bf16[64,256]{1,0:T(8,128)(2,1)S(1)} %get-tuple-element.43.refs_0_), channel_id=1, source_target_pairs={{0,3},{1,4},{2,7},{3,0},{4,1},{5,6},{6,5},{7,2},{8,11},{9,12},{10,... | collective-permute-start | bytes 98312 | tf_op jit(solution)/shard_map/cond/branch_1_fun/ppermute | solution.py:56
  11.0 3.3 %collective-permute-start.16 = (bf16[64,256]{1,0:T(8,128)(2,1)S(1)}, bf16[64,256]{1,0:T(8,128)(2,1)S(1)}, u32[]{:S(2)}, u32[]{:S(2)}) collective-permute-start(bf16[64,256]{1,0:T(8,128)(2,1)S(1)} %get-tuple-element.43.refs_0_), channel_id=1, source_target_pairs={{0,5},{1,2},{2,1},{3,6},{4,7},{5,0},{6,3},{7,4},{8,13},{9,10},{10,... | collective-permute-start | bytes 98312 | tf_op jit(solution)/shard_map/cond/branch_1_fun/ppermute | solution.py:56
  14.4 1.4 %collective-permute-start.17 = (bf16[256,256]{1,0:T(8,128)(2,1)S(1)}, bf16[256,256]{1,0:T(8,128)(2,1)S(1)}, u32[]{:S(2)}, u32[]{:S(2)}) collective-permute-start(bf16[256,256]{1,0:T(8,128)(2,1)S(1)} %join.1), channel_id=1, source_target_pairs={{0,1},{1,0},{2,3},{3,2},{4,5},{5,4},{6,7},{7,6},{8,9},{9,8},{10,11... | collective-permute-start | bytes 393224 | tf_op jit(solution)/shard_map/cond/branch_1_fun/ppermute | solution.py:56
  14.7 1.1 %copy-start = (bf16[128,256]{1,0:T(8,128)(2,1)S(1)}, bf16[128,256]{1,0:T(8,128)(2,1)}, u32[]{:S(2)}) copy-start(bf16[128,256]{1,0:T(8,128)(2,1)} %get-tuple-element.40.queries_ref) | copy-start | bytes 196612 | tf_op jit(solution)/shard_map/cond
  16.4 0.6 %copy-start.4 = (bf16[128,256]{1,0:T(8,128)(2,1)}, bf16[128,256]{1,0:T(8,128)(2,1)S(1)}, u32[]{:S(2)}) copy-start(bf16[128,256]{1,0:T(8,128)(2,1)S(1)} %get-tuple-element.148) | copy-start | bytes 196612

commit v9 on v8

--- a/solution.py
+++ b/solution.py
@@ -207,6 +207,7 @@
     held = [held[step] for step in range(blocks)]
     held[2], held[1] = lax.optimization_barrier((held[2], held[1]))
     held[3], held[2] = lax.optimization_barrier((held[3], held[2]))
+    selected, held[1] = lax.optimization_barrier((selected, held[1]))
     selected = kernel_call(plan_kernel, jax.ShapeDtypeStruct((2 * GROUP, DH), jnp.int32), "plan", [selected])
     level = jnp.minimum(mine, TOPK - 1)
     first = lax.cond(

time: 17.2 us -> 17.3 us (level)
  the two profiles are of different devices: /device:TPU:0 before, /device:TPU:21 now
where the time goes in v9:
time: 17.3 us; the launch traced here: 17.1 us
  starting transfers between devices  9.43 us (55%)
  waiting for transfers between devices  5.1 us (29%)
  Pallas kernels  1.82 us (11%)
  local copies, waits for them, and re-layouts  0.73 us (4%)
    ppermute x10, starting transfers between devices, swapped(): return lax.ppermute(rows, ('seq', 'head'), pairs)  9.43 us
    ppermute x10, waiting for transfers between devices, swapped(): return lax.ppermute(rows, ('seq', 'head'), pairs)  5.1 us
    pallas_call x5, Pallas kernels, kernel_call(): pl.pallas_call(body, out_shape=out_shape, in_specs=[vmem] * len(arrays),...  1.82 us
    unnamed x6, local copies, waits for them, and re-layouts  0.63 us
  transfers between devices with their start and end apart: 10, of which 7 were waited for; matrix products, arithmetic and copies ran while one was open for 0% of the time, Pallas kernels for 7%

profile of v9, /device:TPU:21, one launch (start us, length us, event | category | flops | bytes accessed | tf_op | source)
XLA Modules:
  0.0 17.1 jit_solution(7324349293841760872)
XLA Ops:
  0.0 0.1 collective-permute-start.18
  0.1 1.9 %collective-permute-start.19 = (bf16[64,256]{1,0:T(8,128)(2,1)}, bf16[64,256]{1,0:T(8,128)(2,1)S(1)}, u32[]{:S(2)}, u32[]{:S(2)}) collective-permute-start(bf16[64,256]{1,0:T(8,128)(2,1)} %param.9), channel_id=1, source_target_pairs={{0,9},{1,8},{2,11},{3,10},{4,13},{5,12},{6,15},{7,14},{8,1},{9,0},... | collective-permute-start | bytes 98312 | tf_op jit(solution)/shard_map/ppermute | solution.py:56
  1.9 1.5 %collective-permute-start.20 = (bf16[64,256]{1,0:T(8,128)(2,1)}, bf16[64,256]{1,0:T(8,128)(2,1)S(1)}, u32[]{:S(2)}, u32[]{:S(2)}) collective-permute-start(bf16[64,256]{1,0:T(8,128)(2,1)} %param.9), channel_id=1, source_target_pairs={{0,25},{1,24},{2,27},{3,26},{4,29},{5,28},{6,31},{7,30},{8,16},{9,... | collective-permute-start | bytes 98312 | tf_op jit(solution)/shard_map/ppermute | solution.py:56
  3.5 0.4 %collective-permute-done.18 = bf16[64,256]{1,0:T(8,128)(2,1)S(1)} collective-permute-done((bf16[64,256]{1,0:T(8,128)(2,1)}, bf16[64,256]{1,0:T(8,128)(2,1)S(1)}, u32[]{:S(2)}, u32[]{:S(2)}) %collective-permute-start.18) | collective-permute-done | bytes 32800 | tf_op jit(solution)/shard_map/ppermute | solution.py:56
  3.9 0.6 %collective-permute-done.19 = bf16[64,256]{1,0:T(8,128)(2,1)S(1)} collective-permute-done((bf16[64,256]{1,0:T(8,128)(2,1)}, bf16[64,256]{1,0:T(8,128)(2,1)S(1)}, u32[]{:S(2)}, u32[]{:S(2)}) %collective-permute-start.19) | collective-permute-done | bytes 32800 | tf_op jit(solution)/shard_map/ppermute | solution.py:56
  4.5 1.9 %collective-permute-done.20 = bf16[64,256]{1,0:T(8,128)(2,1)S(1)} collective-permute-done((bf16[64,256]{1,0:T(8,128)(2,1)}, bf16[64,256]{1,0:T(8,128)(2,1)S(1)}, u32[]{:S(2)}, u32[]{:S(2)}) %collective-permute-start.20) | collective-permute-done | bytes 32800 | tf_op jit(solution)/shard_map/ppermute | solution.py:56
  6.4 0.1 copy.7.selected_ref
  6.5 0.1 plan.1
  6.6 9.9 %conditional.3 = (bf16[128,256]{1,0:T(8,128)(2,1)S(1)}) conditional(s32[]{:T(128)} %clamp.3, bf16[128,256]{1,0:T(8,128)(2,1)S(1)} %get-tuple-element.109, (s32[8,128]{1,0:T(8,128)S(1)}, bf16[64,256]{1,0:T(8,128)(2,1)S(1)}, bf16[64,256]{1,0:T(8,128)(2,1)S(1)}, bf16[64,256]{1,0:T(8,128)(2,1)S(1)}, bf16[64,256]{1,0:T(8,128)(2,1)S(1)}, ...), branch_computations={%region_2.3_spmd, %region_3.4_spmd, %region_4.5_spmd} | conditional | bytes 3014972 | solution.py:219
  6.6 1.2 %collective-permute-start.10 = (bf16[192,256]{1,0:T(8,128)(2,1)S(1)}, bf16[192,256]{1,0:T(8,128)(2,1)S(1)}, u32[]{:S(2)}, u32[]{:S(2)}) collective-permute-start(bf16[192,256]{1,0:T(8,128)(2,1)S(1)} %get-tuple-element.74), channel_id=1, source_target_pairs={{0,6},{1,7},{2,4},{3,5},{4,2},{5,3},{6,0},{7,1},{8,15},{9,14},{10,... | collective-permute-start | bytes 294920 | tf_op jit(solution)/shard_map/cond/branch_2_fun/ppermute | solution.py:56
  7.9 2.0 %collective-permute-start.9 = (bf16[192,256]{1,0:T(8,128)(2,1)S(1)}, bf16[192,256]{1,0:T(8,128)(2,1)S(1)}, u32[]{:S(2)}, u32[]{:S(2)}) collective-permute-start(bf16[192,256]{1,0:T(8,128)(2,1)S(1)} %get-tuple-element.72), channel_id=1, source_target_pairs={{0,5},{1,2},{2,1},{3,6},{4,7},{5,0},{6,3},{7,4},{8,13},{9,10},{10,... | collective-permute-start | bytes 294920 | tf_op jit(solution)/shard_map/cond/branch_2_fun/ppermute | solution.py:56
  9.8 0.6 %collective-permute-start.12 = (bf16[192,256]{1,0:T(8,128)(2,1)S(1)}, bf16[192,256]{1,0:T(8,128)(2,1)S(1)}, u32[]{:S(2)}, u32[]{:S(2)}) collective-permute-start(bf16[192,256]{1,0:T(8,128)(2,1)S(1)} %get-tuple-element.73.refs_0_), channel_id=1, source_target_pairs={{0,1},{1,0},{2,3},{3,2},{4,5},{5,4},{6,7},{7,6},{8,9},{9,8},{10,11... | collective-permute-start | bytes 294920 | tf_op jit(solution)/shard_map/cond/branch_2_fun/ppermute | solution.py:56
  10.5 0.9 %collective-permute-done.10.refs_1_ = bf16[192,256]{1,0:T(8,128)(2,1)S(1)} collective-permute-done((bf16[192,256]{1,0:T(8,128)(2,1)S(1)}, bf16[192,256]{1,0:T(8,128)(2,1)S(1)}, u32[]{:S(2)}, u32[]{:S(2)}) %collective-permute-start.10) | collective-permute-done | bytes 98336 | tf_op jit(solution)/shard_map/cond/branch_2_fun/ppermute | solution.py:56
  11.4 1.6 %collective-permute-start.13 = (bf16[192,256]{1,0:T(8,128)(2,1)S(1)}, bf16[192,256]{1,0:T(8,128)(2,1)S(1)}, u32[]{:S(2)}, u32[]{:S(2)}) collective-permute-start(bf16[192,256]{1,0:T(8,128)(2,1)S(1)} %collective-permute-done.10.refs_1_), channel_id=1, source_target_pairs={{0,1},{1,0},{2,3},{3,2},{4,5},{5,4},{6,7},{7,6},{8,9},{9,8},{10,11... | collective-permute-start | bytes 294920 | tf_op jit(solution)/shard_map/cond/branch_2_fun/ppermute | solution.py:56
  13.0 0.5 %attend_2.6 = (f32[256,128]{1,0:T(8,128)S(1)}, f32[256,128]{1,0:T(8,128)S(1)}, f32[256,128]{1,0:T(8,128)S(1)}) custom-call(bf16[128,256]{1,0:T(8,128)(2,1)S(1)} %copy-done.2, bf16[192,256]{1,0:T(8,128)(2,1)S(1)} %get-tuple-element.73.refs_0_, bf16[192,256]{1,0:T(8,128)(2,1)S(1)} %collective-permute-done.10.refs_1_), custom_call_target="tpu_custom_call" | custom-call | tf_op jit(solution)/shard_map/cond/branch_2_fun/attend_2/pallas_call | solution.py:61
  13.5 1.0 %collective-permute-done.9.refs_3_ = bf16[192,256]{1,0:T(8,128)(2,1)S(1)} collective-permute-done((bf16[192,256]{1,0:T(8,128)(2,1)S(1)}, bf16[192,256]{1,0:T(8,128)(2,1)S(1)}, u32[]{:S(2)}, u32[]{:S(2)}) %collective-permute-start.9) | collective-permute-done | bytes 98336 | tf_op jit(solution)/shard_map/cond/branch_2_fun/ppermute | solution.py:56
  14.5 0.0 collective-permute-done.7.refs_2_
  14.5 0.5 %collective-permute-start.8 = (bf16[192,256]{1,0:T(8,128)(2,1)S(1)}, bf16[192,256]{1,0:T(8,128)(2,1)S(1)}, u32[]{:S(2)}, u32[]{:S(2)}) collective-permute-start(bf16[192,256]{1,0:T(8,128)(2,1)S(1)} %collective-permute-done.7.refs_2_), channel_id=1, source_target_pairs={{0,1},{1,0},{2,3},{3,2},{4,5},{5,4},{6,7},{7,6},{8,9},{9,8},{10,11... | collective-permute-start | bytes 294920 | tf_op jit(solution)/shard_map/cond/branch_2_fun/ppermute | solution.py:56
  15.0 0.7 %attend_4.3 = (f32[256,128]{1,0:T(8,128)S(1)}, f32[256,128]{1,0:T(8,128)S(1)}, f32[256,128]{1,0:T(8,128)S(1)}) custom-call(bf16[128,256]{1,0:T(8,128)(2,1)S(1)} %copy-done.2, bf16[192,256]{1,0:T(8,128)(2,1)S(1)} %collective-permute-done.12.refs_0_, bf16[192,256]{1,0:T(8,128)(2,1)S(1)} %collective-permute-done.13.refs_1_, ...), custom_call_target="tpu_custom_call" | custom-call | tf_op jit(solution)/shard_map/cond/branch_2_fun/attend_4/pallas_call | solution.py:61
  15.7 0.1 collective-permute-done.11.refs_1_
  15.8 0.2 collective-permute-done.8.refs_0_
  16.0 0.5 %attend_2.7 = bf16[128,256]{1,0:T(8,128)(2,1)S(1)} custom-call(bf16[128,256]{1,0:T(8,128)(2,1)S(1)} %copy-done.2, bf16[192,256]{1,0:T(8,128)(2,1)S(1)} %collective-permute-done.8.refs_0_, bf16[192,256]{1,0:T(8,128)(2,1)S(1)} %collective-permute-done.11.refs_1_, f32[256,128]{1,0:T(8,128)S(1)} %get-tuple-element.82.refs_2_, ...), custom_call_target="tpu_custom_call" | custom-call | tf_op jit(solution)/shard_map/cond/branch_2_fun/attend_2/pallas_call | solution.py:61
  16.5 0.0 copy-start.4
  16.5 0.6 %copy-done.4 = bf16[128,256]{1,0:T(8,128)(2,1)} copy-done((bf16[128,256]{1,0:T(8,128)(2,1)}, bf16[128,256]{1,0:T(8,128)(2,1)S(1)}, u32[]{:S(2)}) %copy-start.4) | copy-done | bytes 65560
  (13 shorter events, 0.1 us)
Async XLA Ops:
  0.0 3.5 %copy-start.3 = (bf16[64,256]{1,0:T(8,128)(2,1)S(1)}, bf16[64,256]{1,0:T(8,128)(2,1)}, u32[]{:S(2)}) copy-start(bf16[64,256]{1,0:T(8,128)(2,1)} %param.9) | copy-start | bytes 98308
  0.0 3.9 %collective-permute-start.18 = (bf16[64,256]{1,0:T(8,128)(2,1)}, bf16[64,256]{1,0:T(8,128)(2,1)S(1)}, u32[]{:S(2)}, u32[]{:S(2)}) collective-permute-start(bf16[64,256]{1,0:T(8,128)(2,1)} %param.9), channel_id=1, source_target_pairs={{0,16},{1,17},{2,18},{3,19},{4,20},{5,21},{6,22},{7,23},{8,25},{9,... | collective-permute-start | bytes 98312 | tf_op jit(solution)/shard_map/ppermute | solution.py:56
  0.1 4.5 %collective-permute-start.19 = (bf16[64,256]{1,0:T(8,128)(2,1)}, bf16[64,256]{1,0:T(8,128)(2,1)S(1)}, u32[]{:S(2)}, u32[]{:S(2)}) collective-permute-start(bf16[64,256]{1,0:T(8,128)(2,1)} %param.9), channel_id=1, source_target_pairs={{0,9},{1,8},{2,11},{3,10},{4,13},{5,12},{6,15},{7,14},{8,1},{9,0},... | collective-permute-start | bytes 98312 | tf_op jit(solution)/shard_map/ppermute | solution.py:56
  1.9 4.5 %collective-permute-start.20 = (bf16[64,256]{1,0:T(8,128)(2,1)}, bf16[64,256]{1,0:T(8,128)(2,1)S(1)}, u32[]{:S(2)}, u32[]{:S(2)}) collective-permute-start(bf16[64,256]{1,0:T(8,128)(2,1)} %param.9), channel_id=1, source_target_pairs={{0,25},{1,24},{2,27},{3,26},{4,29},{5,28},{6,31},{7,30},{8,16},{9,... | collective-permute-start | bytes 98312 | tf_op jit(solution)/shard_map/ppermute | solution.py:56
  3.5 2.9 %copy-start.5 = (s32[16,3]{0,1:T(4,128)S(1)}, s32[16,3]{0,1:T(4,128)}, u32[]{:S(2)}) copy-start(s32[16,3]{0,1:T(4,128)} %param.10) | copy-start | bytes 580
  6.6 6.4 %copy-start.2 = (bf16[128,256]{1,0:T(8,128)(2,1)S(1)}, bf16[128,256]{1,0:T(8,128)(2,1)}, u32[]{:S(2)}) copy-start(bf16[128,256]{1,0:T(8,128)(2,1)} %get-tuple-element.65.queries_ref) | copy-start | bytes 196612 | tf_op jit(solution)/shard_map/cond
  6.6 4.8 %collective-permute-start.10 = (bf16[192,256]{1,0:T(8,128)(2,1)S(1)}, bf16[192,256]{1,0:T(8,128)(2,1)S(1)}, u32[]{:S(2)}, u32[]{:S(2)}) collective-permute-start(bf16[192,256]{1,0:T(8,128)(2,1)S(1)} %get-tuple-element.74), channel_id=1, source_target_pairs={{0,6},{1,7},{2,4},{3,5},{4,2},{5,3},{6,0},{7,1},{8,15},{9,14},{10,... | collective-permute-start | bytes 294920 | tf_op jit(solution)/shard_map/cond/branch_2_fun/ppermute | solution.py:56
  7.9 6.7 %collective-permute-start.9 = (bf16[192,256]{1,0:T(8,128)(2,1)S(1)}, bf16[192,256]{1,0:T(8,128)(2,1)S(1)}, u32[]{:S(2)}, u32[]{:S(2)}) collective-permute-start(bf16[192,256]{1,0:T(8,128)(2,1)S(1)} %get-tuple-element.72), channel_id=1, source_target_pairs={{0,5},{1,2},{2,1},{3,6},{4,7},{5,0},{6,3},{7,4},{8,13},{9,10},{10,... | collective-permute-start | bytes 294920 | tf_op jit(solution)/shard_map/cond/branch_2_fun/ppermute | solution.py:56
  9.8 4.7 %collective-permute-start.7 = (bf16[192,256]{1,0:T(8,128)(2,1)S(1)}, bf16[192,256]{1,0:T(8,128)(2,1)S(1)}, u32[]{:S(2)}, u32[]{:S(2)}) collective-permute-start(bf16[192,256]{1,0:T(8,128)(2,1)S(1)} %get-tuple-element.71), channel_id=1, source_target_pairs={{0,3},{1,4},{2,7},{3,0},{4,1},{5,6},{6,5},{7,2},{8,11},{9,12},{10,... | collective-permute-start | bytes 294920 | tf_op jit(solution)/shard_map/cond/branch_2_fun/ppermute | solution.py:56
  9.8 5.2 %collective-permute-start.12 = (bf16[192,256]{1,0:T(8,128)(2,1)S(1)}, bf16[192,256]{1,0:T(8,128)(2,1)S(1)}, u32[]{:S(2)}, u32[]{:S(2)}) collective-permute-start(bf16[192,256]{1,0:T(8,128)(2,1)S(1)} %get-tuple-element.73.refs_0_), channel_id=1, source_target_pairs={{0,1},{1,0},{2,3},{3,2},{4,5},{5,4},{6,7},{7,6},{8,9},{9,8},{10,11... | collective-permute-start | bytes 294920 | tf_op jit(solution)/shard_map/cond/branch_2_fun/ppermute | solution.py:56
  11.4 3.6 %collective-permute-start.13 = (bf16[192,256]{1,0:T(8,128)(2,1)S(1)}, bf16[192,256]{1,0:T(8,128)(2,1)S(1)}, u32[]{:S(2)}, u32[]{:S(2)}) collective-permute-start(bf16[192,256]{1,0:T(8,128)(2,1)S(1)} %collective-permute-done.10.refs_1_), channel_id=1, source_target_pairs={{0,1},{1,0},{2,3},{3,2},{4,5},{5,4},{6,7},{7,6},{8,9},{9,8},{10,11... | collective-permute-start | bytes 294920 | tf_op jit(solution)/shard_map/cond/branch_2_fun/ppermute | solution.py:56
  14.5 1.3 %collective-permute-start.11 = (bf16[192,256]{1,0:T(8,128)(2,1)S(1)}, bf16[192,256]{1,0:T(8,128)(2,1)S(1)}, u32[]{:S(2)}, u32[]{:S(2)}) collective-permute-start(bf16[192,256]{1,0:T(8,128)(2,1)S(1)} %collective-permute-done.9.refs_3_), channel_id=1, source_target_pairs={{0,1},{1,0},{2,3},{3,2},{4,5},{5,4},{6,7},{7,6},{8,9},{9,8},{10,11... | collective-permute-start | bytes 294920 | tf_op jit(solution)/shard_map/cond/branch_2_fun/ppermute | solution.py:56
  14.5 1.5 %collective-permute-start.8 = (bf16[192,256]{1,0:T(8,128)(2,1)S(1)}, bf16[192,256]{1,0:T(8,128)(2,1)S(1)}, u32[]{:S(2)}, u32[]{:S(2)}) collective-permute-start(bf16[192,256]{1,0:T(8,128)(2,1)S(1)} %collective-permute-done.7.refs_2_), channel_id=1, source_target_pairs={{0,1},{1,0},{2,3},{3,2},{4,5},{5,4},{6,7},{7,6},{8,9},{9,8},{10,11... | collective-permute-start | bytes 294920 | tf_op jit(solution)/shard_map/cond/branch_2_fun/ppermute | solution.py:56
  16.5 0.6 %copy-start.4 = (bf16[128,256]{1,0:T(8,128)(2,1)}, bf16[128,256]{1,0:T(8,128)(2,1)S(1)}, u32[]{:S(2)}) copy-start(bf16[128,256]{1,0:T(8,128)(2,1)S(1)} %get-tuple-element.152) | copy-start | bytes 196612

commit v10 on v8

--- a/solution.py
+++ b/solution.py
@@ -189,11 +189,9 @@
     length = held[0].shape[0]
     messages = pick(columns, selected, held)
     near = [messages[0]] + [swapped(m, route) for m, route in zip(messages[1:], (across, beside, other_beside))]
-    state = attend(length, queries, [((own, 0), near[0]), ((across, 0), near[1])], last=False)
-    near[3], *state = lax.optimization_barrier((near[3], *state))
     far = [swapped(piece, other_core) for piece in near]
-    placed = [((own, 1), far[0]), ((across, 1), far[1]), ((beside, 0), near[2]), ((other_beside, 0), near[3])]
-    state = attend(length, queries, placed, state, last=False)
+    placed = [((own, 0), near[0]), ((own, 1), far[0]), ((across, 0), near[1]), ((across, 1), far[1]), ((beside, 0), near[2]), ((other_beside, 0), near[3])]
+    state = attend(length, queries, placed, last=False)
     placed = [((beside, 1), far[2]), ((other_beside, 1), far[3])]
     return attend(length, queries, placed, state)
 

time: 17.2 us -> 17.2 us (level)
  no operation moved by 1% of the time
where the time goes in v10:
time: 17.2 us; the launch traced here: 17.1 us
  starting transfers between devices  8.38 us (49%)
  waiting for transfers between devices  6.53 us (38%)
  local copies, waits for them, and re-layouts  1.42 us (8%)
  Pallas kernels  0.65 us (4%)
    ppermute x7, starting transfers between devices, swapped(): return lax.ppermute(rows, ('seq', 'head'), pairs)  8.38 us
    ppermute x7, waiting for transfers between devices, swapped(): return lax.ppermute(rows, ('seq', 'head'), pairs)  6.53 us
    unnamed x7, local copies, waits for them, and re-layouts  1.39 us
    pallas_call x3, Pallas kernels, kernel_call(): pl.pallas_call(body, out_shape=out_shape, in_specs=[vmem] * len(arrays),...  0.65 us
  transfers between devices with their start and end apart: 7, of which 4 were waited for; matrix products, arithmetic and copies ran while one was open for 1% of the time, Pallas kernels for 4%

profile of v10, /device:TPU:0, one launch (start us, length us, event | category | flops | bytes accessed | tf_op | source)
XLA Modules:
  0.0 17.1 jit_solution(17742430344965548683)
XLA Ops:
  0.0 4.0 %collective-permute-start.18 = (bf16[64,256]{1,0:T(8,128)(2,1)}, bf16[64,256]{1,0:T(8,128)(2,1)S(1)}, u32[]{:S(2)}, u32[]{:S(2)}) collective-permute-start(bf16[64,256]{1,0:T(8,128)(2,1)} %param.9), channel_id=1, source_target_pairs={{0,16},{1,17},{2,18},{3,19},{4,20},{5,21},{6,22},{7,23},{8,25},{9,... | collective-permute-start | bytes 98312 | tf_op jit(solution)/shard_map/ppermute | solution.py:56
  4.0 1.3 %collective-permute-start.19 = (bf16[64,256]{1,0:T(8,128)(2,1)}, bf16[64,256]{1,0:T(8,128)(2,1)S(1)}, u32[]{:S(2)}, u32[]{:S(2)}) collective-permute-start(bf16[64,256]{1,0:T(8,128)(2,1)} %param.9), channel_id=1, source_target_pairs={{0,9},{1,8},{2,11},{3,10},{4,13},{5,12},{6,15},{7,14},{8,1},{9,0},... | collective-permute-start | bytes 98312 | tf_op jit(solution)/shard_map/ppermute | solution.py:56
  5.3 0.0 collective-permute-start.20
  5.3 0.7 %copy-done.5 = s32[16,3]{0,1:T(4,128)S(1)} copy-done((s32[16,3]{0,1:T(4,128)S(1)}, s32[16,3]{0,1:T(4,128)}, u32[]{:S(2)}) %copy-start.5) | copy-done | bytes 216
  6.0 0.1 copy.7.selected_ref
  6.1 0.0 copy-done.3
  6.1 0.1 plan.1
  6.2 10.2 %conditional.2 = (bf16[128,256]{1,0:T(8,128)(2,1)S(1)}) conditional(s32[]{:T(128)} %convert_element_type.3, () %tuple.23, (bf16[64,256]{1,0:T(8,128)(2,1)S(1)}, bf16[128,256]{1,0:T(8,128)(2,1)}) %tuple.43), branch_computations={%region_0.1_spmd, %region_1.2_spmd} | conditional | bytes 1704132 | solution.py:210
  6.2 2.7 %collective-permute-start.15 = (bf16[64,256]{1,0:T(8,128)(2,1)S(1)}, bf16[64,256]{1,0:T(8,128)(2,1)S(1)}, u32[]{:S(2)}, u32[]{:S(2)}) collective-permute-start(bf16[64,256]{1,0:T(8,128)(2,1)S(1)} %get-tuple-element.43.refs_0_), channel_id=1, source_target_pairs={{0,6},{1,7},{2,4},{3,5},{4,2},{5,3},{6,0},{7,1},{8,15},{9,14},{10,... | collective-permute-start | bytes 98312 | tf_op jit(solution)/shard_map/cond/branch_1_fun/ppermute | solution.py:56
  8.9 0.0 collective-permute-start.14
  8.9 2.1 %collective-permute-done.15.refs_3_ = bf16[64,256]{1,0:T(8,128)(2,1)S(1)} collective-permute-done((bf16[64,256]{1,0:T(8,128)(2,1)S(1)}, bf16[64,256]{1,0:T(8,128)(2,1)S(1)}, u32[]{:S(2)}, u32[]{:S(2)}) %collective-permute-start.15) | collective-permute-done | bytes 32800 | tf_op jit(solution)/shard_map/cond/branch_1_fun/ppermute | solution.py:56
  11.0 0.0 collective-permute-start.16
  11.0 1.2 %collective-permute-done.14.refs_1_ = bf16[64,256]{1,0:T(8,128)(2,1)S(1)} collective-permute-done((bf16[64,256]{1,0:T(8,128)(2,1)S(1)}, bf16[64,256]{1,0:T(8,128)(2,1)S(1)}, u32[]{:S(2)}, u32[]{:S(2)}) %collective-permute-start.14) | collective-permute-done | bytes 32800 | tf_op jit(solution)/shard_map/cond/branch_1_fun/ppermute | solution.py:56
  12.2 2.1 %collective-permute-done.16.refs_2_ = bf16[64,256]{1,0:T(8,128)(2,1)S(1)} collective-permute-done((bf16[64,256]{1,0:T(8,128)(2,1)S(1)}, bf16[64,256]{1,0:T(8,128)(2,1)S(1)}, u32[]{:S(2)}, u32[]{:S(2)}) %collective-permute-start.16) | collective-permute-done | bytes 32800 | tf_op jit(solution)/shard_map/cond/branch_1_fun/ppermute | solution.py:56
  14.4 0.3 %collective-permute-start.17 = (bf16[256,256]{1,0:T(8,128)(2,1)S(1)}, bf16[256,256]{1,0:T(8,128)(2,1)S(1)}, u32[]{:S(2)}, u32[]{:S(2)}) collective-permute-start(bf16[256,256]{1,0:T(8,128)(2,1)S(1)} %join.1), channel_id=1, source_target_pairs={{0,1},{1,0},{2,3},{3,2},{4,5},{5,4},{6,7},{7,6},{8,9},{9,8},{10,11... | collective-permute-start | bytes 393224 | tf_op jit(solution)/shard_map/cond/branch_1_fun/ppermute | solution.py:56
  14.7 0.0 copy-start
  14.8 1.0 %collective-permute-done.17 = bf16[256,256]{1,0:T(8,128)(2,1)S(1)} collective-permute-done((bf16[256,256]{1,0:T(8,128)(2,1)S(1)}, bf16[256,256]{1,0:T(8,128)(2,1)S(1)}, u32[]{:S(2)}, u32[]{:S(2)}) %collective-permute-start.17) | collective-permute-done | bytes 131104 | tf_op jit(solution)/shard_map/cond/branch_1_fun/ppermute | solution.py:56
  15.8 0.0 copy-done
  15.8 0.6 %attend_8.1 = bf16[128,256]{1,0:T(8,128)(2,1)S(1)} custom-call(bf16[128,256]{1,0:T(8,128)(2,1)S(1)} %copy-done, bf16[64,256]{1,0:T(8,128)(2,1)S(1)} %get-tuple-element.87.refs_0_, bf16[64,256]{1,0:T(8,128)(2,1)S(1)} %get-tuple-element.86.refs_1_, bf16[64,256]{1,0:T(8,128)(2,1)S(1)} %get-tuple-element.85.refs_2_, ...), custom_call_target="tpu_custom_call" | custom-call | tf_op jit(solution)/shard_map/cond/branch_1_fun/attend_8/pallas_call | solution.py:61
  16.4 0.0 collective-permute-done.18
  16.4 0.0 collective-permute-done.19
  16.4 0.0 collective-permute-done.20
  16.4 0.0 copy-start.4
  16.5 0.6 %copy-done.4 = bf16[128,256]{1,0:T(8,128)(2,1)} copy-done((bf16[128,256]{1,0:T(8,128)(2,1)}, bf16[128,256]{1,0:T(8,128)(2,1)S(1)}, u32[]{:S(2)}) %copy-start.4) | copy-done | bytes 65560
  (6 shorter events, 0.0 us)
Async XLA Ops:
  0.0 6.1 %copy-start.3 = (bf16[64,256]{1,0:T(8,128)(2,1)S(1)}, bf16[64,256]{1,0:T(8,128)(2,1)}, u32[]{:S(2)}) copy-start(bf16[64,256]{1,0:T(8,128)(2,1)} %param.9) | copy-start | bytes 98308
  0.0 16.4 %collective-permute-start.18 = (bf16[64,256]{1,0:T(8,128)(2,1)}, bf16[64,256]{1,0:T(8,128)(2,1)S(1)}, u32[]{:S(2)}, u32[]{:S(2)}) collective-permute-start(bf16[64,256]{1,0:T(8,128)(2,1)} %param.9), channel_id=1, source_target_pairs={{0,16},{1,17},{2,18},{3,19},{4,20},{5,21},{6,22},{7,23},{8,25},{9,... | collective-permute-start | bytes 98312 | tf_op jit(solution)/shard_map/ppermute | solution.py:56
  4.0 12.4 %collective-permute-start.19 = (bf16[64,256]{1,0:T(8,128)(2,1)}, bf16[64,256]{1,0:T(8,128)(2,1)S(1)}, u32[]{:S(2)}, u32[]{:S(2)}) collective-permute-start(bf16[64,256]{1,0:T(8,128)(2,1)} %param.9), channel_id=1, source_target_pairs={{0,9},{1,8},{2,11},{3,10},{4,13},{5,12},{6,15},{7,14},{8,1},{9,0},... | collective-permute-start | bytes 98312 | tf_op jit(solution)/shard_map/ppermute | solution.py:56
  5.3 11.1 %collective-permute-start.20 = (bf16[64,256]{1,0:T(8,128)(2,1)}, bf16[64,256]{1,0:T(8,128)(2,1)S(1)}, u32[]{:S(2)}, u32[]{:S(2)}) collective-permute-start(bf16[64,256]{1,0:T(8,128)(2,1)} %param.9), channel_id=1, source_target_pairs={{0,25},{1,24},{2,27},{3,26},{4,29},{5,28},{6,31},{7,30},{8,16},{9,... | collective-permute-start | bytes 98312 | tf_op jit(solution)/shard_map/ppermute | solution.py:56
  5.3 0.7 %copy-start.5 = (s32[16,3]{0,1:T(4,128)S(1)}, s32[16,3]{0,1:T(4,128)}, u32[]{:S(2)}) copy-start(s32[16,3]{0,1:T(4,128)} %param.10) | copy-start | bytes 580
  6.2 4.8 %collective-permute-start.15 = (bf16[64,256]{1,0:T(8,128)(2,1)S(1)}, bf16[64,256]{1,0:T(8,128)(2,1)S(1)}, u32[]{:S(2)}, u32[]{:S(2)}) collective-permute-start(bf16[64,256]{1,0:T(8,128)(2,1)S(1)} %get-tuple-element.43.refs_0_), channel_id=1, source_target_pairs={{0,6},{1,7},{2,4},{3,5},{4,2},{5,3},{6,0},{7,1},{8,15},{9,14},{10,... | collective-permute-start | bytes 98312 | tf_op jit(solution)/shard_map/cond/branch_1_fun/ppermute | solution.py:56
  8.9 3.3 %collective-permute-start.14 = (bf16[64,256]{1,0:T(8,128)(2,1)S(1)}, bf16[64,256]{1,0:T(8,128)(2,1)S(1)}, u32[]{:S(2)}, u32[]{:S(2)}) collective-permute-start(bf16[64,256]{1,0:T(8,128)(2,1)S(1)} %get-tuple-element.43.refs_0_), channel_id=1, source_target_pairs={{0,3},{1,4},{2,7},{3,0},{4,1},{5,6},{6,5},{7,2},{8,11},{9,12},{10,... | collective-permute-start | bytes 98312 | tf_op jit(solution)/shard_map/cond/branch_1_fun/ppermute | solution.py:56
  11.0 3.3 %collective-permute-start.16 = (bf16[64,256]{1,0:T(8,128)(2,1)S(1)}, bf16[64,256]{1,0:T(8,128)(2,1)S(1)}, u32[]{:S(2)}, u32[]{:S(2)}) collective-permute-start(bf16[64,256]{1,0:T(8,128)(2,1)S(1)} %get-tuple-element.43.refs_0_), channel_id=1, source_target_pairs={{0,5},{1,2},{2,1},{3,6},{4,7},{5,0},{6,3},{7,4},{8,13},{9,10},{10,... | collective-permute-start | bytes 98312 | tf_op jit(solution)/shard_map/cond/branch_1_fun/ppermute | solution.py:56
  14.4 1.4 %collective-permute-start.17 = (bf16[256,256]{1,0:T(8,128)(2,1)S(1)}, bf16[256,256]{1,0:T(8,128)(2,1)S(1)}, u32[]{:S(2)}, u32[]{:S(2)}) collective-permute-start(bf16[256,256]{1,0:T(8,128)(2,1)S(1)} %join.1), channel_id=1, source_target_pairs={{0,1},{1,0},{2,3},{3,2},{4,5},{5,4},{6,7},{7,6},{8,9},{9,8},{10,11... | collective-permute-start | bytes 393224 | tf_op jit(solution)/shard_map/cond/branch_1_fun/ppermute | solution.py:56
  14.7 1.1 %copy-start = (bf16[128,256]{1,0:T(8,128)(2,1)S(1)}, bf16[128,256]{1,0:T(8,128)(2,1)}, u32[]{:S(2)}) copy-start(bf16[128,256]{1,0:T(8,128)(2,1)} %get-tuple-element.40.queries_ref) | copy-start | bytes 196612 | tf_op jit(solution)/shard_map/cond
  16.4 0.6 %copy-start.4 = (bf16[128,256]{1,0:T(8,128)(2,1)}, bf16[128,256]{1,0:T(8,128)(2,1)S(1)}, u32[]{:S(2)}) copy-start(bf16[128,256]{1,0:T(8,128)(2,1)S(1)} %get-tuple-element.134) | copy-start | bytes 196612
